TPU v7x, 32 devices: a whole 2x2x4 slice. The times are simulated.
32 devices in a mesh: dp: 8 (over z, x), mp: 4 (over y, core).
Axes of the slice: x: 2, y: 2, z: 4, core: 2. Of those that a mesh axis runs over, the one named last changes fastest.
Arguments:
- inputs: float32 [768, 16384], P('mp', 'dp'), may hold values from -6 to 6
- history: float32 [4, 768, 16384], P(None, 'mp', 'dp'), may hold values from -6 to 6
- segment_ids: int32 [16, 1024], P('dp'), may hold values from 0 to 5, never falling along the last dimension, each value on 1 to 512 neighbouring positions
- cotangent: float32 [768, 16384], P('mp', 'dp'), may hold values from -14 to 14
- input_weight: float32 [2, 3, 768, 768], P(None, None, 'mp'), may hold values from -0.21875 to 0.21875
- input_bias: float32 [2, 3, 768], P(None, None, 'mp'), may hold values from -4 to 4
- merge_weight: float32 [2, 768, 768], P(None, 'mp'), may hold values from -0.875 to 0.875
- merge_bias: float32 [2, 768], P(None, 'mp'), may hold values from -4 to 4
- first_gain: float32 [2, 768], P(None, 'mp'), may hold values from 0.25 to 1.75
- first_shift: float32 [2, 768], P(None, 'mp'), may hold values from -4 to 4
- second_gain: float32 [2, 768], P(None, 'mp'), may hold values from 0.25 to 1.75
- second_shift: float32 [2, 768], P(None, 'mp'), may hold values from -4 to 4
- expand_weight: float32 [2, 768, 3072], P(None, None, 'mp'), may hold values from -0.21875 to 0.21875
- expand_bias: float32 [2, 3072], P(None, 'mp'), may hold values from -4 to 4
- reduce_weight: float32 [2, 3072, 768], P(None, 'mp'), may hold values from -0.109375 to 0.109375
- reduce_bias: float32 [2, 768], P(None, 'mp'), may hold values from -4 to 4
- depth_weights: float32 [2, 5], replicated, may hold values from 0.2 to 0.8
Outputs:
- output: float32 [768, 16384], P('mp', 'dp')
- input_grad: float32 [768, 16384], P('mp', 'dp')
- history_grad: float32 [4, 768, 16384], P(None, 'mp', 'dp')
- input_weight_grad: float32 [2, 3, 768, 768], P(None, None, 'mp')
- input_bias_grad: float32 [2, 3, 768], P(None, None, 'mp')
- merge_weight_grad: float32 [2, 768, 768], P(None, 'mp')
- merge_bias_grad: float32 [2, 768], P(None, 'mp')
- first_gain_grad: float32 [2, 768], P(None, 'mp')
- first_shift_grad: float32 [2, 768], P(None, 'mp')
- second_gain_grad: float32 [2, 768], P(None, 'mp')
- second_shift_grad: float32 [2, 768], P(None, 'mp')
- expand_weight_grad: float32 [2, 768, 3072], P(None, None, 'mp')
- expand_bias_grad: float32 [2, 3072], P(None, 'mp')
- reduce_weight_grad: float32 [2, 3072, 768], P(None, 'mp')
- reduce_bias_grad: float32 [2, 768], P(None, 'mp')
- depth_weights_grad: float32 [2, 5], replicated
Inputs may be any that keep to these rules, and one draw needn't show every extreme that they name: `segment_ids`: along each packed row the segment numbers never fall.
All inputs are finite; a program needn't handle non-finite values.
Results may differ from a plain program's by a relative error of at most 0.023.
Values may be sent and summed in bfloat16 or wider, within the bound.
No kernel may reach another device: no remote copies, remote signals or barrier semaphores. Data moves between devices by JAX's collectives and lax.ppermute only.
A program may use at most 256 MiB of HBM per device.

v0:
```python
import jax
import jax.numpy as jnp
from jax import lax
from jax.sharding import PartitionSpec as P

HEAD = 64
LAYERS = 2
HISTORY = 4


EPS = 1e-05
MASKED = -1e30


def rotary_tables(length):
    positions = jnp.arange(length, dtype=jnp.float32)
    frequency = 10000.0 ** (-jnp.arange(HEAD // 2, dtype=jnp.float32) * 2.0 / HEAD)
    angles = positions[:, None] * frequency[None, :]
    return (jnp.cos(angles)[:, None, :], jnp.sin(angles)[:, None, :])


def rotate(values, cosine, sine):
    first = values[..., : HEAD // 2]
    second = values[..., HEAD // 2 :]
    return jnp.concatenate([first * cosine - second * sine, second * cosine + first * sine], -1)


def rotate_back(grads, cosine, sine):
    first = grads[..., : HEAD // 2]
    second = grads[..., HEAD // 2 :]
    return jnp.concatenate([first * cosine + second * sine, second * cosine - first * sine], -1)


def allowed_mask(segments):
    positions = jnp.arange(segments.shape[0])
    return (segments[:, None] == segments[None, :]) & (positions[None, :] <= positions[:, None])


def masked_scores(query, key_rot, segments):
    scores = jnp.einsum(
        "qhd,khd->hqk", query, key_rot, preferred_element_type=jnp.float32
    ) * HEAD ** (-0.5)
    allowed = allowed_mask(segments)
    return jnp.where(allowed[None], scores, MASKED)


def attend_forward(items):
    query, key_rot, value_low, segments = items
    scores = masked_scores(query, key_rot, segments)
    peak = jnp.max(scores, -1, keepdims=True)
    weights = jnp.exp(scores - peak)
    total = jnp.sum(weights, -1, keepdims=True)
    probs = weights / total
    attended = jnp.einsum(
        "hqk,khd->qhd", probs.astype(jnp.bfloat16), value_low, preferred_element_type=jnp.float32
    )
    return (attended, (peak + jnp.log(total))[..., 0])


def attend_backward(items):
    query, key_rot, value_low, segments, grad_attended, log_total = items
    scores = masked_scores(query, key_rot, segments)
    probs = jnp.exp(scores - log_total[:, :, None])
    grad_probs = jnp.einsum(
        "qhd,khd->hqk", grad_attended, value_low, preferred_element_type=jnp.float32
    )
    grad_value = jnp.einsum(
        "hqk,qhd->khd",
        probs.astype(jnp.bfloat16),
        grad_attended,
        preferred_element_type=jnp.float32,
    )
    delta = jnp.sum(grad_probs * probs, -1, keepdims=True)
    grad_scores = (probs * (grad_probs - delta)).astype(jnp.bfloat16)
    scale = HEAD ** (-0.5)
    grad_query = (
        jnp.einsum("hqk,khd->qhd", grad_scores, key_rot, preferred_element_type=jnp.float32) * scale
    )
    grad_key = (
        jnp.einsum("hqk,qhd->khd", grad_scores, query, preferred_element_type=jnp.float32) * scale
    )
    return (grad_query, grad_key, grad_value)


def norm_rows(values, gain, shift):
    local_width = values.shape[1]
    width = local_width * lax.axis_size("mp")
    row_sum, row_squares = lax.psum((jnp.sum(values, 1), jnp.sum(values * values, 1)), "mp")
    row_mean = (row_sum / width)[:, None]
    variance = (row_squares / width)[:, None] - row_mean * row_mean
    inv_scale = lax.rsqrt(variance + EPS)
    centered = (values - row_mean) * inv_scale
    whole = lax.all_gather((centered * gain + shift).astype(jnp.bfloat16), "mp", axis=1, tiled=True)
    return (whole, centered, inv_scale)


def norm_back(grad_normed, centered, inv_scale, gain):
    width = centered.shape[1] * lax.axis_size("mp")
    gain_grad = jnp.sum(grad_normed * centered, 0)
    shift_grad = jnp.sum(grad_normed, 0)
    grad_centered = grad_normed * gain
    first_sum, second_sum = lax.psum(
        (jnp.sum(grad_centered, 1), jnp.sum(grad_centered * centered, 1)), "mp"
    )
    grad_values = inv_scale * (
        grad_centered - first_sum[:, None] / width - centered * second_sum[:, None] / width
    )
    return (grad_values, gain_grad, shift_grad)


def branch_sum(partial_value, bias):
    return lax.psum_scatter(partial_value, "mp", scatter_dimension=1, tiled=True) + bias


def spread_grad(grad):
    return lax.all_gather(grad.astype(jnp.bfloat16), "mp", axis=1, tiled=True)


def gather_back(partial_value):
    return lax.psum_scatter(partial_value, "mp", scatter_dimension=1, tiled=True)


def block_forward(values, segments, layer, low_set, tables):
    (
        w_input,
        b_input,
        w_merge,
        b_merge,
        gain_one,
        shift_one,
        gain_two,
        shift_two,
        w_expand,
        b_expand,
        w_reduce,
        b_reduce,
    ) = layer
    input_low, merge_low, expand_low, reduce_low = low_set
    cosine, sine = tables
    seq_count, length = segments.shape
    rows, local_width = values.shape
    heads = local_width // HEAD
    whole, centered_one, scale_one = norm_rows(values, gain_one, shift_one)
    projected = (
        jnp.einsum("td,kfd->tkf", whole, input_low, preferred_element_type=jnp.float32)
        + b_input[None]
    )
    parts = projected.reshape(seq_count, length, 3, heads, HEAD)
    query = rotate(parts[:, :, 0], cosine, sine).astype(jnp.bfloat16)
    key_rot = rotate(parts[:, :, 1], cosine, sine).astype(jnp.bfloat16)
    value_low = parts[:, :, 2].astype(jnp.bfloat16)
    attended, log_total = lax.map(attend_forward, (query, key_rot, value_low, segments))
    attended = attended.reshape(rows, local_width).astype(jnp.bfloat16)
    attended_all = lax.all_gather(attended, "mp", axis=1, tiled=True)
    merge_cols = lax.all_to_all(merge_low, "mp", split_axis=1, concat_axis=0, tiled=True)
    middle = (
        values + jnp.dot(attended_all, merge_cols, preferred_element_type=jnp.float32) + b_merge
    )
    whole_two, centered_two, scale_two = norm_rows(middle, gain_two, shift_two)
    pre_gelu = jnp.dot(whole_two, expand_low, preferred_element_type=jnp.float32) + b_expand
    activated = jax.nn.gelu(pre_gelu).astype(jnp.bfloat16)
    result = middle + branch_sum(
        jnp.dot(activated, reduce_low, preferred_element_type=jnp.float32), b_reduce
    )
    saved = (
        whole,
        centered_one,
        scale_one,
        query,
        key_rot,
        value_low,
        log_total,
        attended,
        whole_two,
        centered_two,
        scale_two,
        pre_gelu,
        activated,
    )
    return (result, saved)


def block_backward(grad_out, segments, layer, low_set, saved, tables):
    gain_one = layer[4]
    gain_two = layer[6]
    input_low, merge_low, expand_low, reduce_low = low_set
    (
        whole,
        centered_one,
        scale_one,
        query,
        key_rot,
        value_low,
        log_total,
        attended,
        whole_two,
        centered_two,
        scale_two,
        pre_gelu,
        activated,
    ) = saved
    cosine, sine = tables
    seq_count, length = segments.shape
    rows, local_width = grad_out.shape
    heads = local_width // HEAD
    reduce_bias_grad = jnp.sum(grad_out, 0)
    grad_whole = spread_grad(grad_out)
    reduce_weight_grad = jnp.einsum(
        "tf,td->fd", activated, grad_whole, preferred_element_type=jnp.float32
    )
    grad_activated = jnp.einsum(
        "td,fd->tf", grad_whole, reduce_low, preferred_element_type=jnp.float32
    )
    grad_pre = jax.vjp(jax.nn.gelu, pre_gelu)[1](grad_activated)[0]
    expand_bias_grad = jnp.sum(grad_pre, 0)
    grad_pre_low = grad_pre.astype(jnp.bfloat16)
    expand_weight_grad = jnp.einsum(
        "td,tf->df", whole_two, grad_pre_low, preferred_element_type=jnp.float32
    )
    grad_normed_two = gather_back(
        jnp.einsum("tf,df->td", grad_pre_low, expand_low, preferred_element_type=jnp.float32)
    )
    grad_norm_two, second_gain_grad, second_shift_grad = norm_back(
        grad_normed_two, centered_two, scale_two, gain_two
    )
    grad_middle = grad_out + grad_norm_two
    merge_bias_grad = jnp.sum(grad_middle, 0)
    grad_middle_whole = spread_grad(grad_middle)
    merge_weight_grad = jnp.einsum(
        "tc,td->cd", attended, grad_middle_whole, preferred_element_type=jnp.float32
    )
    grad_attended = jnp.einsum(
        "td,cd->tc", grad_middle_whole, merge_low, preferred_element_type=jnp.float32
    )
    grad_attended = grad_attended.astype(jnp.bfloat16).reshape(seq_count, length, heads, HEAD)
    grad_query, grad_key, grad_value = lax.map(
        attend_backward, (query, key_rot, value_low, segments, grad_attended, log_total)
    )
    grad_lin = jnp.stack(
        [rotate_back(grad_query, cosine, sine), rotate_back(grad_key, cosine, sine), grad_value], 2
    )
    grad_lin = grad_lin.reshape(rows, 3, local_width)
    input_bias_grad = jnp.sum(grad_lin, 0)
    grad_lin_low = grad_lin.astype(jnp.bfloat16)
    input_weight_grad = jnp.einsum(
        "td,tkf->kfd", whole, grad_lin_low, preferred_element_type=jnp.float32
    )
    grad_normed_one = gather_back(
        jnp.einsum("tkf,kfd->td", grad_lin_low, input_low, preferred_element_type=jnp.float32)
    )
    grad_norm_one, first_gain_grad, first_shift_grad = norm_back(
        grad_normed_one, centered_one, scale_one, gain_one
    )
    grad_values = grad_middle + grad_norm_one
    grads = (
        input_weight_grad,
        input_bias_grad,
        merge_weight_grad,
        merge_bias_grad,
        first_gain_grad,
        first_shift_grad,
        second_gain_grad,
        second_shift_grad,
        expand_weight_grad,
        expand_bias_grad,
        reduce_weight_grad,
        reduce_bias_grad,
    )
    return (grad_values, grads)


def sum_replicas(grads):
    (
        g_input_w,
        g_input_b,
        g_merge_w,
        g_merge_b,
        g_gain_one,
        g_shift_one,
        g_gain_two,
        g_shift_two,
        g_expand_w,
        g_expand_b,
        g_reduce_w,
        g_reduce_b,
    ) = grads
    return lax.psum(
        (
            g_input_w,
            g_input_b,
            g_merge_w,
            g_merge_b,
            g_gain_one,
            g_shift_one,
            g_gain_two,
            g_shift_two,
            g_expand_w,
            g_expand_b,
            g_reduce_w,
            g_reduce_b,
        ),
        "dp",
    )


def stack_layers(layer_grads):
    members = len(layer_grads[0])
    return tuple((jnp.stack([grads[member] for grads in layer_grads]) for member in range(members)))


def shards(
    inputs,
    history,
    segment_ids,
    cotangent,
    input_weight,
    input_bias,
    merge_weight,
    merge_bias,
    first_gain,
    first_shift,
    second_gain,
    second_shift,
    expand_weight,
    expand_bias,
    reduce_weight,
    reduce_bias,
    depth_weights,
):
    tables = rotary_tables(segment_ids.shape[1])
    rows_first = jnp.transpose(inputs)
    history_rows = jnp.transpose(history, (0, 2, 1))
    stacks = (
        input_weight,
        input_bias,
        merge_weight,
        merge_bias,
        first_gain,
        first_shift,
        second_gain,
        second_shift,
        expand_weight,
        expand_bias,
        reduce_weight,
        reduce_bias,
    )
    layers = [tuple((item[index] for item in stacks)) for index in range(LAYERS)]
    low_sets = [
        (
            layer[0].astype(jnp.bfloat16),
            layer[2].astype(jnp.bfloat16),
            layer[8].astype(jnp.bfloat16),
            layer[10].astype(jnp.bfloat16),
        )
        for layer in layers
    ]
    current = rows_first
    layer_outputs = []
    saved_list = []
    for index in range(LAYERS):
        result, saved = block_forward(current, segment_ids, layers[index], low_sets[index], tables)
        layer_outputs.append(result)
        saved_list.append(saved)
        entries = [history_rows[j] for j in range(index, HISTORY)] + layer_outputs
        mixed = depth_weights[index, 0] * entries[0]
        for position in range(1, len(entries)):
            mixed = mixed + depth_weights[index, position] * entries[position]
        current = mixed
    grad_current = jnp.transpose(cotangent)
    history_grads = [jnp.zeros_like(history_rows[0]) for slot in range(HISTORY)]
    output_grads = [jnp.zeros_like(grad_current) for slot in range(LAYERS)]
    mix_terms = [None] * LAYERS
    layer_grads = [None] * LAYERS
    for index in reversed(range(LAYERS)):
        entries = [history_rows[j] for j in range(index, HISTORY)] + layer_outputs[: index + 1]
        kept = HISTORY - index
        mix_terms[index] = jnp.stack([jnp.sum(grad_current * entry) for entry in entries])
        for position in range(len(entries)):
            share = depth_weights[index, position] * grad_current
            if position < kept:
                history_grads[index + position] = history_grads[index + position] + share
            else:
                output_grads[position - kept] = output_grads[position - kept] + share
        grad_current, grads = block_backward(
            output_grads[index],
            segment_ids,
            layers[index],
            low_sets[index],
            saved_list[index],
            tables,
        )
        grads = sum_replicas(grads)
        layer_grads[index] = grads
    totals = stack_layers(layer_grads)
    mix_grad = lax.psum(jnp.stack(mix_terms), ("dp", "mp"))
    history_out = jnp.transpose(jnp.stack(history_grads), (0, 2, 1))
    return (
        jnp.transpose(current),
        jnp.transpose(grad_current),
        history_out,
        totals[0],
        totals[1],
        totals[2],
        totals[3],
        totals[4],
        totals[5],
        totals[6],
        totals[7],
        totals[8],
        totals[9],
        totals[10],
        totals[11],
        mix_grad,
    )


def solution(mesh):
    in_specs = (
        P("mp", "dp"),
        P(None, "mp", "dp"),
        P("dp", None),
        P("mp", "dp"),
        P(None, None, "mp", None),
        P(None, None, "mp"),
        P(None, "mp", None),
        P(None, "mp"),
        P(None, "mp"),
        P(None, "mp"),
        P(None, "mp"),
        P(None, "mp"),
        P(None, None, "mp"),
        P(None, "mp"),
        P(None, "mp", None),
        P(None, "mp"),
        P(),
    )
    out_specs = (
        P("mp", "dp"),
        P("mp", "dp"),
        P(None, "mp", "dp"),
        P(None, None, "mp", None),
        P(None, None, "mp"),
        P(None, "mp", None),
        P(None, "mp"),
        P(None, "mp"),
        P(None, "mp"),
        P(None, "mp"),
        P(None, "mp"),
        P(None, None, "mp"),
        P(None, "mp"),
        P(None, "mp", None),
        P(None, "mp"),
        P(),
    )
    return jax.shard_map(shards, mesh=mesh, in_specs=in_specs, out_specs=out_specs, check_vma=False)
```

profile of v0, /device:TPU:0, one launch (start us, length us, event | category | flops | bytes accessed | tf_op | source)
XLA Modules:
  0.0 1609.4 jit_solution(2349350101275155565)
XLA Ops:
  11.6 12.7 all-reduce.9
  31.4 23.7 %all-gather.11.cloned.1.call-done = bf16[2048,768]{0,1:T(8,128)(2,1)} async-done(((bf16[2048,192]{0,1:T(8,128)(2,1)}), bf16[2048,768]{0,1:T(8,128)(2,1)}) %all-gather.11.cloned.1.call-update) | async-done | bytes 3145744 | tf_op jit(solution)/shard_map/all_gather | solution.py:93
  61.3 7.6 reshape.392
  78.4 29.0 %while.52 = (s32[]{:T(128)}, bf16[2,1024,3,64]{1,3,2,0:T(8,128)(2,1)}, f32[2,3,1024]{2,1,0:T(4,128)S(1)}, bf16[2,1024,3,64]{1,3,2,0:T(8,128)(2,1)}, s32[2,1024]{...) while((s32[]{:T(128)}, ...), condition=%wide.region_7.8_spmd, body=%wide.region_4.7_spmd.sunk | while | flops 846197760 | bytes 48228480 | solution.py:152
  117.9 7.9 all-to-all-done
  126.5 15.1 all-gather.13.cloned.1.call-done
  144.4 10.2 all-reduce.8
  164.5 21.1 %all-gather.15.cloned.1.call-done = bf16[2048,768]{0,1:T(8,128)(2,1)} async-done(((bf16[2048,192]{0,1:T(8,128)(2,1)}), bf16[2048,768]{0,1:T(8,128)(2,1)}) %all-gather.15.cloned.1.call-update) | async-done | bytes 3145744 | tf_op jit(solution)/shard_map/all_gather | solution.py:93
  200.5 56.6 %reduce-scatter.7.cloned.1.call-done = f32[2048,192]{0,1:T(8,128)} async-done(((f32[2048,768]{0,1:T(8,128)}), f32[2048,192]{0,1:T(8,128)}) %reduce-scatter.7.cloned.1.call-update) | async-done | bytes 1572880 | tf_op jit(solution)/shard_map/reduce_scatter | solution.py:112
  257.1 9.0 fusion.177
  266.1 10.4 all-reduce.7
  277.9 29.6 %all-gather.17.cloned.1.call-done = bf16[2048,768]{0,1:T(8,128)(2,1)} async-done(((bf16[2048,192]{0,1:T(8,128)(2,1)}), bf16[2048,768]{0,1:T(8,128)(2,1)}) %all-gather.17.cloned.1.call-update) | async-done | bytes 3145744 | tf_op jit(solution)/shard_map/all_gather | solution.py:93
  313.6 7.5 reshape.393
  330.9 29.0 %while.53 = (s32[]{:T(128)}, bf16[2,1024,3,64]{1,3,2,0:T(8,128)(2,1)}, f32[2,3,1024]{2,1,0:T(4,128)S(1)}, bf16[2,1024,3,64]{1,3,2,0:T(8,128)(2,1)}, s32[2,1024]{...) while((s32[]{:T(128)}, ...), condition=%wide.region_20.21_spmd, body=%wide.region_17.20_spmd.sunk | while | flops 846197760 | bytes 48228480 | solution.py:152
  363.2 10.4 all_to_all.32
  374.9 16.9 %all-gather.19.cloned.1.call-done = bf16[2048,768]{0,1:T(8,128)(2,1)} async-done(((bf16[2048,192]{0,1:T(8,128)(2,1)}), bf16[2048,768]{0,1:T(8,128)(2,1)}) %all-gather.19.cloned.1.call-update) | async-done | bytes 3145744 | tf_op jit(solution)/shard_map/all_gather | solution.py:154
  394.8 10.5 all-reduce.6
  408.3 28.1 %all-gather.21.cloned.1.call-done = bf16[2048,768]{0,1:T(8,128)(2,1)} async-done(((bf16[2048,192]{0,1:T(8,128)(2,1)}), bf16[2048,768]{0,1:T(8,128)(2,1)}) %all-gather.21.cloned.1.call-update) | async-done | bytes 3145744 | tf_op jit(solution)/shard_map/all_gather | solution.py:93
  436.3 7.6 fusion.167
  443.9 23.2 %all-gather.23.cloned.1.call-done = bf16[2048,768]{0,1:T(8,128)(2,1)} async-done(((bf16[2048,192]{0,1:T(8,128)(2,1)}), bf16[2048,768]{0,1:T(8,128)(2,1)}) %all-gather.23.cloned.1.call-update) | async-done | bytes 3145744 | tf_op jit(solution)/shard_map/all_gather | solution.py:116
  467.1 10.2 fusion.195
  483.6 58.5 %reduce-scatter.11.cloned.1.call-done = f32[2048,192]{0,1:T(8,128)} async-done(((f32[2048,768]{0,1:T(8,128)}), f32[2048,192]{0,1:T(8,128)}) %reduce-scatter.11.cloned.1.call-update) | async-done | bytes 1572880 | tf_op jit(solution)/shard_map/reduce_scatter | solution.py:120
  544.7 10.1 all-reduce.5
  560.3 29.7 %all-gather.25.cloned.1.call-done = bf16[2048,768]{0,1:T(8,128)(2,1)} async-done(((bf16[2048,192]{0,1:T(8,128)(2,1)}), bf16[2048,768]{0,1:T(8,128)(2,1)}) %all-gather.25.cloned.1.call-update) | async-done | bytes 3145744 | tf_op jit(solution)/shard_map/all_gather | solution.py:116
  597.8 93.4 %while.54 = (s32[]{:T(128)}, f32[2,1024,3,64]{1,3,2,0:T(8,128)}, f32[2,1024,3,64]{1,3,2,0:T(8,128)}, f32[2,1024,3,64]{1,0,3,2:T(2,128)}, bf16[2,1024,3,64]{1,3,2...) while((s32[]{:T(128)}, f32[2,1024,3,64]{1,3,2,0:T(8,128)}, ...), condition=%wide.region_33.34_spmd, body=%wide.region_31.33_spmd.sunk | while | flops 2063987712 | bytes 262119888 | solution.py:236
  607.2 14.4 dynamic_update_slice.56
  621.6 9.3 multiply_reduce_fusion.24
  653.7 14.4 dynamic_update_slice.56
  668.1 9.2 multiply_reduce_fusion.24
  718.2 58.5 %reduce-scatter.13.cloned.1.call-done = f32[2048,192]{0,1:T(8,128)} async-done(((f32[2048,768]{0,1:T(8,128)}), f32[2048,192]{0,1:T(8,128)}) %reduce-scatter.13.cloned.1.call-update) | async-done | bytes 1572880 | tf_op jit(solution)/shard_map/reduce_scatter | solution.py:120
  779.3 10.1 all-reduce.4
  797.3 29.7 %all-gather.27.cloned.1.call-done = bf16[2048,768]{0,1:T(8,128)(2,1)} async-done(((bf16[2048,192]{0,1:T(8,128)(2,1)}), bf16[2048,768]{0,1:T(8,128)(2,1)}) %all-gather.27.cloned.1.call-update) | async-done | bytes 3145744 | tf_op jit(solution)/shard_map/all_gather | solution.py:116
  827.0 10.7 fusion.196
  844.0 58.5 %reduce-scatter.15.cloned.1.call-done = f32[2048,192]{0,1:T(8,128)} async-done(((f32[2048,768]{0,1:T(8,128)}), f32[2048,192]{0,1:T(8,128)}) %reduce-scatter.15.cloned.1.call-update) | async-done | bytes 1572880 | tf_op jit(solution)/shard_map/reduce_scatter | solution.py:120
  905.1 10.1 all-reduce.3
  920.2 8.6 fusion.169
  928.8 21.0 %all-gather.29.cloned.1.call-done = bf16[2048,768]{0,1:T(8,128)(2,1)} async-done(((bf16[2048,192]{0,1:T(8,128)(2,1)}), bf16[2048,768]{0,1:T(8,128)(2,1)}) %all-gather.29.cloned.1.call-update) | async-done | bytes 3145744 | tf_op jit(solution)/shard_map/all_gather | solution.py:116
  957.7 94.2 %while.55 = (s32[]{:T(128)}, f32[2,1024,3,64]{1,3,2,0:T(8,128)}, f32[2,1024,3,64]{1,3,2,0:T(8,128)}, f32[2,1024,3,64]{1,0,3,2:T(2,128)}, bf16[2,1024,3,64]{1,3,2...) while((s32[]{:T(128)}, f32[2,1024,3,64]{1,3,2,0:T(8,128)}, ...), condition=%wide.region_46.47_spmd, body=%wide.region_44.46_spmd.sunk | while | flops 2063987712 | bytes 262119888 | solution.py:236
  967.7 14.4 dynamic_update_slice.59
  982.1 9.4 multiply_reduce_fusion.25
  1014.3 14.3 dynamic_update_slice.59
  1028.7 9.3 multiply_reduce_fusion.25
  1086.6 10.4 convolution_bitcast_fusion.2
  1120.8 10.6 multiply_reduce_fusion.3
  1140.6 44.8 %psum.327 = f32[2,5]{1,0:T(2,128)} all-reduce(f32[2,5]{1,0:T(2,128)S(1)} %pad_maximum_fusion.20), channel_id=1, replica_groups=mesh['dp'=8,'mp'=4] {'dp','mp'}, use_global_device_ids=true, to_apply=%region_102.103 | all-reduce | flops 10 | bytes 80 | tf_op jit(solution)/shard_map/psum | solution.py:395
  1197.9 36.9 %all-reduce = (f32[1,3,192]{2,1,0:T(4,128)S(1)}, f32[1,3,192]{2,1,0:T(4,128)S(1)}, f32[1,192]{1,0:T(1,128)S(1)}, f32[1,192]{1,0:T(1,128)S(1)}, f32[1,192]{1,0:T(...) all-reduce(f32[1,3,192]{2,1,0:T(4,128)S(1)} %bitcast.565, ...), channel_id=1, replica_groups=mesh['dp'=8,'mp'=4] {'dp'}, use_global_device_ids=true, to_apply=%region_57.58 | all-reduce | flops 4992 | bytes 39936 | tf_op jit(solution)/shard_map/psum | solution.py:287
  1235.5 10.9 all-reduce.2
  1253.7 336.0 %all-reduce.12.cloned.1.call-done = (f32[1,3,192,768]{3,2,1,0:T(8,128)}, f32[1,3,192,768]{3,2,1,0:T(8,128)}, f32[1,192,768]{2,1,0:T(8,128)}, f32[1,192,768]{2,1,...) async-done(((f32[1,3,192,768]{3,2,1,0:T(8,128)}, f32[1,3,192,768]{3,2,1,0:T(8,128)}, ...) | async-done | bytes 14155792 | tf_op jit(solution)/shard_map/psum | solution.py:287
  (583 shorter events, 424.4 us)
Async XLA Ops:
  7.2 48.0 %all-gather.11.cloned.1.call-start = ((), (), s32[]{:S(2)}) async-start(), calls=%async_computation.8 | async-start | bytes 3932160 | tf_op jit(solution)/shard_map/all_gather | solution.py:93
  26.2 115.4 %all-gather.13.cloned.1.call-start = ((), (), s32[]{:S(2)}) async-start(), calls=%async_computation.9 | async-start | bytes 3932160 | tf_op jit(solution)/shard_map/all_gather | solution.py:154
  30.9 30.4 %copy-start.73 = (bf16[2,3,192,768]{3,2,1,0:T(8,128)(2,1)}, bf16[2,3,192,768]{3,2,1,0:T(8,128)(2,1)S(1)}, u32[]{:S(2)}) copy-start(bf16[2,3,192,768]{3,2,1,0:T(8,128)(2,1)S(1)} %convert.42) | copy-start | bytes 5308420
  31.4 44.5 %copy-start.53 = (f32[1024,32]{0,1:T(8,128)}, f32[1024,32]{0,1:T(8,128)S(1)}, u32[]{:S(2)}) copy-start(f32[1024,32]{0,1:T(8,128)S(1)} %get-tuple-element.534) | copy-start | bytes 393220
  31.4 44.5 %copy-start.57 = (f32[1024,32]{0,1:T(8,128)}, f32[1024,32]{0,1:T(8,128)S(1)}, u32[]{:S(2)}) copy-start(f32[1024,32]{0,1:T(8,128)S(1)} %get-tuple-element.535) | copy-start | bytes 393220
  110.6 31.0 %copy-start.11 = (f32[192,2048]{1,0:T(8,128)S(1)}, f32[192,2048]{1,0:T(8,128)}, u32[]{:S(2)}) copy-start(f32[192,2048]{1,0:T(8,128)} %param.25) | copy-start | bytes 4718596
  111.4 30.2 %copy-start.61 = (bf16[1,192,768]{2,1,0:T(8,128)(2,1)}, bf16[1,192,768]{2,1,0:T(8,128)(2,1)S(1)}, u32[]{:S(2)}) copy-start(bf16[1,192,768]{2,1,0:T(8,128)(2,1)S(1)} %get-tuple-element.493) | copy-start | bytes 884740
  112.3 13.6 all-to-all-start
  115.8 69.9 %all-gather.15.cloned.1.call-start = ((), (), s32[]{:S(2)}) async-start(), calls=%async_computation.10 | async-start | bytes 3932160 | tf_op jit(solution)/shard_map/all_gather | solution.py:93
  117.4 37.3 %copy-start.98 = (f32[1,192]{1,0:T(1,128)}, f32[1,192]{1,0:T(1,128)S(1)}, u32[]{:S(2)}) copy-start(f32[1,192]{1,0:T(1,128)S(1)} %get-tuple-element.515) | copy-start | bytes 2308
  144.4 112.7 %copy-start.18 = (f32[2048,192]{0,1:T(8,128)}, f32[2048,192]{0,1:T(8,128)S(1)}, u32[]{:S(2)}) copy-start(f32[2048,192]{0,1:T(8,128)S(1)} %get-tuple-element.536) | copy-start | bytes 4718596
  155.9 101.2 %reduce-scatter.7.cloned.1.call-start = ((), (), s32[]{:S(2)}) async-start(), calls=%async_computation.11 | async-start | bytes 7864320 | tf_op jit(solution)/shard_map/reduce_scatter | solution.py:112
  164.5 26.3 %copy-start.118 = (f32[768]{0:T(1024)}, f32[768]{0:T(1024)S(1)}, u32[]{:S(2)}) copy-start(f32[768]{0:T(1024)S(1)} %get-tuple-element.339) | copy-start | bytes 9220
  198.6 108.9 %all-gather.17.cloned.1.call-start = ((), (), s32[]{:S(2)}) async-start(), calls=%async_computation.12 | async-start | bytes 3932160 | tf_op jit(solution)/shard_map/all_gather | solution.py:93
  266.1 47.5 %copy-start.20 = (f32[2048,192]{0,1:T(8,128)}, f32[2048,192]{0,1:T(8,128)S(1)}, u32[]{:S(2)}) copy-start(f32[2048,192]{0,1:T(8,128)S(1)} %get-tuple-element.455) | copy-start | bytes 4718596
  266.1 41.4 %copy-start.74 = (bf16[2,3,192,768]{3,2,1,0:T(8,128)(2,1)S(1)}, bf16[2,3,192,768]{3,2,1,0:T(8,128)(2,1)}, u32[]{:S(2)}) copy-start(bf16[2,3,192,768]{3,2,1,0:T(8,128)(2,1)} %copy-done.73) | copy-start | bytes 5308420
  276.5 37.1 %copy-start.91 = (f32[2048]{0:T(1024)}, f32[2048]{0:T(1024)S(1)}, u32[]{:S(2)}) copy-start(f32[2048]{0:T(1024)S(1)} %get-tuple-element.504) | copy-start | bytes 24580
  276.5 37.1 %copy-start.93 = (f32[2048]{0:T(1024)}, f32[2048]{0:T(1024)S(1)}, u32[]{:S(2)}) copy-start(f32[2048]{0:T(1024)S(1)} %get-tuple-element.505) | copy-start | bytes 24580
  277.8 114.1 %all-gather.19.cloned.1.call-start = ((), (), s32[]{:S(2)}) async-start(), calls=%async_computation.13 | async-start | bytes 3932160 | tf_op jit(solution)/shard_map/all_gather | solution.py:154
  361.8 30.0 %copy-start.21 = (f32[2048,192]{0,1:T(8,128)S(1)}, f32[2048,192]{0,1:T(8,128)}, u32[]{:S(2)}) copy-start(f32[2048,192]{0,1:T(8,128)} %copy-done.20) | copy-start | bytes 4718596
  361.9 30.0 %copy-start.126 = (f32[1,192]{1,0:T(1,128)S(1)}, f32[1,192]{1,0:T(1,128)}, u32[]{:S(2)}) copy-start(f32[1,192]{1,0:T(1,128)} %get-tuple-element.518) | copy-start | bytes 2308
  363.0 73.3 %all-gather.21.cloned.1.call-start = ((), (), s32[]{:S(2)}) async-start(), calls=%async_computation.14 | async-start | bytes 3932160 | tf_op jit(solution)/shard_map/all_gather | solution.py:93
  394.8 160.0 %copy-start.13 = (f32[2048,192]{0,1:T(8,128)}, f32[2048,192]{0,1:T(8,128)S(1)}, u32[]{:S(2)}) copy-start(f32[2048,192]{0,1:T(8,128)S(1)} %get-tuple-element.537) | copy-start | bytes 4718596
  406.6 60.5 %all-gather.23.cloned.1.call-start = ((), (), s32[]{:S(2)}) async-start(), calls=%async_computation.16 | async-start | bytes 3932160 | tf_op jit(solution)/shard_map/all_gather | solution.py:116
  408.2 58.9 %copy-start.121 = (f32[768]{0:T(1024)S(1)}, f32[768]{0:T(1024)}, u32[]{:S(2)}) copy-start(f32[768]{0:T(1024)} %get-tuple-element.338) | copy-start | bytes 9220
  408.2 133.8 %reduce-scatter.11.cloned.1.call-start = ((), (), s32[]{:S(2)}) async-start(), calls=%async_computation.17 | async-start | bytes 7864320 | tf_op jit(solution)/shard_map/reduce_scatter | solution.py:120
  483.5 106.5 %all-gather.25.cloned.1.call-start = ((), (), s32[]{:S(2)}) async-start(), calls=%async_computation.18 | async-start | bytes 3932160 | tf_op jit(solution)/shard_map/all_gather | solution.py:116
  560.2 216.4 %reduce-scatter.13.cloned.1.call-start = ((), (), s32[]{:S(2)}) async-start(), calls=%async_computation.19 | async-start | bytes 7864320 | tf_op jit(solution)/shard_map/reduce_scatter | solution.py:120
  718.1 58.6 %copy-start.22 = (f32[2048,192]{0,1:T(8,128)S(1)}, f32[2048,192]{0,1:T(8,128)}, u32[]{:S(2)}) copy-start(f32[2048,192]{0,1:T(8,128)} %copy-done.20) | copy-start | bytes 4718596
  718.1 58.6 %copy-start.92 = (f32[2048]{0:T(1024)S(1)}, f32[2048]{0:T(1024)}, u32[]{:S(2)}) copy-start(f32[2048]{0:T(1024)} %copy-done.91) | copy-start | bytes 24580
  718.1 58.6 %copy-start.94 = (f32[2048]{0:T(1024)S(1)}, f32[2048]{0:T(1024)}, u32[]{:S(2)}) copy-start(f32[2048]{0:T(1024)} %copy-done.93) | copy-start | bytes 24580
  718.1 58.6 %copy-start.97 = (f32[1,192]{1,0:T(1,128)S(1)}, f32[1,192]{1,0:T(1,128)}, u32[]{:S(2)}) copy-start(f32[1,192]{1,0:T(1,128)} %get-tuple-element.520) | copy-start | bytes 2308
  718.1 71.3 %copy-start.16 = (f32[192,2048]{1,0:T(8,128)S(1)}, f32[192,2048]{1,0:T(8,128)}, u32[]{:S(2)}) copy-start(f32[192,2048]{1,0:T(8,128)} %param.28) | copy-start | bytes 4718596
  718.1 108.9 %all-gather.27.cloned.1.call-start = ((), (), s32[]{:S(2)}) async-start(), calls=%async_computation.20 | async-start | bytes 3932160 | tf_op jit(solution)/shard_map/all_gather | solution.py:116
  795.1 31.9 %copy-start.65 = (bf16[2,768,768]{2,1,0:T(8,128)(2,1)S(1)}, bf16[2,768,768]{2,1,0:T(8,128)(2,1)}, u32[]{:S(2)}) copy-start(bf16[2,768,768]{2,1,0:T(8,128)(2,1)} %convert.49) | copy-start | bytes 7077892
  795.1 31.9 %copy-start.119 = (f32[768]{0:T(1024)S(1)}, f32[768]{0:T(1024)}, u32[]{:S(2)}) copy-start(f32[768]{0:T(1024)} %copy-done.118) | copy-start | bytes 9220
  797.3 105.2 %reduce-scatter.15.cloned.1.call-start = ((), (), s32[]{:S(2)}) async-start(), calls=%async_computation.21 | async-start | bytes 7864320 | tf_op jit(solution)/shard_map/reduce_scatter | solution.py:120
  843.9 58.6 %copy-start.19 = (f32[2048,192]{0,1:T(8,128)S(1)}, f32[2048,192]{0,1:T(8,128)}, u32[]{:S(2)}) copy-start(f32[2048,192]{0,1:T(8,128)} %copy-done.18) | copy-start | bytes 4718596
  843.9 58.6 %copy-start.88 = (f32[2048]{0:T(1024)S(1)}, f32[2048]{0:T(1024)}, u32[]{:S(2)}) copy-start(f32[2048]{0:T(1024)} %copy-done.87) | copy-start | bytes 24580
  843.9 58.6 %copy-start.90 = (f32[2048]{0:T(1024)S(1)}, f32[2048]{0:T(1024)}, u32[]{:S(2)}) copy-start(f32[2048]{0:T(1024)} %copy-done.89) | copy-start | bytes 24580
  843.9 58.6 %copy-start.99 = (f32[1,192]{1,0:T(1,128)S(1)}, f32[1,192]{1,0:T(1,128)}, u32[]{:S(2)}) copy-start(f32[1,192]{1,0:T(1,128)} %copy-done.98) | copy-start | bytes 2308
  843.9 71.3 %copy-start.34 = (f32[2048,192]{0,1:T(8,128)S(1)}, f32[2048,192]{0,1:T(8,128)}, u32[]{:S(2)}) copy-start(f32[2048,192]{0,1:T(8,128)} %copy-done.33) | copy-start | bytes 4718596
  843.9 105.9 %all-gather.29.cloned.1.call-start = ((), (), s32[]{:S(2)}) async-start(), calls=%async_computation.22 | async-start | bytes 3932160 | tf_op jit(solution)/shard_map/all_gather | solution.py:116
  920.1 199.4 %reduce-scatter.9.cloned.1.call-start = ((), (), s32[]{:S(2)}) async-start(), calls=%async_computation.15 | async-start | bytes 7864320 | tf_op jit(solution)/shard_map/reduce_scatter | solution.py:112
  928.8 266.8 %reduce-scatter.17.cloned.1.call-start = ((), (), s32[]{:S(2)}) async-start(), calls=%async_computation.23 | async-start | bytes 7864320 | tf_op jit(solution)/shard_map/reduce_scatter | solution.py:120
  1078.7 511.0 %all-reduce.12.cloned.1.call-start = ((), (), s32[]{:S(2)}) async-start(), calls=%async_computation.24 | async-start | bytes 28311552 | tf_op jit(solution)/shard_map/psum | solution.py:287
  1137.8 47.5 %copy-start.31 = (f32[2048,192]{0,1:T(8,128)S(1)}, f32[2048,192]{0,1:T(8,128)}, u32[]{:S(2)}) copy-start(f32[2048,192]{0,1:T(8,128)} %get-tuple-element.450) | copy-start | bytes 4718596
  1195.6 54.9 %copy-start.30 = (f32[2048,192]{0,1:T(8,128)S(1)}, f32[2048,192]{0,1:T(8,128)}, u32[]{:S(2)}) copy-start(f32[2048,192]{0,1:T(8,128)} %copy-done.29) | copy-start | bytes 4718596
  (139 other events, 701.2 us)
Sparse Core Ops, SparseCore 0:
  26.3 28.8 all-gather.10
  110.7 30.8 all-gather.12
  156.0 29.5 all-gather.14
  198.7 58.3 reduce-scatter.6
  277.9 29.5 all-gather.16
  363.1 28.7 all-gather.18
  406.7 29.5 all-gather.20
  438.5 28.5 all-gather.22
  483.6 58.3 reduce-scatter.10
  560.3 29.5 all-gather.24
  718.2 58.3 reduce-scatter.12
  797.4 29.5 all-gather.26
  844.0 58.3 reduce-scatter.14
  920.2 29.5 all-gather.28
  952.2 58.3 reduce-scatter.8
  1078.8 59.0 reduce-scatter.16
  1143.8 445.7 all-reduce.11
where the time goes:
time: 1620 us; the launch traced here: 1610 us
  waiting for transfers between devices  814 us (50%)
  matrix products  258 us (16%)
  local copies, waits for them, and re-layouts  183 us (11%)
  blocking collectives  177 us (11%)
  other arithmetic  154 us (10%)
    psum x1, waiting for transfers between devices, sum_replicas(): lax.psum((g_input_w, g_input_b, g_merge_w, g_merge_b, g_gain_one, g_shift...  336 us
    reduce_scatter x4, waiting for transfers between devices, gather_back(): lax.psum_scatter(partial_value, 'mp', scatter_dimension=1, tiled=True)  175 us
    all_gather x4, waiting for transfers between devices, spread_grad(): return lax.all_gather(grad.astype(jnp.bfloat16), 'mp', axis=1, tiled=True)  104 us
    all_gather x4, waiting for transfers between devices, norm_rows(): lax.all_gather((centered * gain + shift).astype(jnp.bfloat16), 'mp', axis...  103 us
    dynamic_update_slice x8, local copies, waits for them, and re-layouts, block_forward(): lax.map(attend_forward, (query, key_rot, value_low, segments))  60.7 us
    reduce_scatter x2, waiting for transfers between devices, branch_sum(): lax.psum_scatter(partial_value, 'mp', scatter_dimension=1, tiled=True)  56.6 us
    psum x1, blocking collectives, shards(): mix_grad = lax.psum(jnp.stack(mix_terms), ('dp', 'mp'))  44.8 us
    psum x4, blocking collectives, norm_rows(): lax.psum((jnp.sum(values, 1), jnp.sum(values * values, 1)), 'mp')  43.8 us
  transfers between devices with their start and end apart: 18, of which 16 were waited for; matrix products, arithmetic and copies ran while one was open for 15% of the time, Pallas kernels for 0%

commit v1 on v0

v1 whole, which is shorter than its diff:
```python
import functools

import jax
import jax.numpy as jnp
from jax import lax
from jax.experimental import pallas as pl
from jax.experimental.pallas import tpu as pltpu
from jax.sharding import PartitionSpec as P

HEAD = 64
HALF = HEAD // 2
LAYERS = 2
HISTORY = 4
EPS = 1e-05
MASKED = -1e30
BLK = 256
REACH = 512
TILE = 256
STRIP = 96
BF = jnp.bfloat16
F32 = jnp.float32
GELU_A = 0.7978845608028654
GELU_B = 0.044715
GAIN1, SHIFT1, GAIN2, SHIFT2, MERGE_B, REDUCE_B, INPUT_B, EXPAND_B = 0, 1, 2, 3, 4, 5, 6, 8


def dot(a, b, on):
    return lax.dot_general(a, b, (on, ((), ())), preferred_element_type=F32)


def nn(a, b):
    return dot(a, b, ((1,), (0,)))


def nt(a, b):
    return dot(a, b, ((1,), (1,)))


def tn(a, b):
    return dot(a, b, ((0,), (0,)))


def full(shape):
    return pl.BlockSpec(shape, lambda t: (0,) * len(shape))


def shape(dims, kind=BF):
    return jax.ShapeDtypeStruct(dims, kind)


def launch(kernel, name, steps, ins, outs, scratch, micros, vmem):
    return pl.pallas_call(
        kernel,
        grid=(steps,),
        in_specs=[spec for _, spec in ins],
        out_specs=[spec for _, spec in outs],
        out_shape=[struct for struct, _ in outs],
        scratch_shapes=scratch,
        compiler_params=pltpu.CompilerParams(
            dimension_semantics=("arbitrary",), vmem_limit_bytes=vmem * 1024 * 1024
        ),
        cost_estimate=pl.CostEstimate(
            flops=int(micros * 1.0e9), bytes_accessed=1 << 20, transcendentals=0
        ),
        name=name,
    )(*[operand for operand, _ in ins])


def whole(*operands):
    return [(operand, full(operand.shape)) for operand in operands]


def scalars(operand):
    return [(operand, pl.BlockSpec(memory_space=pltpu.SMEM))]


def out_full(dims, kind=BF):
    return (shape(dims, kind), full(dims))


def strips(size):
    return [slice(at, at + STRIP) for at in range(0, size, STRIP)]


def key_range(block):
    return max(0, block * BLK - REACH), (block + 1) * BLK


def mask_shape(length):
    return (length // BLK, min(length, REACH + BLK), BLK)


def fill_mask(mask, segments, length):
    line = segments[...]
    column = jnp.broadcast_to(line, (8, length)).T[:, 0:1]
    for block in range(length // BLK):
        low, high = key_range(block)
        span = high - low
        here = line[:, block * BLK : high]
        there = column[low:high, :]
        query_pos = lax.broadcasted_iota(jnp.int32, (span, BLK), 1) + block * BLK
        key_pos = lax.broadcasted_iota(jnp.int32, (span, BLK), 0) + low
        allowed = (here == there) & (key_pos <= query_pos)
        mask[block, :span, :] = jnp.where(allowed, 0.0, MASKED)


def normalise(source, target, stats, columns, gain, shift, width, length):
    total = jnp.zeros((1, length), F32)
    squares = jnp.zeros((1, length), F32)
    for rows in strips(width):
        x = source(rows)
        total += jnp.sum(x, 0, keepdims=True)
        squares += jnp.sum(x * x, 0, keepdims=True)
    mean = total * (1.0 / width)
    scale = lax.rsqrt(squares * (1.0 / width) - mean * mean + EPS)
    stats[0:1, :] = mean
    stats[1:2, :] = scale
    return mean, scale


def apply_norm(x, mean, scale, columns, gain, shift, rows):
    return ((x - mean) * scale * columns[rows, gain : gain + 1] + columns[rows, shift : shift + 1]).astype(BF)


def norm_back(x, stats, left, right, base, gain, width, length, grad_n, grad_gain, emit):
    mean, scale = stats[0:1, :], stats[1:2, :]
    first = jnp.zeros((1, length), F32)
    second = jnp.zeros((1, length), F32)
    for rows in strips(width):
        hat = (x[rows, :].astype(F32) - mean) * scale
        grad = left[rows, :].astype(F32) + right[rows, :].astype(F32)
        grad_n[rows, :] = grad.astype(BF)
        product = grad * hat
        grad_gain[rows, :] = product.astype(BF)
        column = gain[rows]
        first += jnp.sum(grad * column, 0, keepdims=True)
        second += jnp.sum(product * column, 0, keepdims=True)
    first = first * (1.0 / width)
    second = second * (1.0 / width)
    for rows in strips(width):
        hat = (x[rows, :].astype(F32) - mean) * scale
        grad = left[rows, :].astype(F32) + right[rows, :].astype(F32)
        emit(rows, base(rows) + scale * (grad * gain[rows] - first - hat * second))


def row_sums(value):
    return nt(jnp.ones((8, value.shape[1]), BF), value)


def attention_forward_kernel(mixing, heads, length, width, *refs):
    refs = list(refs)
    if mixing:
        coef, history_i, mid_i, left, right, before = refs[:6]
        del refs[:6]
    else:
        x_i = refs.pop(0)
    vectors, a0d, a0r, a1d, a1r, cos, sin, segments = refs[:8]
    del refs[:8]
    if mixing:
        y_o, x_o = refs[:2]
        del refs[:2]
    n1_o, st_o, q_o, k_o, v_o, o_o, lse_o, part_o, lin, mask, o_all = refs
    head = pl.program_id(0)
    quarter = (heads // 2) * HEAD
    half = width // 2

    @pl.when(head == 0)
    def _():
        columns = vectors[...].T
        if mixing:
            bias = before[...].T
            weight = coef[0, HISTORY]
            for rows in strips(width):
                y = (
                    mid_i[rows, :].astype(F32)
                    + left[rows, :].astype(F32)
                    + right[rows, :].astype(F32)
                    + bias[rows, REDUCE_B : REDUCE_B + 1]
                )
                y_o[rows, :] = y.astype(BF)
                x_o[rows, :] = (history_i[rows, :].astype(F32) + weight * y).astype(BF)
            source = x_o
        else:
            source = x_i
        mean, scale = normalise(
            lambda rows: source[rows, :].astype(F32), None, st_o, None, None, None, width, length
        )
        for rows in strips(width):
            n1_o[rows, :] = apply_norm(
                source[rows, :].astype(F32), mean, scale, columns, GAIN1, SHIFT1, rows
            )
        for index, (d, r) in enumerate(((a0d, a0r), (a1d, a1r))):
            at = index * 3 * quarter
            lin[at : at + 3 * quarter, :] = (
                nn(d[: 3 * quarter, :], n1_o[:half, :])
                + nn(r[: 3 * quarter, :], n1_o[half:, :])
                + columns[: 3 * quarter, INPUT_B + index : INPUT_B + index + 1]
            )
        fill_mask(mask, segments, length)

    c, s = cos[...], sin[...]
    group = head // (heads // 2)
    base = group * 3 * quarter + (head - group * (heads // 2)) * HEAD

    def rope(start):
        first = lin[pl.ds(pl.multiple_of(start, HALF), HALF), :]
        second = lin[pl.ds(pl.multiple_of(start + HALF, HALF), HALF), :]
        return jnp.concatenate([first * c - second * s, second * c + first * s], 0)

    q = (rope(base).astype(BF) * BF(HEAD**-0.5)).astype(BF)
    key = rope(base + quarter).astype(BF)
    v = lin[pl.ds(pl.multiple_of(base + 2 * quarter, HEAD), HEAD), :].astype(BF)
    q_o[0] = q
    k_o[0] = key
    v_o[0] = v
    for block in range(length // BLK):
        low, high = key_range(block)
        cols = slice(block * BLK, high)
        scores = tn(key[:, low:high], q[:, cols]) + mask[block, : high - low, :]
        peak = jnp.max(scores, 0, keepdims=True)
        weights = jnp.exp(scores - peak)
        total = jnp.sum(weights, 0, keepdims=True)
        out = (nn(v[:, low:high], weights.astype(BF)) * (1.0 / total)).astype(BF)
        o_o[0, :, cols] = out
        o_all[pl.ds(pl.multiple_of(head * HEAD, HEAD), HEAD), cols] = out
        lse_o[0, :, cols] = peak + jnp.log(total)

    @pl.when(head == heads - 1)
    def _():
        for at, own, other in ((0, a0d, a1d), (half, a0r, a1r)):
            part_o[at : at + half, :] = (
                tn(own[3 * quarter :, :], o_all[:quarter, :])
                + tn(other[3 * quarter :, :], o_all[quarter:, :])
            ).astype(BF)


def attention_forward(mix, x, vectors, weights, cos, sin, segments):
    length = segments.shape[1]
    rows, half = weights[0].shape
    width = 2 * half
    quarter = rows // 4
    heads = 2 * quarter // HEAD
    if mix is not None:
        ins = scalars(mix[0]) + whole(*mix[1:])
        outs = [out_full((width, length)), out_full((width, length))]
    else:
        ins = whole(x)
        outs = []
    ins = ins + whole(vectors, *weights, cos, sin, segments)
    per_head = lambda size: pl.BlockSpec((1, size, length), lambda h: (h, 0, 0))
    heads_out = (shape((heads, HEAD, length)), per_head(HEAD))
    outs = outs + [
        out_full((width, length)),
        out_full((8, length), F32),
        heads_out,
        heads_out,
        heads_out,
        heads_out,
        (shape((heads, 1, length), F32), per_head(1)),
        out_full((width, length)),
    ]
    return launch(
        functools.partial(attention_forward_kernel, mix is not None, heads, length, width),
        "attention_forward",
        heads,
        ins,
        outs,
        [
            pltpu.VMEM((6 * quarter, length), F32),
            pltpu.VMEM(mask_shape(length), F32),
            pltpu.VMEM((2 * quarter, length), BF),
        ],
        20,
        44,
    )


def attention_backward_kernel(opening, heads, length, width, *refs):
    refs = list(refs)
    if opening:
        grad_i, left, right, mid, st, vectors = refs[:6]
        del refs[:6]
    else:
        gmb = refs.pop(0)
    n1, ad, ar, cos, sin, segments, q_i, k_i, v_i, o_i, lse_i = refs[:11]
    del refs[:11]
    if opening:
        gmb, sums_o = refs[:2]
        del refs[:2]
    else:
        add = refs.pop(0)
    dw_o, db_o, part_o, mask, go_all, gl_all, gk_s, gv_s = refs[:8]
    del refs[:8]
    head = pl.program_id(0)
    quarter = heads * HEAD
    half = width // 2

    @pl.when(head == 0)
    def _():
        if opening:
            grad_n, grad_gain = refs
            columns = vectors[...].T
            norm_back(
                mid,
                st,
                left,
                right,
                lambda rows: grad_i[rows, :].astype(F32),
                columns[:, GAIN2 : GAIN2 + 1],
                width,
                length,
                grad_n,
                grad_gain,
                lambda rows, value: gmb.__setitem__((rows, slice(None)), value.astype(BF)),
            )
            sums_o[0:8, :] = row_sums(grad_gain[...])
            sums_o[8:16, :] = row_sums(grad_n[...])
            sums_o[16:24, :] = row_sums(gmb[...])
        go_all[...] = (
            nn(ad[3 * quarter :, :], gmb[:half, :]) + nn(ar[3 * quarter :, :], gmb[half:, :])
        ).astype(BF)
        o_flat = o_i[...].reshape(quarter, length)
        dw_o[0, 3 * quarter :, :] = nt(o_flat, gmb[:half, :]).astype(BF)
        dw_o[1, 3 * quarter :, :] = nt(o_flat, gmb[half:, :]).astype(BF)
        fill_mask(mask, segments, length)

    base = pl.multiple_of(head * HEAD, HEAD)
    q, key, v = q_i[0], k_i[0], v_i[0]
    go = go_all[pl.ds(base, HEAD), :]
    delta = jnp.sum(go.astype(F32) * o_i[head].astype(F32), 0, keepdims=True)
    gk_s[...] = jnp.zeros_like(gk_s)
    gv_s[...] = jnp.zeros_like(gv_s)
    gq_parts = []
    for block in range(length // BLK):
        low, high = key_range(block)
        cols = slice(block * BLK, high)
        scores = tn(key[:, low:high], q[:, cols]) + mask[block, : high - low, :]
        probs = jnp.exp(scores - lse_i[0, :, cols])
        grad_probs = tn(v[:, low:high], go[:, cols])
        grad_scores = (probs * (grad_probs - delta[:, cols])).astype(BF)
        gv_s[:, low:high] += nt(go[:, cols], probs.astype(BF))
        gk_s[:, low:high] += nt(q[:, cols], grad_scores)
        gq_parts.append(nn(key[:, low:high], grad_scores))
    c, s = cos[...], sin[...]

    def store(part, top, bottom):
        start = pl.multiple_of(part * quarter + base, HEAD)
        gl_all[pl.ds(start, HEAD), :] = jnp.concatenate([top, bottom], 0).astype(BF)

    gq = jnp.concatenate(gq_parts, 1) * HEAD**-0.5
    store(0, gq[:HALF] * c + gq[HALF:] * s, gq[HALF:] * c - gq[:HALF] * s)
    gk = gk_s[...]
    store(1, gk[:HALF] * c + gk[HALF:] * s, gk[HALF:] * c - gk[:HALF] * s)
    store(2, gv_s[:HALF, :], gv_s[HALF:, :])

    @pl.when(head == heads - 1)
    def _():
        db_o[...] = row_sums(gl_all[...])
        dw_o[0, : 3 * quarter, :] = nt(gl_all[...], n1[:half, :]).astype(BF)
        dw_o[1, : 3 * quarter, :] = nt(gl_all[...], n1[half:, :]).astype(BF)
        for at, w in ((0, ad), (half, ar)):
            value = tn(w[: 3 * quarter, :], gl_all[...])
            if not opening:
                value = value + add[at : at + half, :]
            part_o[at : at + half, :] = value.astype(part_o.dtype)


def attention_backward(opening, gmb, n1, weights, cos, sin, segments, saved, group, add):
    length = segments.shape[1]
    rows, half = weights[0].shape
    width = 2 * half
    quarter = rows // 4
    heads = quarter // HEAD
    q, key, v, o, lse = saved
    if opening is not None:
        ins = whole(*opening)
        outs = [out_full((width, length)), out_full((24, width), F32)]
        scratch = [pltpu.VMEM((width, length), BF), pltpu.VMEM((width, length), BF)]
    else:
        ins = whole(gmb)
        outs = []
        scratch = []
    at = group * heads
    per_head = lambda size: pl.BlockSpec((1, size, length), lambda h: (at + h, 0, 0))
    ins = ins + whole(n1, *weights, cos, sin, segments)
    ins = ins + [(item, per_head(HEAD)) for item in (q, key, v)]
    ins = ins + [(o, pl.BlockSpec((heads, HEAD, length), lambda h: (group, 0, 0))), (lse, per_head(1))]
    if add is not None:
        ins = ins + whole(add)
    outs = outs + [
        out_full((2, rows, half)),
        out_full((8, 3 * quarter), F32),
        out_full((width, length), BF if add is not None else F32),
    ]
    return launch(
        functools.partial(attention_backward_kernel, opening is not None, heads, length, width),
        "attention_backward",
        heads,
        ins,
        outs,
        [
            pltpu.VMEM(mask_shape(length), F32),
            pltpu.VMEM((quarter, length), BF),
            pltpu.VMEM((3 * quarter, length), BF),
            pltpu.VMEM((HEAD, length), F32),
            pltpu.VMEM((HEAD, length), F32),
        ]
        + scratch,
        14,
        44,
    )


def mlp_forward_kernel(tiles, length, width, *refs):
    (x, left, right, vectors, e0d, e0r, e1d, e1r, r0d, r0r, r1d, r1r) = refs[:12]
    mid_o, n2_o, st_o, u_o, act_o, part_o, acts, columns_s = refs[12:]
    t = pl.program_id(0)
    half = width // 2
    units = tiles * TILE

    @pl.when(t == 0)
    def _():
        columns = vectors[...].T
        columns_s[:, : columns.shape[1]] = columns
        for rows in strips(width):
            mid_o[rows, :] = (
                x[rows, :].astype(F32)
                + left[rows, :].astype(F32)
                + right[rows, :].astype(F32)
                + columns[rows, MERGE_B : MERGE_B + 1]
            ).astype(BF)
        mean, scale = normalise(
            lambda rows: mid_o[rows, :].astype(F32), None, st_o, None, None, None, width, length
        )
        for rows in strips(width):
            n2_o[rows, :] = apply_norm(
                mid_o[rows, :].astype(F32), mean, scale, columns, GAIN2, SHIFT2, rows
            )

    def expand(group, d, r):
        at = pl.multiple_of((t - group * tiles) * TILE, TILE)
        bias = columns_s[pl.ds(at, TILE), EXPAND_B + group : EXPAND_B + group + 1]
        u = tn(d[...], n2_o[:half, :]) + tn(r[...], n2_o[half:, :]) + bias
        act = (0.5 * u * (1.0 + jnp.tanh(GELU_A * (u + GELU_B * (u * u * u))))).astype(BF)
        u_o[...] = u.astype(BF)
        act_o[...] = act
        acts[pl.ds(pl.multiple_of(t * TILE, TILE), TILE), :] = act

    @pl.when(t < tiles)
    def _():
        expand(0, e0d, e0r)

    @pl.when(t >= tiles)
    def _():
        expand(1, e1d, e1r)

    @pl.when(t == 2 * tiles - 1)
    def _():
        for at, own, other in ((0, r0d, r1d), (half, r0r, r1r)):
            part_o[at : at + half, :] = (
                tn(own[...], acts[:units, :]) + tn(other[...], acts[units:, :])
            ).astype(BF)


def mlp_forward(x, left, right, vectors, expand, reduce):
    width, length = x.shape
    half, units = expand[0].shape
    tiles = units // TILE
    first = pl.BlockSpec((half, TILE), lambda t: (0, jnp.minimum(t, tiles - 1)))
    second = pl.BlockSpec((half, TILE), lambda t: (0, jnp.maximum(t - tiles, 0)))
    ins = whole(x, left, right, vectors)
    ins = ins + list(zip(expand, (first, first, second, second))) + whole(*reduce)
    per_tile = (shape((2 * units, length)), pl.BlockSpec((TILE, length), lambda t: (t, 0)))
    return launch(
        functools.partial(mlp_forward_kernel, tiles, length, width),
        "mlp_forward",
        2 * tiles,
        ins,
        [
            out_full((width, length)),
            out_full((width, length)),
            out_full((8, length), F32),
            per_tile,
            per_tile,
            out_full((width, length)),
        ],
        [pltpu.VMEM((2 * units, length), BF), pltpu.VMEM((width, 128), F32)],
        14,
        44,
    )


def mlp_backward_kernel(mode, tiles, length, width, *refs):
    refs = list(refs)
    half = width // 2
    units = tiles * TILE
    if mode == "last":
        coef, cot, mid, left, right, y0, vectors = refs[:7]
        del refs[:7]
    elif mode == "first":
        coef, cot, gmid, x, st, left, right, y0, vectors = refs[:9]
        del refs[:9]
    else:
        gyb = refs.pop(0)
    n2, u_i, act, rd, rr, ed, er = refs[:7]
    del refs[:7]
    if mode == "own":
        add = refs.pop(0)
    else:
        gyb = refs.pop(0)
        if mode == "first":
            gx_o = refs.pop(0)
        sums_o, dots_o = refs[:2]
        del refs[:2]
    g_o, be_o, part_o, gubs = refs[:4]
    del refs[:4]
    t = pl.program_id(0)

    if mode != "own":

        @pl.when(t == 0)
        def _():
            columns = vectors[...].T
            dots_o[...] = jnp.zeros_like(dots_o)
            if mode == "last":
                for rows in strips(width):
                    value = cot[rows, :].astype(F32)
                    gyb[rows, :] = (coef[1, HISTORY] * value).astype(BF)
                    y1 = (
                        mid[rows, :].astype(F32)
                        + left[rows, :].astype(F32)
                        + right[rows, :].astype(F32)
                        + columns[rows, REDUCE_B : REDUCE_B + 1]
                    )
                    dots_o[0:1, :] += jnp.sum(value * y0[rows, :].astype(F32), 0, keepdims=True)
                    dots_o[1:2, :] += jnp.sum(value * y1, 0, keepdims=True)
                sums_o[0:8, :] = row_sums(gyb[...])
            else:
                grad_n, grad_gain = refs

                def emit(rows, value):
                    gx_o[rows, :] = value.astype(BF)
                    gyb[rows, :] = (
                        coef[1, HISTORY - 1] * cot[rows, :].astype(F32) + coef[0, HISTORY] * value
                    ).astype(BF)
                    dots_o[0:1, :] += jnp.sum(value * y0[rows, :].astype(F32), 0, keepdims=True)

                norm_back(
                    x,
                    st,
                    left,
                    right,
                    lambda rows: gmid[rows, :].astype(F32),
                    columns[:, GAIN1 : GAIN1 + 1],
                    width,
                    length,
                    grad_n,
                    grad_gain,
                    emit,
                )
                sums_o[0:8, :] = row_sums(gyb[...])
                sums_o[8:16, :] = row_sums(grad_gain[...])
                sums_o[16:24, :] = row_sums(grad_n[...])

    ga = nn(rd[...], gyb[:half, :]) + nn(rr[...], gyb[half:, :])
    u = u_i[...].astype(F32)
    square = u * u
    th = jnp.tanh(GELU_A * u * (1.0 + GELU_B * square))
    slope = 0.5 * (1.0 + th) + (0.5 * GELU_A) * u * (1.0 - th * th) * (1.0 + (3.0 * GELU_B) * square)
    gub = (ga * slope).astype(BF)
    gubs[pl.ds(pl.multiple_of(t * TILE, TILE), TILE), :] = gub
    be_o[...] = row_sums(gub)
    g_o[0, 0] = nt(gub, n2[:half, :]).astype(BF)
    g_o[1, 0] = nt(gub, n2[half:, :]).astype(BF)
    g_o[0, 1] = nt(act[...], gyb[:half, :]).astype(BF)
    g_o[1, 1] = nt(act[...], gyb[half:, :]).astype(BF)

    @pl.when(t == tiles - 1)
    def _():
        for at, w in ((0, ed), (half, er)):
            value = nn(w[...], gubs[...])
            if mode == "own":
                value = value + add[at : at + half, :]
            part_o[at : at + half, :] = value.astype(part_o.dtype)


def mlp_backward(mode, opening, gyb, n2, u, act, group, reduce, expand, add):
    width, length = n2.shape
    half, units = expand[0].shape
    tiles = units // TILE
    outs = []
    scratch = [pltpu.VMEM((units, length), BF)]
    if mode == "own":
        ins = whole(gyb)
    else:
        ins = scalars(opening[0]) + whole(*opening[1:])
        outs = outs + [out_full((width, length))]
        if mode == "first":
            outs = outs + [out_full((width, length))]
            scratch = scratch + [pltpu.VMEM((width, length), BF), pltpu.VMEM((width, length), BF)]
        outs = outs + [out_full((24, width), F32), out_full((8, length), F32)]
    at = group * tiles
    per_tile = pl.BlockSpec((TILE, length), lambda t: (at + t, 0))
    reduce_tile = pl.BlockSpec((TILE, half), lambda t: (t, 0))
    ins = ins + whole(n2) + [(u, per_tile), (act, per_tile)]
    ins = ins + [(item, reduce_tile) for item in reduce] + whole(*expand)
    if add is not None:
        ins = ins + whole(add)
    outs = outs + [
        (shape((2, 2, units, half)), pl.BlockSpec((2, 2, TILE, half), lambda t: (0, 0, t, 0))),
        (shape((8, units), F32), pl.BlockSpec((8, TILE), lambda t: (0, t))),
        out_full((width, length), BF if add is not None else F32),
    ]
    return launch(
        functools.partial(mlp_backward_kernel, mode, tiles, length, width),
        "mlp_backward",
        tiles,
        ins,
        outs,
        scratch,
        13,
        44,
    )


def final_kernel(length, width, gmid, x, st, left, right, vectors, gx_o, sums_o, grad_n, grad_gain):
    columns = vectors[...].T
    norm_back(
        x,
        st,
        left,
        right,
        lambda rows: gmid[rows, :].astype(F32),
        columns[:, GAIN1 : GAIN1 + 1],
        width,
        length,
        grad_n,
        grad_gain,
        lambda rows, value: gx_o.__setitem__((rows, slice(None)), value.astype(BF)),
    )
    sums_o[0:8, :] = row_sums(grad_gain[...])
    sums_o[8:16, :] = row_sums(grad_n[...])


def final_backward(*operands):
    width, length = operands[0].shape
    return launch(
        functools.partial(final_kernel, length, width),
        "norm_backward",
        1,
        whole(*operands),
        [out_full((width, length)), out_full((16, width), F32)],
        [pltpu.VMEM((width, length), BF), pltpu.VMEM((width, length), BF)],
        5,
        32,
    )


def swap_core(value):
    size = lax.axis_size("mp")
    return lax.ppermute(value, "mp", [(i, i ^ 1) for i in range(size)])


def swap_row(value):
    size = lax.axis_size("mp")
    return lax.ppermute(value, "mp", [(i, i ^ 2) for i in range(size)])


def swap_dp(value, bit):
    size = lax.axis_size("dp")
    return lax.ppermute(value, "dp", [(i, i ^ bit) for i in range(size)])


def half_of(value, which, axis=0):
    size = value.shape[axis] // 2
    return lax.dynamic_slice_in_dim(value, which * size, size, axis)


def ordered(mine, theirs, which, axis=0):
    return jnp.where(
        which == 0,
        jnp.concatenate([mine, theirs], axis),
        jnp.concatenate([theirs, mine], axis),
    )


def spread(mine, flip, core):
    theirs = swap_row(mine)
    pair = ordered(mine[None], theirs[None], flip)
    other = swap_core(pair)
    return (
        jnp.where(
            core == 0,
            jnp.stack([pair[0], other[0], pair[1], other[1]]),
            jnp.stack([other[0], pair[0], other[1], pair[1]]),
        ),
        theirs,
    )


def to_row(value, row, core, flip):
    length = value.shape[1] // 2
    low = value.astype(BF)
    mine = lax.dynamic_slice_in_dim(low, row * length, length, 1)
    theirs = swap_row(lax.dynamic_slice_in_dim(low, (1 - row) * length, length, 1))
    pair = ordered(mine[None], theirs[None], flip)
    other = swap_core(pair)
    gathered = jnp.where(
        core == 0,
        jnp.stack([pair[0], other[0], pair[1], other[1]]),
        jnp.stack([other[0], pair[0], other[1], pair[1]]),
    )
    return gathered.reshape(4 * value.shape[0], length)


def from_row(pick, row, core, flip):
    mine = pick(2 * flip + core).astype(BF)
    sent = pick(2 * (1 - flip) + core).astype(BF)
    return ordered(mine, swap_row(sent), row, 1).astype(F32)


def fetch_other(low, bit):
    direct = swap_row(low)
    return direct, swap_dp(direct, 1)


def sum_dp(kept, sent, bits):
    value = (kept.astype(F32) + swap_dp(sent, 1).astype(F32)).astype(BF)
    for step in range(1, len(bits)):
        away = half_of(value, 1 - bits[step])
        value = (
            half_of(value, bits[step]).astype(F32) + swap_dp(away, 1 << step).astype(F32)
        ).astype(BF)
    for step in reversed(range(1, len(bits))):
        value = ordered(value, swap_dp(value, 1 << step), bits[step])
    return value, swap_dp(value, 1)


def add_rows(own, received):
    total = own.astype(F32) + received.astype(F32)
    return total.astype(BF)


def reduce_grad(own, other, bits):
    received = swap_row(other)
    return sum_dp(add_rows(own[0], received[0]), add_rows(own[1], received[1]), bits)


def shards(
    inputs,
    history,
    segment_ids,
    cotangent,
    input_weight,
    input_bias,
    merge_weight,
    merge_bias,
    first_gain,
    first_shift,
    second_gain,
    second_shift,
    expand_weight,
    expand_bias,
    reduce_weight,
    reduce_bias,
    depth_weights,
):
    member = lax.axis_index("mp")
    row, core = member // 2, member % 2
    dp = lax.axis_index("dp")
    bits = []
    size = lax.axis_size("dp")
    while (1 << len(bits)) < size:
        bits.append((dp >> len(bits)) & 1)
    bit = bits[0]
    flip = row ^ bit
    length = segment_ids.shape[1]
    part = inputs.shape[0]
    width = 4 * part
    half = width // 2
    units = expand_bias.shape[1]
    last = HISTORY - 1

    segments = lax.dynamic_slice_in_dim(segment_ids, row, 1, 0).astype(F32)
    frequency = 10000.0 ** (-jnp.arange(HALF, dtype=F32) * 2.0 / HEAD)
    angles = frequency[:, None] * jnp.arange(length, dtype=F32)[None, :]
    cos, sin = jnp.cos(angles), jnp.sin(angles)

    x0 = to_row(inputs, row, core, flip)

    small = jnp.concatenate(
        [
            item.reshape(LAYERS, -1)
            for item in (
                input_bias,
                expand_bias,
                first_gain,
                first_shift,
                second_gain,
                second_shift,
                merge_bias,
                reduce_bias,
            )
        ],
        1,
    )
    quarters, small_other = spread(small, flip, core)
    at = 3 * part + units
    wide = quarters[:, :, at:].reshape(4, LAYERS, 6, part).transpose(1, 2, 0, 3)
    wide = wide.reshape(LAYERS, 6, width)
    pair = jnp.stack([small, small_other], 1)
    input_rows = jnp.pad(pair[:, :, : 3 * part], ((0, 0), (0, 0), (0, width - 3 * part)))
    vectors = jnp.concatenate(
        [wide, input_rows, pair[:, :, 3 * part : at], jnp.zeros((LAYERS, 6, width), F32)], 1
    )

    attn_w, expand_w, reduce_w = [], [], []
    for l in range(LAYERS):
        merged = jnp.concatenate([input_weight[l].reshape(3 * part, width), merge_weight[l]], 0)
        for source, axis, held in (
            (merged, 1, attn_w),
            (expand_weight[l], 0, expand_w),
            (reduce_weight[l], 1, reduce_w),
        ):
            near = half_of(source, bit, axis).astype(BF)
            far = half_of(source, 1 - bit, axis).astype(BF)
            held.append((near, far) + fetch_other(near, bit))

    mixed_history = sum(depth_weights[0, j] * history[j] for j in range(HISTORY))
    hm0 = to_row(mixed_history, row, core, flip)
    cot = to_row(cotangent, row, core, flip)

    saved = []
    mix = None
    for l in range(LAYERS):
        vec = vectors[l]
        outs = attention_forward(
            mix, x0 if l == 0 else None, vec, attn_w[l], cos, sin, segments
        )
        if l == 0:
            x = x0
        else:
            y0, x = outs[:2]
            outs = outs[2:]
        n1, st1, q, k, v, o, lse, left = outs
        right = swap_core(left)
        mid, n2, st2, u, act, left = mlp_forward(x, left, right, vec, expand_w[l], reduce_w[l])
        right = swap_core(left)
        saved.append((x, n1, st1, (q, k, v, o, lse), mid, n2, st2, u, act, left, right))
        mix = (depth_weights, hm0, mid, left, right, vec)

    mid1, left1, right1 = saved[1][4], saved[1][9], saved[1][10]

    def tail_quarter(index):
        cut = lambda item: lax.dynamic_slice_in_dim(item, index * part, part, 0).astype(F32)
        bias = lax.dynamic_slice_in_dim(vectors[1, REDUCE_B], index * part, part, 0)
        y1 = cut(mid1) + cut(left1) + cut(right1) + bias[:, None]
        return depth_weights[1, last] * cut(y0) + depth_weights[1, last + 1] * y1

    output = sum(depth_weights[1, j] * history[j + 1] for j in range(last)) + from_row(
        tail_quarter, row, core, flip
    )

    totals = [None] * LAYERS
    sums = [{} for _ in range(LAYERS)]
    for l in reversed(range(LAYERS)):
        x, n1, st1, heads, mid, n2, st2, u, act, y_left, y_right = saved[l]
        vec = vectors[l]
        aw, ew, rw = attn_w[l], expand_w[l], reduce_w[l]
        if l == 1:
            opening = (depth_weights, cot, mid, y_left, y_right, y0, vec)
            gyb, wide_sums, dots1, g1, be1, partial = mlp_backward(
                "last", opening, None, n2, u, act, 1, rw[2:], ew[2:], None
            )
            sums[1]["reduce_b"] = wide_sums[0]
        else:
            opening = (depth_weights, cot, gmb, saved[1][0], saved[1][2], left, right, y0, vectors[1])
            gyb, gx1, wide_sums, dots0, g1, be1, partial = mlp_backward(
                "first", opening, None, n2, u, act, 1, rw[2:], ew[2:], None
            )
            sums[0]["reduce_b"] = wide_sums[0]
            sums[1]["gain1"], sums[1]["shift1"] = wide_sums[8], wide_sums[16]
        g0, be0, left = mlp_backward(
            "own", None, gyb, n2, u, act, 0, rw[:2], ew[:2], partial
        )
        right = swap_core(left)
        shape_two = (2, 2 * units, half)
        mlp_total = reduce_grad(g0.reshape(shape_two), g1.reshape(shape_two), bits)
        opening = (gyb, left, right, mid, st2, vec)
        gmb, wide_sums, a1, db1, partial = attention_backward(
            opening, None, n1, aw[2:], cos, sin, segments, heads, 1, None
        )
        sums[l]["gain2"], sums[l]["shift2"], sums[l]["merge_b"] = (
            wide_sums[0],
            wide_sums[8],
            wide_sums[16],
        )
        a0, db0, left = attention_backward(
            None, gmb, n1, aw[:2], cos, sin, segments, heads, 0, partial
        )
        right = swap_core(left)
        attn_total = reduce_grad(a0, a1, bits)
        totals[l] = (mlp_total, attn_total)
        sums[l]["pair"] = ((db0[0], be0[0]), (db1[0], be1[0]))
    gx0, wide_sums = final_backward(gmb, saved[0][0], saved[0][2], left, right, vectors[0])
    sums[0]["gain1"], sums[0]["shift1"] = wide_sums[0], wide_sums[8]

    def quarter_of(value):
        return lambda index: lax.dynamic_slice_in_dim(value, index * part, part, 0)

    g0_home = from_row(quarter_of(gx1), row, core, flip)
    input_grad = from_row(quarter_of(gx0), row, core, flip)

    history_out = []
    for j in range(HISTORY):
        term = depth_weights[0, j] * g0_home
        if j >= 1:
            term = term + depth_weights[1, j - 1] * cotangent
        history_out.append(term)

    def by_core(value):
        return jnp.where(core == 0, jnp.sum(value), 0.0)

    mix0 = [jnp.sum(g0_home * history[j]) for j in range(HISTORY)] + [by_core(dots0[0])]
    mix1 = [jnp.sum(cotangent * history[j + 1]) for j in range(last)] + [
        by_core(dots1[0]),
        by_core(dots1[1]),
    ]
    mix_sum = jnp.concatenate([jnp.stack(mix0), jnp.stack(mix1)])
    mix_sum = mix_sum + swap_core(mix_sum)

    names = ("gain1", "shift1", "gain2", "shift2", "merge_b", "reduce_b")
    lines = []
    for index, which in ((2 * flip + core, 0), (2 * (1 - flip) + core, 1)):
        line = []
        for l in range(LAYERS):
            stacked = jnp.stack([sums[l][name] for name in names])
            cut = lax.dynamic_slice_in_dim(stacked, index * part, part, 1)
            line += [sums[l]["pair"][which][0], sums[l]["pair"][which][1], cut.reshape(-1)]
        lines.append(jnp.concatenate(line + [mix_sum]))
    total = lines[0] + swap_row(lines[1])
    for step in range(len(bits)):
        total = total + swap_dp(total, 1 << step)
    mix_grad = total[-mix_sum.shape[0] :].reshape(LAYERS, HISTORY + 1)
    per_layer = total[: -mix_sum.shape[0]].reshape(LAYERS, -1)
    wide_out = [per_layer[:, at + i * part : at + (i + 1) * part] for i in range(6)]

    attn_t, expand_t, reduce_t = [], [], []
    for l in range(LAYERS):
        (near, far), (attn_near, attn_far) = totals[l]
        attn_t.append(ordered(attn_near, attn_far, bit, 1))
        expand_t.append(ordered(near[:units], far[:units], bit, 1).T)
        reduce_t.append(ordered(near[units:], far[units:], bit, 1))
    attn_t = jnp.stack(attn_t).astype(F32)
    expand_t = jnp.stack(expand_t).astype(F32)
    reduce_t = jnp.stack(reduce_t).astype(F32)
    return (
        output,
        input_grad,
        jnp.stack(history_out),
        attn_t[:, : 3 * part].reshape(LAYERS, 3, part, width),
        per_layer[:, : 3 * part].reshape(LAYERS, 3, part),
        attn_t[:, 3 * part :],
        wide_out[4],
        wide_out[0],
        wide_out[1],
        wide_out[2],
        wide_out[3],
        expand_t,
        per_layer[:, 3 * part : at],
        reduce_t,
        wide_out[5],
        mix_grad,
    )


def solution(mesh):
    in_specs = (
        P("mp", "dp"),
        P(None, "mp", "dp"),
        P("dp", None),
        P("mp", "dp"),
        P(None, None, "mp", None),
        P(None, None, "mp"),
        P(None, "mp", None),
        P(None, "mp"),
        P(None, "mp"),
        P(None, "mp"),
        P(None, "mp"),
        P(None, "mp"),
        P(None, None, "mp"),
        P(None, "mp"),
        P(None, "mp", None),
        P(None, "mp"),
        P(),
    )
    out_specs = (
        P("mp", "dp"),
        P("mp", "dp"),
        P(None, "mp", "dp"),
        P(None, None, "mp", None),
        P(None, None, "mp"),
        P(None, "mp", None),
        P(None, "mp"),
        P(None, "mp"),
        P(None, "mp"),
        P(None, "mp"),
        P(None, "mp"),
        P(None, None, "mp"),
        P(None, "mp"),
        P(None, "mp", None),
        P(None, "mp"),
        P(),
    )
    return jax.shard_map(shards, mesh=mesh, in_specs=in_specs, out_specs=out_specs, check_vma=False)
```

time: 1620 us -> 679 us (0.42)
  waiting for transfers between devices: 814 us -> 261 us
  matrix products: 258 us -> 0 us
  Pallas kernels: 0 us -> 187 us
  blocking collectives: 177 us -> 0 us
  local copies, waits for them, and re-layouts: 183 us -> 67.6 us
  other arithmetic: 154 us -> 84.8 us
  starting transfers between devices: 4.97 us -> 65 us
    psum x1 -> x0, waiting for transfers between devices: 336 us -> none  [sum_replicas(): lax.psum((g_input_w, g_input_b, g_merge_w, g_merge_b, g_gain_one, g_shift...]
    ppermute x0 -> x64, waiting for transfers between devices: none -> 261 us  [the longest x33 142 us: swap_dp(): return lax.ppermute(value, 'dp', [(i, i ^ bit) for i in range(size)])]
    dot_general x52 -> x0, matrix products: 258 us -> none  [the longest x4 37.1 us: attend_backward(): jnp.einsum('qhd,khd->hqk', grad_attended, value_low, preferred_element_ty...]
    all_gather x10 -> x0, waiting for transfers between devices: 238 us -> none  [the longest x4 104 us: spread_grad(): return lax.all_gather(grad.astype(jnp.bfloat16), 'mp', axis=1, tiled=True)]
    reduce_scatter x6 -> x0, waiting for transfers between devices: 232 us -> none  [the longest x4 175 us: gather_back(): lax.psum_scatter(partial_value, 'mp', scatter_dimension=1, tiled=True)]
    pallas_call x0 -> x13, Pallas kernels: none -> 187 us  [launch(): pl.pallas_call(kernel, grid=(steps,), in_specs=[spec for _, spec in ins],...]
    psum x10 -> x0, blocking collectives: 167 us -> none  [the longest x1 44.8 us: shards(): mix_grad = lax.psum(jnp.stack(mix_terms), ('dp', 'mp'))]
    ppermute x0 -> x64, starting transfers between devices: none -> 65 us  [the longest x33 42.7 us: swap_dp(): return lax.ppermute(value, 'dp', [(i, i ^ bit) for i in range(size)])]
  transfers between devices with their start and end apart: 18 -> 64, of which waited for: 16 -> 26; matrix products, arithmetic and copies ran while one was open for 15% -> 18% of each run, Pallas kernels for 0% -> 21%
where the time goes in v1:
time: 679 us; the launch traced here: 670 us
  waiting for transfers between devices  261 us (38%)
  Pallas kernels  187 us (28%)
  other arithmetic  84.8 us (12%)
  local copies, waits for them, and re-layouts  67.6 us (10%)
  starting transfers between devices  65 us (10%)
    pallas_call x13, Pallas kernels, launch(): pl.pallas_call(kernel, grid=(steps,), in_specs=[spec for _, spec in ins],...  187 us
    ppermute x33, waiting for transfers between devices, swap_dp(): return lax.ppermute(value, 'dp', [(i, i ^ bit) for i in range(size)])  142 us
    ppermute x18, waiting for transfers between devices, swap_row(): return lax.ppermute(value, 'mp', [(i, i ^ 2) for i in range(size)])  114 us
    ppermute x33, starting transfers between devices, swap_dp(): return lax.ppermute(value, 'dp', [(i, i ^ bit) for i in range(size)])  42.7 us
    unnamed x237, local copies, waits for them, and re-layouts  28.1 us
    ppermute x18, starting transfers between devices, swap_row(): return lax.ppermute(value, 'mp', [(i, i ^ 2) for i in range(size)])  20.8 us
    select_n x16, other arithmetic, ordered(): jnp.where(which == 0, jnp.concatenate([mine, theirs], axis), jnp.concaten...  14.7 us
  transfers between devices with their start and end apart: 64, of which 26 were waited for; matrix products, arithmetic and copies ran while one was open for 18% of the time, Pallas kernels for 21%

profile of v1, /device:TPU:0, one launch (start us, length us, event | category | flops | bytes accessed | tf_op | source)
XLA Modules:
  0.0 669.9 jit_solution(6428083930310178601)
XLA Ops:
  7.9 3.2 fusion.57
  14.1 3.6 fusion.56
  24.0 8.7 %collective-permute-done.6.refs_4_.refs_7_ = bf16[768,384]{1,0:T(8,128)(2,1)S(1)} collective-permute-done((bf16[768,384]{1,0:T(8,128)(2,1)S(1)}, bf16[768,384]{1,0:T(8,128)(2,1)S(1)}, u32[]{:S(2)}, u32[]{:S(2)}) %collective-permute-start.6) | collective-permute-done | bytes 589856 | tf_op jit(solution)/shard_map/ppermute | solution.py:666
  38.0 7.2 %collective-permute-done.7.refs_5_.refs_8_ = bf16[768,384]{1,0:T(8,128)(2,1)S(1)} collective-permute-done((bf16[768,384]{1,0:T(8,128)(2,1)S(1)}, bf16[768,384]{1,0:T(8,128)(2,1)S(1)}, u32[]{:S(2)}, u32[]{:S(2)}) %collective-permute-start.7) | collective-permute-done | bytes 589856 | tf_op jit(solution)/shard_map/ppermute | solution.py:671
  45.1 16.2 %attention_forward.2 = (bf16[768,1024]{1,0:T(8,128)(2,1)S(1)}, f32[8,1024]{1,0:T(8,128)S(1)}, bf16[6,64,1024]{2,1,0:T(8,128)(2,1)S(1)}, bf16[6,64,1024]{2,1,0:T(...) custom-call(bf16[768,1024]{1,0:T(8,128)(2,1)} %bitcast.191, ...), custom_call_target="tpu_custom_call" | custom-call | flops 20000000000 | bytes 1048576 | tf_op jit(solution)/shard_map/attention_forward/pallas_call | solution.py:52
  69.4 11.3 %collective-permute-done.11.refs_10_.refs_12_ = bf16[768,384]{1,0:T(8,128)(2,1)S(1)} collective-permute-done((bf16[768,384]{1,0:T(8,128)(2,1)S(1)}, bf16[768,384]{1,0:T(8,128)(2,1)S(1)}, u32[]{:S(2)}, u32[]{:S(2)}) %collective-permute-start.11) | collective-permute-done | bytes 589856 | tf_op jit(solution)/shard_map/ppermute | solution.py:666
  82.2 6.1 fusion.17
  88.9 5.7 collective-permute-done.12.refs_11_.refs_13_
  96.0 14.4 %mlp_forward.2 = (bf16[768,1024]{1,0:T(8,128)(2,1)S(1)}, bf16[768,1024]{1,0:T(8,128)(2,1)S(1)}, f32[8,1024]{1,0:T(8,128)S(1)}, bf16[1536,1024]{1,0:T(8,128)(2,1)...) custom-call(bf16[768,1024]{1,0:T(8,128)(2,1)} %bitcast.192, bf16[768,1024]{1,0:T(8,128)(2,1)} %copy-done.32, ...), custom_call_target="tpu_custom_call" | custom-call | flops 14000000000 | bytes 1048576 | tf_op jit(solution)/shard_map/mlp_forward/pallas_call | solution.py:52
  113.7 13.9 %collective-permute-done.14.refs_9_.refs_7_ = bf16[768,384]{1,0:T(8,128)(2,1)S(1)} collective-permute-done((bf16[768,384]{1,0:T(8,128)(2,1)S(1)}, bf16[768,384]{1,0:T(8,128)(2,1)S(1)}, u32[]{:S(2)}, u32[]{:S(2)}) %collective-permute-start.14) | collective-permute-done | bytes 589856 | tf_op jit(solution)/shard_map/ppermute | solution.py:666
  130.6 12.0 %collective-permute-done.15.refs_10_.refs_8_ = bf16[768,384]{1,0:T(8,128)(2,1)S(1)} collective-permute-done((bf16[768,384]{1,0:T(8,128)(2,1)S(1)}, bf16[768,384]{1,0:T(8,128)(2,1)S(1)}, u32[]{:S(2)}, u32[]{:S(2)}) %collective-permute-start.15) | collective-permute-done | bytes 589856 | tf_op jit(solution)/shard_map/ppermute | solution.py:671
  143.8 20.6 %attention_forward.3 = (bf16[768,1024]{1,0:T(8,128)(2,1)S(1)}, bf16[768,1024]{1,0:T(8,128)(2,1)S(1)}, bf16[768,1024]{1,0:T(8,128)(2,1)}, f32[8,1024]{1,0:T(8,128...) custom-call(f32[2,5]{1,0:T(2,128)S(1)} %copy-done.29, ...), custom_call_target="tpu_custom_call" | custom-call | flops 20000000000 | bytes 1048576 | tf_op jit(solution)/shard_map/attention_forward/pallas_call | solution.py:52
  169.7 12.8 %collective-permute-done.17.refs_6_.refs_12_ = bf16[384,768]{1,0:T(8,128)(2,1)S(1)} collective-permute-done((bf16[384,768]{1,0:T(8,128)(2,1)S(1)}, bf16[384,768]{1,0:T(8,128)(2,1)S(1)}, u32[]{:S(2)}, u32[]{:S(2)}) %collective-permute-start.17) | collective-permute-done | bytes 589856 | tf_op jit(solution)/shard_map/ppermute | solution.py:666
  184.0 10.8 %collective-permute-done.19.refs_10_ = bf16[768,384]{1,0:T(8,128)(2,1)S(1)} collective-permute-done((bf16[768,384]{1,0:T(8,128)(2,1)S(1)}, bf16[768,384]{1,0:T(8,128)(2,1)S(1)}, u32[]{:S(2)}, u32[]{:S(2)}) %collective-permute-start.19) | collective-permute-done | bytes 589856 | tf_op jit(solution)/shard_map/ppermute | solution.py:666
  197.7 11.9 %collective-permute-done.20.refs_11_ = bf16[768,384]{1,0:T(8,128)(2,1)S(1)} collective-permute-done((bf16[768,384]{1,0:T(8,128)(2,1)S(1)}, bf16[768,384]{1,0:T(8,128)(2,1)S(1)}, u32[]{:S(2)}, u32[]{:S(2)}) %collective-permute-start.20) | collective-permute-done | bytes 589856 | tf_op jit(solution)/shard_map/ppermute | solution.py:671
  210.8 14.3 %mlp_forward.3 = (bf16[768,1024]{1,0:T(8,128)(2,1)S(1)}, bf16[768,1024]{1,0:T(8,128)(2,1)S(1)}, f32[8,1024]{1,0:T(8,128)S(1)}, bf16[1536,1024]{1,0:T(8,128)(2,1)...) custom-call(bf16[768,1024]{1,0:T(8,128)(2,1)} %copy-done.47, bf16[768,1024]{1,0:T(8,128)(2,1)} %get-tuple-element.88.refs_1_, ...), custom_call_target="tpu_custom_call" | custom-call | flops 14000000000 | bytes 1048576 | tf_op jit(solution)/shard_map/mlp_forward/pallas_call | solution.py:52
  227.1 3.8 collective-permute-done.24
  231.4 15.2 %mlp_backward.4 = (bf16[768,1024]{1,0:T(8,128)(2,1)S(1)}, f32[24,768]{1,0:T(8,128)S(1)}, f32[8,1024]{1,0:T(8,128)S(1)}, bf16[2,2,768,384]{3,2,1,0:T(8,128)(2,1)}...) custom-call(f32[2,5]{1,0:T(2,128)S(1)} %copy-done.29, bf16[768,1024]{1,0:T(8,128)(2,1)S(1)} %bitcast.194, ...), custom_call_target="tpu_custom_call" | custom-call | flops 12999999488 | bytes 1048576 | tf_op jit(solution)/shard_map/mlp_backward/pallas_call | solution.py:52
  246.6 12.4 %mlp_backward.5 = (bf16[2,2,768,384]{3,2,1,0:T(8,128)(2,1)S(1)}, f32[8,768]{1,0:T(8,128)S(1)}, bf16[768,1024]{1,0:T(8,128)(2,1)}) custom-call(bf16[768,1024]{1,0:T(8,128)(2,1)S(1)} %get-tuple-element.94.refs_0_, bf16[768,1024]{1,0:T(8,128)(2,1)S(1)} %copy-done.53, bf16[1536,1024]{1,0:T(8,128)(2,1)} %get-tuple-element.92.refs_8_.refs_2_, ...), custom_call_target="tpu_custom_call" | custom-call | flops 12999999488 | bytes 1048576 | tf_op jit(solution)/shard_map/mlp_backward/pallas_call | solution.py:52
  259.9 4.5 add_convert_fusion.9
  274.0 17.1 %attention_backward.4 = (bf16[768,1024]{1,0:T(8,128)(2,1)S(1)}, f32[24,768]{1,0:T(8,128)S(1)}, bf16[2,768,384]{2,1,0:T(8,128)(2,1)S(1)}, f32[8,576]{1,0:T(8,128)S(1)}, f32[768,1024]{1,0:T(8,128)}) custom-call(bf16[768,1024]{1,0:T(8,128)(2,1)S(1)} %copy-done.51, bf16[768,1024]{1,0:T(8,128)(2,1)} %get-tuple-element.96.refs_1_, ...), custom_call_target="tpu_custom_call" | custom-call | flops 14000000000 | bytes 1048576 | tf_op jit(solution)/shard_map/attention_backward/pallas_call | solution.py:52
  291.2 12.2 %attention_backward.5 = (bf16[2,768,384]{2,1,0:T(8,128)(2,1)S(1)}, f32[8,576]{1,0:T(8,128)S(1)}, bf16[768,1024]{1,0:T(8,128)(2,1)S(1)}) custom-call(bf16[768,1024]{1,0:T(8,128)(2,1)S(1)} %get-tuple-element.104.refs_0_.refs_2_, bf16[768,1024]{1,0:T(8,128)(2,1)} %get-tuple-element.98.refs_6_.refs_1_, bf16[768,384]{1,0:T(8,128)(2,1)S(1)} %copy-done.18, ...), custom_call_target="tpu_custom_call" | custom-call | flops 14000000000 | bytes 1048576 | tf_op jit(solution)/shard_map/attention_backward/pallas_call | solution.py:52
  304.9 6.3 fusion.19
  313.0 14.1 %collective-permute-done.57 = bf16[2,1536,384]{2,1,0:T(8,128)(2,1)S(1)} collective-permute-done((bf16[2,1536,384]{2,1,0:T(8,128)(2,1)}, bf16[2,1536,384]{2,1,0:T(8,128)(2,1)S(1)}, u32[]{:S(2)}, u32[]{:S(2)}) %collective-permute-start.57) | collective-permute-done | bytes 2359328 | tf_op jit(solution)/shard_map/ppermute | solution.py:666
  330.4 21.5 %collective-permute-done.38 = bf16[2,768,384]{2,1,0:T(8,128)(2,1)S(1)} collective-permute-done((bf16[2,768,384]{2,1,0:T(8,128)(2,1)S(1)}, bf16[2,768,384]{2,1,0:T(8,128)(2,1)S(1)}, u32[]{:S(2)}, u32[]{:S(2)}) %collective-permute-start.38) | collective-permute-done | bytes 1179680 | tf_op jit(solution)/shard_map/ppermute | solution.py:666
  355.7 19.5 %mlp_backward.6 = (bf16[768,1024]{1,0:T(8,128)(2,1)S(1)}, bf16[768,1024]{1,0:T(8,128)(2,1)S(1)}, f32[24,768]{1,0:T(8,128)S(1)}, f32[8,1024]{1,0:T(8,128)S(1)}, b...) custom-call(f32[2,5]{1,0:T(2,128)S(1)} %copy-done.29, bf16[768,1024]{1,0:T(8,128)(2,1)S(1)} %bitcast.195, ...), custom_call_target="tpu_custom_call" | custom-call | flops 12999999488 | bytes 1048576 | tf_op jit(solution)/shard_map/mlp_backward/pallas_call | solution.py:52
  375.3 12.3 %mlp_backward.7 = (bf16[2,2,768,384]{3,2,1,0:T(8,128)(2,1)S(1)}, f32[8,768]{1,0:T(8,128)S(1)}, bf16[768,1024]{1,0:T(8,128)(2,1)}) custom-call(bf16[768,1024]{1,0:T(8,128)(2,1)S(1)} %get-tuple-element.111.refs_0_, bf16[768,1024]{1,0:T(8,128)(2,1)S(1)} %copy-done.46, bf16[1536,1024]{1,0:T(8,128)(2,1)} %get-tuple-element.109.refs_10_.refs_2_, ...), custom_call_target="tpu_custom_call" | custom-call | flops 12999999488 | bytes 1048576 | tf_op jit(solution)/shard_map/mlp_backward/pallas_call | solution.py:52
  400.8 4.6 fusion.13
  405.4 4.5 concatenate.315
  413.8 4.2 fusion.5
  424.6 5.6 collective-permute-done.41
  430.2 3.4 collective-permute-start.42
  434.1 3.9 convert_multiply_fusion.7
  438.0 9.8 %collective-permute-done.42 = bf16[192,384]{1,0:T(8,128)(2,1)S(1)} collective-permute-done((bf16[192,384]{1,0:T(8,128)(2,1)S(1)}, bf16[192,384]{1,0:T(8,128)(2,1)S(1)}, u32[]{:S(2)}, u32[]{:S(2)}) %collective-permute-start.42) | collective-permute-done | bytes 147488 | tf_op jit(solution)/shard_map/ppermute | solution.py:671
  447.9 5.4 collective-permute-done.60
  453.6 17.1 %attention_backward.6 = (bf16[768,1024]{1,0:T(8,128)(2,1)S(1)}, f32[24,768]{1,0:T(8,128)S(1)}, bf16[2,768,384]{2,1,0:T(8,128)(2,1)S(1)}, f32[8,576]{1,0:T(8,128)S(1)}, f32[768,1024]{1,0:T(8,128)}) custom-call(bf16[768,1024]{1,0:T(8,128)(2,1)S(1)} %copy-done.49, bf16[768,1024]{1,0:T(8,128)(2,1)} %get-tuple-element.113.refs_1_, ...), custom_call_target="tpu_custom_call" | custom-call | flops 14000000000 | bytes 1048576 | tf_op jit(solution)/shard_map/attention_backward/pallas_call | solution.py:52
  470.7 12.0 %attention_backward.7 = (bf16[2,768,384]{2,1,0:T(8,128)(2,1)S(1)}, f32[8,576]{1,0:T(8,128)S(1)}, bf16[768,1024]{1,0:T(8,128)(2,1)S(1)}) custom-call(bf16[768,1024]{1,0:T(8,128)(2,1)S(1)} %get-tuple-element.121.refs_0_.gmid, bf16[768,1024]{1,0:T(8,128)(2,1)} %copy-done.54, bf16[768,384]{1,0:T(8,128)(2,1)S(1)} %copy-done.6, bf16[768,384]{1,0:T(8,128)(2,1)S(1)} %copy-done.4, ...), custom_call_target="tpu_custom_call" | custom-call | flops 14000000000 | bytes 1048576 | tf_op jit(solution)/shard_map/attention_backward/pallas_call | solution.py:52
  482.8 3.1 pad_maximum_fusion
  489.2 3.1 collective-permute-start.62
  496.3 18.0 %collective-permute-done.31 = bf16[2,768,384]{2,1,0:T(8,128)(2,1)S(1)} collective-permute-done((bf16[2,768,384]{2,1,0:T(8,128)(2,1)S(1)}, bf16[2,768,384]{2,1,0:T(8,128)(2,1)S(1)}, u32[]{:S(2)}, u32[]{:S(2)}) %collective-permute-start.31) | collective-permute-done | bytes 1179680 | tf_op jit(solution)/shard_map/ppermute | solution.py:666
  516.1 3.7 norm_backward.1
  519.9 22.1 %collective-permute-done.32 = bf16[768,384]{1,0:T(8,128)(2,1)} collective-permute-done((bf16[768,384]{1,0:T(8,128)(2,1)}, bf16[768,384]{1,0:T(8,128)(2,1)}, u32[]{:S(2)}, u32[]{:S(2)}) %collective-permute-start.32) | collective-permute-done | bytes 589856 | tf_op jit(solution)/shard_map/ppermute | solution.py:671
  559.2 10.8 %collective-permute-done.52 = bf16[768,384]{1,0:T(8,128)(2,1)} collective-permute-done((bf16[768,384]{1,0:T(8,128)(2,1)}, bf16[768,384]{1,0:T(8,128)(2,1)}, u32[]{:S(2)}, u32[]{:S(2)}) %collective-permute-start.52) | collective-permute-done | bytes 589856 | tf_op jit(solution)/shard_map/ppermute | solution.py:671
  577.8 10.8 %collective-permute-done.53 = bf16[384,384]{1,0:T(8,128)(2,1)S(1)} collective-permute-done((bf16[384,384]{1,0:T(8,128)(2,1)S(1)}, bf16[384,384]{1,0:T(8,128)(2,1)S(1)}, u32[]{:S(2)}, u32[]{:S(2)}) %collective-permute-start.53) | collective-permute-done | bytes 294944 | tf_op jit(solution)/shard_map/ppermute | solution.py:671
  596.3 9.9 %collective-permute-done.49 = f32[5002]{0:T(1024)S(1)} collective-permute-done((f32[5002]{0:T(1024)S(1)}, f32[5002]{0:T(1024)S(1)}, u32[]{:S(2)}, u32[]{:S(2)}) %collective-permute-start.49) | collective-permute-done | bytes 20040 | tf_op jit(solution)/shard_map/ppermute | solution.py:671
  619.3 9.7 %collective-permute-done.55 = bf16[768,384]{1,0:T(8,128)(2,1)} collective-permute-done((bf16[768,384]{1,0:T(8,128)(2,1)S(1)}, bf16[768,384]{1,0:T(8,128)(2,1)}, u32[]{:S(2)}, u32[]{:S(2)}) %collective-permute-start.55) | collective-permute-done | bytes 589856 | tf_op jit(solution)/shard_map/ppermute | solution.py:671
  639.0 18.8 %collective-permute-done.56 = bf16[1536,384]{1,0:T(8,128)(2,1)S(1)} collective-permute-done((bf16[1536,384]{1,0:T(8,128)(2,1)S(1)}, bf16[1536,384]{1,0:T(8,128)(2,1)S(1)}, u32[]{:S(2)}, u32[]{:S(2)}) %collective-permute-start.56) | collective-permute-done | bytes 1179680 | tf_op jit(solution)/shard_map/ppermute | solution.py:671
  660.7 6.0 copy.42
  (478 shorter events, 166.8 us)
Async XLA Ops:
  2.3 16.7 %collective-permute-start.4 = (f32[2,2496]{1,0:T(2,128)S(1)}, f32[2,2496]{1,0:T(2,128)S(1)}, u32[]{:S(2)}, u32[]{:S(2)}) collective-permute-start(f32[2,2496]{1,0:T(2,128)S(1)} %concatenate.281), channel_id=1, source_target_pairs={{0,2},{1,3},{2,0},{3,1},{4,6},{5,7},{6,4},{7,5},{8,10},{9,11},{10,... | collective-permute-start | bytes 59912 | tf_op jit(solution)/shard_map/ppermute | solution.py:666
  12.0 20.7 %collective-permute-start.6 = (bf16[768,384]{1,0:T(8,128)(2,1)S(1)}, bf16[768,384]{1,0:T(8,128)(2,1)S(1)}, u32[]{:S(2)}, u32[]{:S(2)}) collective-permute-start(bf16[768,384]{1,0:T(8,128)(2,1)S(1)} %get-tuple-element.234.refs_2_), channel_id=1, source_target_pairs={{0,2},{1,3},{2,0},{3,1},{4,6},{5,7},{6,4},{7,5},{8,10},{9,11},{10,... | collective-permute-start | bytes 1769480 | tf_op jit(solution)/shard_map/ppermute | solution.py:666
  17.8 50.3 %collective-permute-start.9 = (bf16[384,768]{1,0:T(8,128)(2,1)S(1)}, bf16[384,768]{1,0:T(8,128)(2,1)}, u32[]{:S(2)}, u32[]{:S(2)}) collective-permute-start(bf16[384,768]{1,0:T(8,128)(2,1)S(1)} %get-tuple-element.232.refs_4_.refs_6_), channel_id=1, source_target_pairs={{0,2},{1,3},{2,0},{3,1},{4,6},{5,7},{6,4},{7,5},{8,10},{9,11},{10,... | collective-permute-start | bytes 1769480 | tf_op jit(solution)/shard_map/ppermute | solution.py:666
  64.4 30.3 %collective-permute-start.8 = (bf16[768,1024]{1,0:T(8,128)(2,1)S(1)}, bf16[768,1024]{1,0:T(8,128)(2,1)S(1)}, u32[]{:S(2)}, u32[]{:S(2)}) collective-permute-start(bf16[768,1024]{1,0:T(8,128)(2,1)S(1)} %get-tuple-element.83.refs_1_), channel_id=1, source_target_pairs={{0,1},{1,0},{2,3},{3,2},{4,5},{5,4},{6,7},{7,6},{8,9},{9,8},{10,11... | collective-permute-start | bytes 4718600 | tf_op jit(solution)/shard_map/ppermute | solution.py:661
  68.1 20.8 %collective-permute-start.10 = (bf16[384,768]{1,0:T(8,128)(2,1)}, bf16[384,768]{1,0:T(8,128)(2,1)S(1)}, u32[]{:S(2)}, u32[]{:S(2)}) collective-permute-start(bf16[384,768]{1,0:T(8,128)(2,1)} %collective-permute-done.9.refs_6_.refs_14_), channel_id=1, source_target_pairs={{0,4},{4,0},{8,12},{12,8},{16,20},{20,16},{24,28},{28,24},{1,5},{5... | collective-permute-start | bytes 1769480 | tf_op jit(solution)/shard_map/ppermute | solution.py:671
  88.4 24.9 %collective-permute-start = (bf16[192,1024]{1,0:T(8,128)(2,1)S(1)}, bf16[192,1024]{1,0:T(8,128)(2,1)S(1)}, u32[]{:S(2)}, u32[]{:S(2)}) collective-permute-start(bf16[192,1024]{1,0:T(8,128)(2,1)S(1)} %get-tuple-element.252), channel_id=1, source_target_pairs={{0,2},{1,3},{2,0},{3,1},{4,6},{5,7},{6,4},{7,5},{8,10},{9,11},{10,... | collective-permute-start | bytes 1179656 | tf_op jit(solution)/shard_map/ppermute | solution.py:666
  111.6 30.9 %collective-permute-start.13 = (bf16[768,1024]{1,0:T(8,128)(2,1)S(1)}, bf16[768,1024]{1,0:T(8,128)(2,1)S(1)}, u32[]{:S(2)}, u32[]{:S(2)}) collective-permute-start(bf16[768,1024]{1,0:T(8,128)(2,1)S(1)} %get-tuple-element.85.refs_3_), channel_id=1, source_target_pairs={{0,1},{1,0},{2,3},{3,2},{4,5},{5,4},{6,7},{7,6},{8,9},{9,8},{10,11... | collective-permute-start | bytes 4718600 | tf_op jit(solution)/shard_map/ppermute | solution.py:661
  111.9 15.8 %collective-permute-start.14 = (bf16[768,384]{1,0:T(8,128)(2,1)S(1)}, bf16[768,384]{1,0:T(8,128)(2,1)S(1)}, u32[]{:S(2)}, u32[]{:S(2)}) collective-permute-start(bf16[768,384]{1,0:T(8,128)(2,1)S(1)} %get-tuple-element.226.refs_7_.refs_2_), channel_id=1, source_target_pairs={{0,2},{1,3},{2,0},{3,1},{4,6},{5,7},{6,4},{7,5},{8,10},{9,11},{10,... | collective-permute-start | bytes 1769480 | tf_op jit(solution)/shard_map/ppermute | solution.py:666
  113.5 15.7 %collective-permute-start.1 = (bf16[2,192,1024]{2,1,0:T(8,128)(2,1)S(1)}, bf16[2,192,1024]{2,1,0:T(8,128)(2,1)S(1)}, u32[]{:S(2)}, u32[]{:S(2)}) collective-permute-start(bf16[2,192,1024]{2,1,0:T(8,128)(2,1)S(1)} %maximum_select_fusion.11), channel_id=1, source_target_pairs={{0,1},{1,0},{2,3},{3,2},{4,5},{5,4},{6,7},{7,6},{8,9},{9,8},{10,11... | collective-permute-start | bytes 2359304 | tf_op jit(solution)/shard_map/ppermute | solution.py:661
  127.6 14.9 %collective-permute-start.15 = (bf16[768,384]{1,0:T(8,128)(2,1)S(1)}, bf16[768,384]{1,0:T(8,128)(2,1)S(1)}, u32[]{:S(2)}, u32[]{:S(2)}) collective-permute-start(bf16[768,384]{1,0:T(8,128)(2,1)S(1)} %collective-permute-done.14.refs_9_.refs_7_), channel_id=1, source_target_pairs={{0,4},{4,0},{8,12},{12,8},{16,20},{20,16},{24,28},{28,24},{1,5},{5... | collective-permute-start | bytes 1769480 | tf_op jit(solution)/shard_map/ppermute | solution.py:671
  166.1 43.5 %collective-permute-start.16 = (bf16[768,1024]{1,0:T(8,128)(2,1)}, bf16[768,1024]{1,0:T(8,128)(2,1)S(1)}, u32[]{:S(2)}, u32[]{:S(2)}) collective-permute-start(bf16[768,1024]{1,0:T(8,128)(2,1)} %get-tuple-element.88.refs_1_), channel_id=1, source_target_pairs={{0,1},{1,0},{2,3},{3,2},{4,5},{5,4},{6,7},{7,6},{8,9},{9,8},{10,11... | collective-permute-start | bytes 4718600 | tf_op jit(solution)/shard_map/ppermute | solution.py:661
  166.3 16.2 %collective-permute-start.17 = (bf16[384,768]{1,0:T(8,128)(2,1)S(1)}, bf16[384,768]{1,0:T(8,128)(2,1)S(1)}, u32[]{:S(2)}, u32[]{:S(2)}) collective-permute-start(bf16[384,768]{1,0:T(8,128)(2,1)S(1)} %get-tuple-element.224.refs_4_.refs_6_), channel_id=1, source_target_pairs={{0,2},{1,3},{2,0},{3,1},{4,6},{5,7},{6,4},{7,5},{8,10},{9,11},{10,... | collective-permute-start | bytes 1769480 | tf_op jit(solution)/shard_map/ppermute | solution.py:666
  168.4 26.4 %collective-permute-start.19 = (bf16[768,384]{1,0:T(8,128)(2,1)S(1)}, bf16[768,384]{1,0:T(8,128)(2,1)S(1)}, u32[]{:S(2)}, u32[]{:S(2)}) collective-permute-start(bf16[768,384]{1,0:T(8,128)(2,1)S(1)} %get-tuple-element.222.refs_8_.refs_4_), channel_id=1, source_target_pairs={{0,2},{1,3},{2,0},{3,1},{4,6},{5,7},{6,4},{7,5},{8,10},{9,11},{10,... | collective-permute-start | bytes 1769480 | tf_op jit(solution)/shard_map/ppermute | solution.py:666
  182.5 15.2 %collective-permute-start.18 = (bf16[384,768]{1,0:T(8,128)(2,1)S(1)}, bf16[384,768]{1,0:T(8,128)(2,1)S(1)}, u32[]{:S(2)}, u32[]{:S(2)}) collective-permute-start(bf16[384,768]{1,0:T(8,128)(2,1)S(1)} %collective-permute-done.17.refs_6_.refs_12_), channel_id=1, source_target_pairs={{0,4},{4,0},{8,12},{12,8},{16,20},{20,16},{24,28},{28,24},{1,5},{5... | collective-permute-start | bytes 1769480 | tf_op jit(solution)/shard_map/ppermute | solution.py:671
  196.4 30.0 %collective-permute-start.23 = (bf16[192,1024]{1,0:T(8,128)(2,1)S(1)}, bf16[192,1024]{1,0:T(8,128)(2,1)S(1)}, u32[]{:S(2)}, u32[]{:S(2)}) collective-permute-start(bf16[192,1024]{1,0:T(8,128)(2,1)S(1)} %get-tuple-element.240), channel_id=1, source_target_pairs={{0,2},{1,3},{2,0},{3,1},{4,6},{5,7},{6,4},{7,5},{8,10},{9,11},{10,... | collective-permute-start | bytes 1179656 | tf_op jit(solution)/shard_map/ppermute | solution.py:666
  264.5 40.4 %collective-permute-start.22 = (bf16[192,1024]{1,0:T(8,128)(2,1)}, bf16[192,1024]{1,0:T(8,128)(2,1)}, u32[]{:S(2)}, u32[]{:S(2)}) collective-permute-start(bf16[192,1024]{1,0:T(8,128)(2,1)} %get-tuple-element.196), channel_id=1, source_target_pairs={{0,2},{1,3},{2,0},{3,1},{4,6},{5,7},{6,4},{7,5},{8,10},{9,11},{10,... | collective-permute-start | bytes 1179656 | tf_op jit(solution)/shard_map/ppermute | solution.py:666
  268.3 58.8 %collective-permute-start.57 = (bf16[2,1536,384]{2,1,0:T(8,128)(2,1)}, bf16[2,1536,384]{2,1,0:T(8,128)(2,1)S(1)}, u32[]{:S(2)}, u32[]{:S(2)}) collective-permute-start(bf16[2,1536,384]{2,1,0:T(8,128)(2,1)} %bitcast.215), channel_id=1, source_target_pairs={{0,2},{1,3},{2,0},{3,1},{4,6},{5,7},{6,4},{7,5},{8,10},{9,11},{10,... | collective-permute-start | bytes 7077896 | tf_op jit(solution)/shard_map/ppermute | solution.py:666
  303.4 51.1 %collective-permute-start.26 = (bf16[768,1024]{1,0:T(8,128)(2,1)S(1)}, bf16[768,1024]{1,0:T(8,128)(2,1)S(1)}, u32[]{:S(2)}, u32[]{:S(2)}) collective-permute-start(bf16[768,1024]{1,0:T(8,128)(2,1)S(1)} %get-tuple-element.107.refs_5_), channel_id=1, source_target_pairs={{0,1},{1,0},{2,3},{3,2},{4,5},{5,4},{6,7},{7,6},{8,9},{9,8},{10,11... | collective-permute-start | bytes 4718600 | tf_op jit(solution)/shard_map/ppermute | solution.py:661
  303.5 48.4 %collective-permute-start.38 = (bf16[2,768,384]{2,1,0:T(8,128)(2,1)S(1)}, bf16[2,768,384]{2,1,0:T(8,128)(2,1)S(1)}, u32[]{:S(2)}, u32[]{:S(2)}) collective-permute-start(bf16[2,768,384]{2,1,0:T(8,128)(2,1)S(1)} %get-tuple-element.130), channel_id=1, source_target_pairs={{0,2},{1,3},{2,0},{3,1},{4,6},{5,7},{6,4},{7,5},{8,10},{9,11},{10,... | collective-permute-start | bytes 3538952 | tf_op jit(solution)/shard_map/ppermute | solution.py:666
  329.0 81.0 %collective-permute-start.58 = (bf16[1536,384]{1,0:T(8,128)(2,1)}, bf16[1536,384]{1,0:T(8,128)(2,1)}, u32[]{:S(2)}, u32[]{:S(2)}) collective-permute-start(bf16[1536,384]{1,0:T(8,128)(2,1)} %fusion), channel_id=1, source_target_pairs={{0,4},{4,0},{8,12},{12,8},{16,20},{20,16},{24,28},{28,24},{1,5},{5... | collective-permute-start | bytes 3538952 | tf_op jit(solution)/shard_map/ppermute | solution.py:671
  353.1 43.1 %collective-permute-start.39 = (bf16[768,384]{1,0:T(8,128)(2,1)}, bf16[768,384]{1,0:T(8,128)(2,1)}, u32[]{:S(2)}, u32[]{:S(2)}) collective-permute-start(bf16[768,384]{1,0:T(8,128)(2,1)} %fusion.48), channel_id=1, source_target_pairs={{0,4},{4,0},{8,12},{12,8},{16,20},{20,16},{24,28},{28,24},{1,5},{5... | collective-permute-start | bytes 1769480 | tf_op jit(solution)/shard_map/ppermute | solution.py:671
  387.6 65.9 %collective-permute-start.27 = (bf16[768,1024]{1,0:T(8,128)(2,1)}, bf16[768,1024]{1,0:T(8,128)(2,1)}, u32[]{:S(2)}, u32[]{:S(2)}) collective-permute-start(bf16[768,1024]{1,0:T(8,128)(2,1)} %get-tuple-element.113.refs_1_), channel_id=1, source_target_pairs={{0,1},{1,0},{2,3},{3,2},{4,5},{5,4},{6,7},{7,6},{8,9},{9,8},{10,11... | collective-permute-start | bytes 4718600 | tf_op jit(solution)/shard_map/ppermute | solution.py:661
  392.3 100.0 %collective-permute-start.50 = (bf16[2,1536,384]{2,1,0:T(8,128)(2,1)}, bf16[2,1536,384]{2,1,0:T(8,128)(2,1)}, u32[]{:S(2)}, u32[]{:S(2)}) collective-permute-start(bf16[2,1536,384]{2,1,0:T(8,128)(2,1)} %bitcast.214), channel_id=1, source_target_pairs={{0,2},{1,3},{2,0},{3,1},{4,6},{5,7},{6,4},{7,5},{8,10},{9,11},{10,... | collective-permute-start | bytes 7077896 | tf_op jit(solution)/shard_map/ppermute | solution.py:666
  397.6 20.4 %collective-permute-start.40 = (bf16[384,384]{1,0:T(8,128)(2,1)S(1)}, bf16[384,384]{1,0:T(8,128)(2,1)}, u32[]{:S(2)}, u32[]{:S(2)}) collective-permute-start(bf16[384,384]{1,0:T(8,128)(2,1)S(1)} %constant_dynamic-slice_fusion.6), channel_id=1, source_target_pairs={{0,8},{4,12},{8,0},{12,4},{16,24},{20,28},{24,16},{28,20},{1,9},{5... | collective-permute-start | bytes 884744 | tf_op jit(solution)/shard_map/ppermute | solution.py:671
  409.9 76.0 %collective-permute-start.45 = (f32[10]{0:T(128)S(1)}, f32[10]{0:T(128)S(1)}, u32[]{:S(2)}, u32[]{:S(2)}) collective-permute-start(f32[10]{0:T(128)S(1)} %concatenate.315), channel_id=1, source_target_pairs={{0,1},{1,0},{2,3},{3,2},{4,5},{5,4},{6,7},{7,6},{8,9},{9,8},{10,11... | collective-permute-start | bytes 128 | tf_op jit(solution)/shard_map/ppermute | solution.py:661
  412.2 21.5 %collective-permute-start.59 = (bf16[768,384]{1,0:T(8,128)(2,1)S(1)}, bf16[768,384]{1,0:T(8,128)(2,1)S(1)}, u32[]{:S(2)}, u32[]{:S(2)}) collective-permute-start(bf16[768,384]{1,0:T(8,128)(2,1)S(1)} %constant_dynamic-slice_fusion.16), channel_id=1, source_target_pairs={{0,8},{4,12},{8,0},{12,4},{16,24},{20,28},{24,16},{28,20},{1,9},{5... | collective-permute-start | bytes 1769480 | tf_op jit(solution)/shard_map/ppermute | solution.py:671
  430.2 17.5 %collective-permute-start.42 = (bf16[192,384]{1,0:T(8,128)(2,1)S(1)}, bf16[192,384]{1,0:T(8,128)(2,1)S(1)}, u32[]{:S(2)}, u32[]{:S(2)}) collective-permute-start(bf16[192,384]{1,0:T(8,128)(2,1)S(1)} %add_convert_fusion.14), channel_id=1, source_target_pairs={{0,16},{4,20},{8,24},{12,28},{16,0},{20,4},{24,8},{28,12},{1,17},{... | collective-permute-start | bytes 442376 | tf_op jit(solution)/shard_map/ppermute | solution.py:671
  433.9 19.4 %collective-permute-start.60 = (bf16[384,384]{1,0:T(8,128)(2,1)S(1)}, bf16[384,384]{1,0:T(8,128)(2,1)S(1)}, u32[]{:S(2)}, u32[]{:S(2)}) collective-permute-start(bf16[384,384]{1,0:T(8,128)(2,1)S(1)} %constant_dynamic-slice_fusion.15), channel_id=1, source_target_pairs={{0,16},{4,20},{8,24},{12,28},{16,0},{20,4},{24,8},{28,12},{1,17},{... | collective-permute-start | bytes 884744 | tf_op jit(solution)/shard_map/ppermute | solution.py:671
  447.9 39.5 %collective-permute-start.43 = (bf16[384,384]{1,0:T(8,128)(2,1)S(1)}, bf16[384,384]{1,0:T(8,128)(2,1)S(1)}, u32[]{:S(2)}, u32[]{:S(2)}) collective-permute-start(bf16[384,384]{1,0:T(8,128)(2,1)S(1)} %maximum_select_fusion.23), channel_id=1, source_target_pairs={{0,8},{4,12},{8,0},{12,4},{16,24},{20,28},{24,16},{28,20},{1,9},{5... | collective-permute-start | bytes 884744 | tf_op jit(solution)/shard_map/ppermute | solution.py:671
  453.4 35.6 %collective-permute-start.61 = (bf16[384,384]{1,0:T(8,128)(2,1)S(1)}, bf16[384,384]{1,0:T(8,128)(2,1)S(1)}, u32[]{:S(2)}, u32[]{:S(2)}) collective-permute-start(bf16[384,384]{1,0:T(8,128)(2,1)S(1)} %add_convert_fusion.10), channel_id=1, source_target_pairs={{0,16},{4,20},{8,24},{12,28},{16,0},{20,4},{24,8},{28,12},{1,17},{... | collective-permute-start | bytes 884744 | tf_op jit(solution)/shard_map/ppermute | solution.py:671
  482.7 33.4 %collective-permute-start.28 = (bf16[768,1024]{1,0:T(8,128)(2,1)S(1)}, bf16[768,1024]{1,0:T(8,128)(2,1)S(1)}, u32[]{:S(2)}, u32[]{:S(2)}) collective-permute-start(bf16[768,1024]{1,0:T(8,128)(2,1)S(1)} %get-tuple-element.124.left), channel_id=1, source_target_pairs={{0,1},{1,0},{2,3},{3,2},{4,5},{5,4},{6,7},{7,6},{8,9},{9,8},{10,11... | collective-permute-start | bytes 4718600 | tf_op jit(solution)/shard_map/ppermute | solution.py:661
  486.0 28.4 %collective-permute-start.31 = (bf16[2,768,384]{2,1,0:T(8,128)(2,1)S(1)}, bf16[2,768,384]{2,1,0:T(8,128)(2,1)S(1)}, u32[]{:S(2)}, u32[]{:S(2)}) collective-permute-start(bf16[2,768,384]{2,1,0:T(8,128)(2,1)S(1)} %get-tuple-element.128), channel_id=1, source_target_pairs={{0,2},{1,3},{2,0},{3,1},{4,6},{5,7},{6,4},{7,5},{8,10},{9,11},{10,... | collective-permute-start | bytes 3538952 | tf_op jit(solution)/shard_map/ppermute | solution.py:666
  488.4 64.1 %collective-permute-start.44 = (bf16[768,384]{1,0:T(8,128)(2,1)}, bf16[768,384]{1,0:T(8,128)(2,1)}, u32[]{:S(2)}, u32[]{:S(2)}) collective-permute-start(bf16[768,384]{1,0:T(8,128)(2,1)} %maximum_select_fusion.19), channel_id=1, source_target_pairs={{0,4},{4,0},{8,12},{12,8},{16,20},{20,16},{24,28},{28,24},{1,5},{5... | collective-permute-start | bytes 1769480 | tf_op jit(solution)/shard_map/ppermute | solution.py:671
  489.2 82.1 %collective-permute-start.62 = (bf16[768,384]{1,0:T(8,128)(2,1)S(1)}, bf16[768,384]{1,0:T(8,128)(2,1)}, u32[]{:S(2)}, u32[]{:S(2)}) collective-permute-start(bf16[768,384]{1,0:T(8,128)(2,1)S(1)} %maximum_select_fusion.21), channel_id=1, source_target_pairs={{0,8},{4,12},{8,0},{12,4},{16,24},{20,28},{24,16},{28,20},{1,9},{5... | collective-permute-start | bytes 1769480 | tf_op jit(solution)/shard_map/ppermute | solution.py:671
  494.9 52.4 %collective-permute-start.51 = (bf16[1536,384]{1,0:T(8,128)(2,1)}, bf16[1536,384]{1,0:T(8,128)(2,1)}, u32[]{:S(2)}, u32[]{:S(2)}) collective-permute-start(bf16[1536,384]{1,0:T(8,128)(2,1)} %fusion.2), channel_id=1, source_target_pairs={{0,4},{4,0},{8,12},{12,8},{16,20},{20,16},{24,28},{28,24},{1,5},{5... | collective-permute-start | bytes 3538952 | tf_op jit(solution)/shard_map/ppermute | solution.py:671
  515.5 26.5 %collective-permute-start.32 = (bf16[768,384]{1,0:T(8,128)(2,1)}, bf16[768,384]{1,0:T(8,128)(2,1)}, u32[]{:S(2)}, u32[]{:S(2)}) collective-permute-start(bf16[768,384]{1,0:T(8,128)(2,1)} %fusion.46), channel_id=1, source_target_pairs={{0,4},{4,0},{8,12},{12,8},{16,20},{20,16},{24,28},{28,24},{1,5},{5... | collective-permute-start | bytes 1769480 | tf_op jit(solution)/shard_map/ppermute | solution.py:671
  551.3 18.6 %collective-permute-start.52 = (bf16[768,384]{1,0:T(8,128)(2,1)}, bf16[768,384]{1,0:T(8,128)(2,1)}, u32[]{:S(2)}, u32[]{:S(2)}) collective-permute-start(bf16[768,384]{1,0:T(8,128)(2,1)} %constant_dynamic-slice_fusion), channel_id=1, source_target_pairs={{0,8},{4,12},{8,0},{12,4},{16,24},{20,28},{24,16},{28,20},{1,9},{5... | collective-permute-start | bytes 1769480 | tf_op jit(solution)/shard_map/ppermute | solution.py:671
  555.5 19.1 %collective-permute-start.47 = (f32[5002]{0:T(1024)S(1)}, f32[5002]{0:T(1024)S(1)}, u32[]{:S(2)}, u32[]{:S(2)}) collective-permute-start(f32[5002]{0:T(1024)S(1)} %add.290), channel_id=1, source_target_pairs={{0,4},{4,0},{8,12},{12,8},{16,20},{20,16},{24,28},{28,24},{1,5},{5... | collective-permute-start | bytes 60032 | tf_op jit(solution)/shard_map/ppermute | solution.py:671
  557.3 19.2 %collective-permute-start.34 = (bf16[192,384]{1,0:T(8,128)(2,1)S(1)}, bf16[192,384]{1,0:T(8,128)(2,1)S(1)}, u32[]{:S(2)}, u32[]{:S(2)}) collective-permute-start(bf16[192,384]{1,0:T(8,128)(2,1)S(1)} %constant_dynamic-slice_fusion.7), channel_id=1, source_target_pairs={{0,16},{4,20},{8,24},{12,28},{16,0},{20,4},{24,8},{28,12},{1,17},{... | collective-permute-start | bytes 442376 | tf_op jit(solution)/shard_map/ppermute | solution.py:671
  571.2 17.4 %collective-permute-start.53 = (bf16[384,384]{1,0:T(8,128)(2,1)S(1)}, bf16[384,384]{1,0:T(8,128)(2,1)S(1)}, u32[]{:S(2)}, u32[]{:S(2)}) collective-permute-start(bf16[384,384]{1,0:T(8,128)(2,1)S(1)} %constant_dynamic-slice_fusion.18), channel_id=1, source_target_pairs={{0,16},{4,20},{8,24},{12,28},{16,0},{20,4},{24,8},{28,12},{1,17},{... | collective-permute-start | bytes 884744 | tf_op jit(solution)/shard_map/ppermute | solution.py:671
  574.0 39.6 %collective-permute-start.63 = (bf16[1536,384]{1,0:T(8,128)(2,1)}, bf16[1536,384]{1,0:T(8,128)(2,1)}, u32[]{:S(2)}, u32[]{:S(2)}) collective-permute-start(bf16[1536,384]{1,0:T(8,128)(2,1)} %maximum_select_fusion.7), channel_id=1, source_target_pairs={{0,4},{4,0},{8,12},{12,8},{16,20},{20,16},{24,28},{28,24},{1,5},{5... | collective-permute-start | bytes 3538952 | tf_op jit(solution)/shard_map/ppermute | solution.py:671
  574.6 17.0 %collective-permute-start.48 = (f32[5002]{0:T(1024)S(1)}, f32[5002]{0:T(1024)S(1)}, u32[]{:S(2)}, u32[]{:S(2)}) collective-permute-start(f32[5002]{0:T(1024)S(1)} %add.291), channel_id=1, source_target_pairs={{0,8},{4,12},{8,0},{12,4},{16,24},{20,28},{24,16},{28,20},{1,9},{5... | collective-permute-start | bytes 60032 | tf_op jit(solution)/shard_map/ppermute | solution.py:671
  576.6 29.6 %collective-permute-start.35 = (bf16[192,384]{1,0:T(8,128)(2,1)S(1)}, bf16[192,384]{1,0:T(8,128)(2,1)}, u32[]{:S(2)}, u32[]{:S(2)}) collective-permute-start(bf16[192,384]{1,0:T(8,128)(2,1)S(1)} %add_convert_fusion.15), channel_id=1, source_target_pairs={{0,16},{4,20},{8,24},{12,28},{16,0},{20,4},{24,8},{28,12},{1,17},{... | collective-permute-start | bytes 442376 | tf_op jit(solution)/shard_map/ppermute | solution.py:671
  589.5 18.0 %collective-permute-start.54 = (bf16[384,384]{1,0:T(8,128)(2,1)}, bf16[384,384]{1,0:T(8,128)(2,1)}, u32[]{:S(2)}, u32[]{:S(2)}) collective-permute-start(bf16[384,384]{1,0:T(8,128)(2,1)} %add_convert_fusion.11), channel_id=1, source_target_pairs={{0,16},{4,20},{8,24},{12,28},{16,0},{20,4},{24,8},{28,12},{1,17},{... | collective-permute-start | bytes 884744 | tf_op jit(solution)/shard_map/ppermute | solution.py:671
  595.6 36.4 %collective-permute-start.29 = (bf16[192,1024]{1,0:T(8,128)(2,1)}, bf16[192,1024]{1,0:T(8,128)(2,1)}, u32[]{:S(2)}, u32[]{:S(2)}) collective-permute-start(bf16[192,1024]{1,0:T(8,128)(2,1)} %get-tuple-element.212), channel_id=1, source_target_pairs={{0,2},{1,3},{2,0},{3,1},{4,6},{5,7},{6,4},{7,5},{8,10},{9,11},{10,... | collective-permute-start | bytes 1179656 | tf_op jit(solution)/shard_map/ppermute | solution.py:666
  608.8 20.3 %collective-permute-start.55 = (bf16[768,384]{1,0:T(8,128)(2,1)S(1)}, bf16[768,384]{1,0:T(8,128)(2,1)}, u32[]{:S(2)}, u32[]{:S(2)}) collective-permute-start(bf16[768,384]{1,0:T(8,128)(2,1)S(1)} %maximum_select_fusion.20), channel_id=1, source_target_pairs={{0,8},{4,12},{8,0},{12,4},{16,24},{20,28},{24,16},{28,20},{1,9},{5... | collective-permute-start | bytes 1769480 | tf_op jit(solution)/shard_map/ppermute | solution.py:671
  618.6 16.5 %collective-permute-start.37 = (bf16[768,384]{1,0:T(8,128)(2,1)S(1)}, bf16[768,384]{1,0:T(8,128)(2,1)S(1)}, u32[]{:S(2)}, u32[]{:S(2)}) collective-permute-start(bf16[768,384]{1,0:T(8,128)(2,1)S(1)} %maximum_select_fusion.18), channel_id=1, source_target_pairs={{0,4},{4,0},{8,12},{12,8},{16,20},{20,16},{24,28},{28,24},{1,5},{5... | collective-permute-start | bytes 1769480 | tf_op jit(solution)/shard_map/ppermute | solution.py:671
  630.7 27.1 %collective-permute-start.56 = (bf16[1536,384]{1,0:T(8,128)(2,1)S(1)}, bf16[1536,384]{1,0:T(8,128)(2,1)S(1)}, u32[]{:S(2)}, u32[]{:S(2)}) collective-permute-start(bf16[1536,384]{1,0:T(8,128)(2,1)S(1)} %maximum_select_fusion.5), channel_id=1, source_target_pairs={{0,4},{4,0},{8,12},{12,8},{16,20},{20,16},{24,28},{28,24},{1,5},{5... | collective-permute-start | bytes 3538952 | tf_op jit(solution)/shard_map/ppermute | solution.py:671
  (133 other events, 2257.5 us)

commit v2 on v1

--- a/solution.py
+++ b/solution.py
@@ -48,7 +48,7 @@
     return jax.ShapeDtypeStruct(dims, kind)
 
 
-def launch(kernel, name, steps, ins, outs, scratch, micros, vmem):
+def launch(kernel, name, steps, ins, outs, scratch, micros, vmem, aliases=None):
     return pl.pallas_call(
         kernel,
         grid=(steps,),
@@ -62,6 +62,7 @@
         cost_estimate=pl.CostEstimate(
             flops=int(micros * 1.0e9), bytes_accessed=1 << 20, transcendentals=0
         ),
+        input_output_aliases=aliases or {},
         name=name,
     )(*[operand for operand, _ in ins])
 
@@ -76,6 +77,25 @@
 
 def out_full(dims, kind=BF):
     return (shape(dims, kind), full(dims))
+
+
+class Pieces:
+    def __init__(self, refs):
+        self.refs = refs
+        self.size = refs[0].shape[0]
+
+    def __getitem__(self, index):
+        rows = index[0]
+        at = rows.start // self.size
+        return self.refs[at][slice(rows.start - at * self.size, rows.stop - at * self.size), :]
+
+    def store(self, at, value):
+        for start in range(0, value.shape[0], self.size):
+            self.refs[(at + start) // self.size][...] = value[start : start + self.size].astype(BF)
+
+
+def out_pieces(width, length):
+    return [out_full((width // 4, length)) for _ in range(4)]
 
 
 def strips(size):
@@ -150,8 +170,9 @@
 def attention_forward_kernel(mixing, heads, length, width, *refs):
     refs = list(refs)
     if mixing:
-        coef, history_i, mid_i, left, right, before = refs[:6]
-        del refs[:6]
+        coef, history_i, mid_i = refs[:3]
+        left, right, before = Pieces(refs[3:7]), Pieces(refs[7:11]), refs[11]
+        del refs[:12]
     else:
         x_i = refs.pop(0)
     vectors, a0d, a0r, a1d, a1r, cos, sin, segments = refs[:8]
@@ -159,7 +180,9 @@
     if mixing:
         y_o, x_o = refs[:2]
         del refs[:2]
-    n1_o, st_o, q_o, k_o, v_o, o_o, lse_o, part_o, lin, mask, o_all = refs
+    n1_o, st_o, q_o, k_o, v_o, o_o, lse_o = refs[:7]
+    part_o = Pieces(refs[7:11])
+    lin, mask, o_all = refs[11:]
     head = pl.program_id(0)
     quarter = (heads // 2) * HEAD
     half = width // 2
@@ -228,10 +251,11 @@
     @pl.when(head == heads - 1)
     def _():
         for at, own, other in ((0, a0d, a1d), (half, a0r, a1r)):
-            part_o[at : at + half, :] = (
+            part_o.store(
+                at,
                 tn(own[3 * quarter :, :], o_all[:quarter, :])
-                + tn(other[3 * quarter :, :], o_all[quarter:, :])
-            ).astype(BF)
+                + tn(other[3 * quarter :, :], o_all[quarter:, :]),
+            )
 
 
 def attention_forward(mix, x, vectors, weights, cos, sin, segments):
@@ -257,8 +281,8 @@
         heads_out,
         heads_out,
         (shape((heads, 1, length), F32), per_head(1)),
-        out_full((width, length)),
     ]
+    outs = outs + out_pieces(width, length)
     return launch(
         functools.partial(attention_forward_kernel, mix is not None, heads, length, width),
         "attention_forward",
@@ -275,11 +299,28 @@
     )
 
 
-def attention_backward_kernel(opening, heads, length, width, *refs):
+def halves_of(refs, natural, place, half):
+    if not natural:
+        return [lambda index, value, ref=ref: ref.__setitem__(index, value.astype(BF)) for ref in refs]
+
+    def at(which):
+        cols = pl.ds(pl.multiple_of((place[0, 0] ^ which) * half, half), half)
+
+        def put(index, value):
+            refs[0][index[:-1] + (cols,)] = value.astype(BF)
+
+        return put
+
+    return [at(0), at(1)]
+
+
+def attention_backward_kernel(opening, natural, heads, length, width, *refs):
     refs = list(refs)
+    place = refs.pop(0)
     if opening:
-        grad_i, left, right, mid, st, vectors = refs[:6]
-        del refs[:6]
+        grad_i, mid, st, vectors = refs[0], refs[9], refs[10], refs[11]
+        left, right = Pieces(refs[1:5]), Pieces(refs[5:9])
+        del refs[:12]
     else:
         gmb = refs.pop(0)
     n1, ad, ar, cos, sin, segments, q_i, k_i, v_i, o_i, lse_i = refs[:11]
@@ -289,8 +330,17 @@
         del refs[:2]
     else:
         add = refs.pop(0)
-    dw_o, db_o, part_o, mask, go_all, gl_all, gk_s, gv_s = refs[:8]
-    del refs[:8]
+    count = 1 if natural else 2
+    put = halves_of(refs[:count], natural, place, width // 2)
+    db_o = refs[count]
+    del refs[: count + 1]
+    if opening:
+        part_o = refs.pop(0)
+    else:
+        part_o = Pieces(refs[:4])
+        del refs[:4]
+    mask, go_all, gl_all, gk_s, gv_s = refs[:5]
+    del refs[:5]
     head = pl.program_id(0)
     quarter = heads * HEAD
     half = width // 2
@@ -320,8 +370,9 @@
             nn(ad[3 * quarter :, :], gmb[:half, :]) + nn(ar[3 * quarter :, :], gmb[half:, :])
         ).astype(BF)
         o_flat = o_i[...].reshape(quarter, length)
-        dw_o[0, 3 * quarter :, :] = nt(o_flat, gmb[:half, :]).astype(BF)
-        dw_o[1, 3 * quarter :, :] = nt(o_flat, gmb[half:, :]).astype(BF)
+        below = (slice(3 * quarter, 4 * quarter), slice(None))
+        put[0](below, nt(o_flat, gmb[:half, :]))
+        put[1](below, nt(o_flat, gmb[half:, :]))
         fill_mask(mask, segments, length)
 
     base = pl.multiple_of(head * HEAD, HEAD)
@@ -356,16 +407,18 @@
     @pl.when(head == heads - 1)
     def _():
         db_o[...] = row_sums(gl_all[...])
-        dw_o[0, : 3 * quarter, :] = nt(gl_all[...], n1[:half, :]).astype(BF)
-        dw_o[1, : 3 * quarter, :] = nt(gl_all[...], n1[half:, :]).astype(BF)
+        above = (slice(0, 3 * quarter), slice(None))
+        put[0](above, nt(gl_all[...], n1[:half, :]))
+        put[1](above, nt(gl_all[...], n1[half:, :]))
         for at, w in ((0, ad), (half, ar)):
             value = tn(w[: 3 * quarter, :], gl_all[...])
-            if not opening:
-                value = value + add[at : at + half, :]
-            part_o[at : at + half, :] = value.astype(part_o.dtype)
-
-
-def attention_backward(opening, gmb, n1, weights, cos, sin, segments, saved, group, add):
+            if opening:
+                part_o[at : at + half, :] = value
+            else:
+                part_o.store(at, value + add[at : at + half, :])
+
+
+def attention_backward(place, natural, opening, gmb, n1, weights, cos, sin, segments, saved, group, add):
     length = segments.shape[1]
     rows, half = weights[0].shape
     width = 2 * half
@@ -373,11 +426,11 @@
     heads = quarter // HEAD
     q, key, v, o, lse = saved
     if opening is not None:
-        ins = whole(*opening)
+        ins = scalars(place) + whole(*opening)
         outs = [out_full((width, length)), out_full((24, width), F32)]
         scratch = [pltpu.VMEM((width, length), BF), pltpu.VMEM((width, length), BF)]
     else:
-        ins = whole(gmb)
+        ins = scalars(place) + whole(gmb)
         outs = []
         scratch = []
     at = group * heads
@@ -387,13 +440,13 @@
     ins = ins + [(o, pl.BlockSpec((heads, HEAD, length), lambda h: (group, 0, 0))), (lse, per_head(1))]
     if add is not None:
         ins = ins + whole(add)
-    outs = outs + [
-        out_full((2, rows, half)),
-        out_full((8, 3 * quarter), F32),
-        out_full((width, length), BF if add is not None else F32),
-    ]
+    outs = outs + ([out_full((rows, width))] if natural else [out_full((rows, half))] * 2)
+    outs = outs + [out_full((8, 3 * quarter), F32)]
+    outs = outs + (out_pieces(width, length) if add is not None else [out_full((width, length), F32)])
     return launch(
-        functools.partial(attention_backward_kernel, opening is not None, heads, length, width),
+        functools.partial(
+            attention_backward_kernel, opening is not None, natural, heads, length, width
+        ),
         "attention_backward",
         heads,
         ins,
@@ -411,9 +464,19 @@
     )
 
 
-def mlp_forward_kernel(tiles, length, width, *refs):
-    (x, left, right, vectors, e0d, e0r, e1d, e1r, r0d, r0r, r1d, r1r) = refs[:12]
-    mid_o, n2_o, st_o, u_o, act_o, part_o, acts, columns_s = refs[12:]
+def mlp_forward_kernel(merged, tiles, length, width, *refs):
+    refs = list(refs)
+    x, left, right, vectors = refs[0], Pieces(refs[1:5]), Pieces(refs[5:9]), refs[9]
+    e0d, e0r, e1d, e1r = refs[10:14]
+    del refs[:14]
+    if merged:
+        r0d, r0r, r1d, r1r = refs[:4]
+        del refs[:4]
+    mid_o, n2_o, st_o, u_o, act_o = refs[:5]
+    del refs[:5]
+    columns_s = refs.pop(0 if not merged else 4)
+    if merged:
+        part_o, acts = Pieces(refs[:4]), refs[4]
     t = pl.program_id(0)
     half = width // 2
     units = tiles * TILE
@@ -444,7 +507,8 @@
         act = (0.5 * u * (1.0 + jnp.tanh(GELU_A * (u + GELU_B * (u * u * u))))).astype(BF)
         u_o[...] = u.astype(BF)
         act_o[...] = act
-        acts[pl.ds(pl.multiple_of(t * TILE, TILE), TILE), :] = act
+        if merged:
+            acts[pl.ds(pl.multiple_of(t * TILE, TILE), TILE), :] = act
 
     @pl.when(t < tiles)
     def _():
@@ -454,52 +518,85 @@
     def _():
         expand(1, e1d, e1r)
 
-    @pl.when(t == 2 * tiles - 1)
-    def _():
-        for at, own, other in ((0, r0d, r1d), (half, r0r, r1r)):
-            part_o[at : at + half, :] = (
-                tn(own[...], acts[:units, :]) + tn(other[...], acts[units:, :])
-            ).astype(BF)
+    if merged:
+
+        @pl.when(t == 2 * tiles - 1)
+        def _():
+            for at, own, other in ((0, r0d, r1d), (half, r0r, r1r)):
+                part_o.store(at, tn(own[...], acts[:units, :]) + tn(other[...], acts[units:, :]))
 
 
 def mlp_forward(x, left, right, vectors, expand, reduce):
     width, length = x.shape
     half, units = expand[0].shape
     tiles = units // TILE
+    merged = reduce is not None
     first = pl.BlockSpec((half, TILE), lambda t: (0, jnp.minimum(t, tiles - 1)))
     second = pl.BlockSpec((half, TILE), lambda t: (0, jnp.maximum(t - tiles, 0)))
-    ins = whole(x, left, right, vectors)
-    ins = ins + list(zip(expand, (first, first, second, second))) + whole(*reduce)
+    ins = whole(x, *left, *right, vectors)
+    ins = ins + list(zip(expand, (first, first, second, second)))
     per_tile = (shape((2 * units, length)), pl.BlockSpec((TILE, length), lambda t: (t, 0)))
+    outs = [
+        out_full((width, length)),
+        out_full((width, length)),
+        out_full((8, length), F32),
+        per_tile,
+        per_tile,
+    ]
+    scratch = [pltpu.VMEM((width, 128), F32)]
+    if merged:
+        ins = ins + whole(*reduce)
+        outs = outs + out_pieces(width, length)
+        scratch = scratch + [pltpu.VMEM((2 * units, length), BF)]
     return launch(
-        functools.partial(mlp_forward_kernel, tiles, length, width),
+        functools.partial(mlp_forward_kernel, merged, tiles, length, width),
         "mlp_forward",
         2 * tiles,
         ins,
-        [
-            out_full((width, length)),
-            out_full((width, length)),
-            out_full((8, length), F32),
-            per_tile,
-            per_tile,
-            out_full((width, length)),
-        ],
-        [pltpu.VMEM((2 * units, length), BF), pltpu.VMEM((width, 128), F32)],
-        14,
+        outs,
+        scratch,
+        14 if merged else 10,
         44,
     )
 
 
-def mlp_backward_kernel(mode, tiles, length, width, *refs):
+def reduce_forward_kernel(units, half, act, *refs):
+    r0d, r0r, r1d, r1r = refs[:4]
+    part_o = Pieces(refs[4:])
+    for at, own, other in ((0, r0d, r1d), (half, r0r, r1r)):
+        part_o.store(at, tn(own[...], act[:units, :]) + tn(other[...], act[units:, :]))
+
+
+def reduce_forward(act, reduce):
+    units, half = reduce[0].shape
+    length = act.shape[1]
+    return launch(
+        functools.partial(reduce_forward_kernel, units, half),
+        "reduce_forward",
+        1,
+        whole(act, *reduce),
+        out_pieces(2 * half, length),
+        [],
+        4,
+        32,
+    )
+
+
+def mlp_backward_kernel(mode, natural, tiles, length, width, *refs):
     refs = list(refs)
+    place = refs.pop(0)
     half = width // 2
     units = tiles * TILE
     if mode == "last":
-        coef, cot, mid, left, right, y0, vectors = refs[:7]
-        del refs[:7]
+        coef, cot, mid = refs[:3]
+        left, right = Pieces(refs[3:7]), Pieces(refs[7:11])
+        y0, vectors = refs[11:13]
+        del refs[:13]
     elif mode == "first":
-        coef, cot, gmid, x, st, left, right, y0, vectors = refs[:9]
-        del refs[:9]
+        coef, cot, gmid, x, st = refs[:5]
+        left, right = Pieces(refs[5:9]), Pieces(refs[9:13])
+        y0, vectors = refs[13:15]
+        del refs[:15]
     else:
         gyb = refs.pop(0)
     n2, u_i, act, rd, rr, ed, er = refs[:7]
@@ -512,8 +609,17 @@
             gx_o = refs.pop(0)
         sums_o, dots_o = refs[:2]
         del refs[:2]
-    g_o, be_o, part_o, gubs = refs[:4]
-    del refs[:4]
+    count = 1 if natural else 2
+    put_expand = halves_of(refs[:count], natural, place, half)
+    put_reduce = halves_of(refs[count : 2 * count], natural, place, half)
+    be_o = refs[2 * count]
+    del refs[: 2 * count + 1]
+    if mode == "own":
+        part_o = Pieces(refs[:4])
+        del refs[:4]
+    else:
+        part_o = refs.pop(0)
+    gubs = refs.pop(0)
     t = pl.program_id(0)
 
     if mode != "own":
@@ -570,30 +676,31 @@
     gub = (ga * slope).astype(BF)
     gubs[pl.ds(pl.multiple_of(t * TILE, TILE), TILE), :] = gub
     be_o[...] = row_sums(gub)
-    g_o[0, 0] = nt(gub, n2[:half, :]).astype(BF)
-    g_o[1, 0] = nt(gub, n2[half:, :]).astype(BF)
-    g_o[0, 1] = nt(act[...], gyb[:half, :]).astype(BF)
-    g_o[1, 1] = nt(act[...], gyb[half:, :]).astype(BF)
+    every = (slice(None), slice(None))
+    for index, rows in enumerate((slice(0, half), slice(half, width))):
+        put_expand[index](every, nt(gub, n2[rows, :]))
+        put_reduce[index](every, nt(act[...], gyb[rows, :]))
 
     @pl.when(t == tiles - 1)
     def _():
         for at, w in ((0, ed), (half, er)):
             value = nn(w[...], gubs[...])
             if mode == "own":
-                value = value + add[at : at + half, :]
-            part_o[at : at + half, :] = value.astype(part_o.dtype)
-
-
-def mlp_backward(mode, opening, gyb, n2, u, act, group, reduce, expand, add):
+                part_o.store(at, value + add[at : at + half, :])
+            else:
+                part_o[at : at + half, :] = value
+
+
+def mlp_backward(place, natural, mode, opening, gyb, n2, u, act, group, reduce, expand, add):
     width, length = n2.shape
     half, units = expand[0].shape
     tiles = units // TILE
     outs = []
     scratch = [pltpu.VMEM((units, length), BF)]
     if mode == "own":
-        ins = whole(gyb)
+        ins = scalars(place) + whole(gyb)
     else:
-        ins = scalars(opening[0]) + whole(*opening[1:])
+        ins = scalars(place) + scalars(opening[0]) + whole(*opening[1:])
         outs = outs + [out_full((width, length))]
         if mode == "first":
             outs = outs + [out_full((width, length))]
@@ -606,13 +713,16 @@
     ins = ins + [(item, reduce_tile) for item in reduce] + whole(*expand)
     if add is not None:
         ins = ins + whole(add)
+    if natural:
+        outs = outs + [(shape((units, width)), pl.BlockSpec((TILE, width), lambda t: (t, 0)))] * 2
+    else:
+        outs = outs + [(shape((units, half)), reduce_tile)] * 4
     outs = outs + [
-        (shape((2, 2, units, half)), pl.BlockSpec((2, 2, TILE, half), lambda t: (0, 0, t, 0))),
         (shape((8, units), F32), pl.BlockSpec((8, TILE), lambda t: (0, t))),
-        out_full((width, length), BF if add is not None else F32),
     ]
+    outs = outs + (out_pieces(width, length) if add is not None else [out_full((width, length), F32)])
     return launch(
-        functools.partial(mlp_backward_kernel, mode, tiles, length, width),
+        functools.partial(mlp_backward_kernel, mode, natural, tiles, length, width),
         "mlp_backward",
         tiles,
         ins,
@@ -623,7 +733,10 @@
     )
 
 
-def final_kernel(length, width, gmid, x, st, left, right, vectors, gx_o, sums_o, grad_n, grad_gain):
+def final_kernel(length, width, *refs):
+    gmid, x, st = refs[:3]
+    left, right = Pieces(refs[3:7]), Pieces(refs[7:11])
+    vectors, gx_o, sums_o, grad_n, grad_gain = refs[11:]
     columns = vectors[...].T
     norm_back(
         x,
@@ -698,11 +811,11 @@
     )
 
 
-def to_row(value, row, core, flip):
+def row_steps(value, row, core, flip):
     length = value.shape[1] // 2
     low = value.astype(BF)
     mine = lax.dynamic_slice_in_dim(low, row * length, length, 1)
-    theirs = swap_row(lax.dynamic_slice_in_dim(low, (1 - row) * length, length, 1))
+    (theirs,) = yield [swap_row(lax.dynamic_slice_in_dim(low, (1 - row) * length, length, 1))]
     pair = ordered(mine[None], theirs[None], flip)
     other = swap_core(pair)
     gathered = jnp.where(
@@ -710,40 +823,152 @@
         jnp.stack([pair[0], other[0], pair[1], other[1]]),
         jnp.stack([other[0], pair[0], other[1], pair[1]]),
     )
-    return gathered.reshape(4 * value.shape[0], length)
-
-
-def from_row(pick, row, core, flip):
-    mine = pick(2 * flip + core).astype(BF)
-    sent = pick(2 * (1 - flip) + core).astype(BF)
-    return ordered(mine, swap_row(sent), row, 1).astype(F32)
-
-
-def fetch_other(low, bit):
-    direct = swap_row(low)
-    return direct, swap_dp(direct, 1)
-
-
-def sum_dp(kept, sent, bits):
-    value = (kept.astype(F32) + swap_dp(sent, 1).astype(F32)).astype(BF)
+    yield gathered.reshape(4 * value.shape[0], length)
+
+
+def home_steps(mine, sent, row):
+    (theirs,) = yield [swap_row(sent)]
+    yield ordered(mine, theirs, row, 1).astype(F32)
+
+
+def fetch_steps(near, far, relay):
+    (direct,) = yield [swap_row(near)]
+    (rest,) = yield [swap_dp(direct, 1) if relay else swap_row(far)]
+    yield direct, rest
+
+
+class Weight:
+    def __init__(self, near, far, relay=True):
+        self.own = (near, far)
+        self.chain = Chain(fetch_steps(near, far, relay))
+
+    def other(self):
+        return self.chain.finish()
+
+    def parts(self):
+        return self.own + tuple(self.other())
+
+
+def swap_pieces(pieces):
+    return [swap_core(piece) for piece in pieces]
+
+
+def add_kernel(count, *refs):
+    for a, b, out in zip(refs[:count], refs[count : 2 * count], refs[2 * count :]):
+        out[...] = (a[...].astype(F32) + b[...].astype(F32)).astype(BF)
+
+
+def add_all(mine, theirs):
+    return launch(
+        functools.partial(add_kernel, len(mine)),
+        "add",
+        1,
+        whole(*mine, *theirs),
+        [out_full(item.shape) for item in mine],
+        [],
+        2,
+        16,
+    )
+
+
+def add_low(mine, theirs):
+    return (mine.astype(F32) + theirs.astype(F32)).astype(BF)
+
+
+def assemble_kernel(turned, counts, halves, *refs):
+    if halves:
+        place, near, far = refs[:3]
+        scratch = refs[-1]
+        outs = refs[len(refs) - 1 - len(counts) : -1]
+        half = near.shape[1]
+        a, b = near[...].astype(F32), far[...].astype(F32)
+        first = place[0, 0] == 0
+        scratch[:, :half] = jnp.where(first, a, b)
+        scratch[:, half:] = jnp.where(first, b, a)
+    else:
+        scratch = refs[0]
+        outs = refs[len(refs) - len(counts) :]
+    at = 0
+    for out, count in zip(outs, counts):
+        value = scratch[at : at + count, :].astype(F32)
+        out[...] = (value.T if turned else value).reshape(out.shape)
+        at += count
+
+
+def assemble(total, place, layer, shapes, counts, turned, held):
+    halves = isinstance(total, tuple)
+    ins = scalars(place) + whole(*total) if halves else whole(total)
+    aliases = {}
+    if held is not None:
+        for index, item in enumerate(held):
+            aliases[len(ins)] = index
+            ins.append((item, pl.BlockSpec(memory_space=pl.ANY)))
+    outs = []
+    for dims in shapes:
+        block = pl.BlockSpec((1,) + dims[1:], lambda t, dims=dims: (layer,) + (0,) * (len(dims) - 1))
+        outs.append((shape(dims, F32), block))
+    rows = sum(counts)
+    scratch = [pltpu.VMEM((rows, 2 * total[0].shape[1]), F32)] if halves else []
+    return launch(
+        functools.partial(assemble_kernel, turned, counts, halves),
+        "assemble",
+        1,
+        ins,
+        outs,
+        scratch,
+        3,
+        24,
+        aliases,
+    )
+
+
+def reduce_steps(own, other, bits):
+    (near,) = yield [swap_row(other[0])]
+    near, far = yield [near, swap_row(other[1])]
+    near, far = add_all(own, (near, far))
+    got = yield [swap_dp(far, 1)]
+    (value,) = add_all((near,), got)
     for step in range(1, len(bits)):
         away = half_of(value, 1 - bits[step])
-        value = (
-            half_of(value, bits[step]).astype(F32) + swap_dp(away, 1 << step).astype(F32)
-        ).astype(BF)
+        got = yield [swap_dp(away, 1 << step)]
+        value = add_low(half_of(value, bits[step]), got[0])
     for step in reversed(range(1, len(bits))):
-        value = ordered(value, swap_dp(value, 1 << step), bits[step])
-    return value, swap_dp(value, 1)
-
-
-def add_rows(own, received):
-    total = own.astype(F32) + received.astype(F32)
-    return total.astype(BF)
-
-
-def reduce_grad(own, other, bits):
-    received = swap_row(other)
-    return sum_dp(add_rows(own[0], received[0]), add_rows(own[1], received[1]), bits)
+        got = yield [swap_dp(value, 1 << step)]
+        value = ordered(value, got[0], bits[step])
+    got = yield [swap_dp(value, 1)]
+    yield value, got[0]
+
+
+def whole_steps(own, other):
+    (got,) = yield [swap_row(other)]
+    yield add_all((own,), (got,))
+
+
+class Chain:
+    def __init__(self, steps):
+        self.steps = steps
+        self.held = None
+
+    def advance(self):
+        try:
+            self.held = self.steps.send(self.held)
+            return True
+        except StopIteration:
+            return False
+
+    def finish(self):
+        while self.advance():
+            pass
+        return self.held
+
+
+def pin(anchor, *chains):
+    for chain in chains:
+        chain.advance()
+    held = lax.optimization_barrier((anchor, [chain.held for chain in chains]))
+    for chain, value in zip(chains, held[1]):
+        chain.held = value
+    return held[0]
 
 
 def shards(
@@ -786,7 +1011,9 @@
     angles = frequency[:, None] * jnp.arange(length, dtype=F32)[None, :]
     cos, sin = jnp.cos(angles), jnp.sin(angles)
 
-    x0 = to_row(inputs, row, core, flip)
+    place = bit.reshape(1, 1).astype(jnp.int32)
+    x0_chain = Chain(row_steps(inputs, row, core, flip))
+    x0_chain.advance()
 
     small = jnp.concatenate(
         [
@@ -804,6 +1031,20 @@
         ],
         1,
     )
+    def low_halves(source, axis):
+        return half_of(source, bit, axis).astype(BF), half_of(source, 1 - bit, axis).astype(BF)
+
+    def merged(l, first, second):
+        return jnp.concatenate([first[l].reshape(3 * part, width), second[l]], 0)
+
+    attn_w = [Weight(*low_halves(merged(0, input_weight, merge_weight), 1))]
+    attn_w[0].chain.advance()
+    attn_w[0].chain.held, early, small = lax.optimization_barrier(
+        (attn_w[0].chain.held, (expand_weight, reduce_weight), small)
+    )
+    expand_w = [Weight(*low_halves(early[0][0], 0))]
+    expand_w[0].chain.advance()
+    reduce_w = [Weight(*low_halves(early[1][0], 1))]
     quarters, small_other = spread(small, flip, core)
     at = 3 * part + units
     wide = quarters[:, :, at:].reshape(4, LAYERS, 6, part).transpose(1, 2, 0, 3)
@@ -814,124 +1055,201 @@
         [wide, input_rows, pair[:, :, 3 * part : at], jnp.zeros((LAYERS, 6, width), F32)], 1
     )
 
-    attn_w, expand_w, reduce_w = [], [], []
-    for l in range(LAYERS):
-        merged = jnp.concatenate([input_weight[l].reshape(3 * part, width), merge_weight[l]], 0)
-        for source, axis, held in (
-            (merged, 1, attn_w),
-            (expand_weight[l], 0, expand_w),
-            (reduce_weight[l], 1, reduce_w),
-        ):
-            near = half_of(source, bit, axis).astype(BF)
-            far = half_of(source, 1 - bit, axis).astype(BF)
-            held.append((near, far) + fetch_other(near, bit))
-
-    mixed_history = sum(depth_weights[0, j] * history[j] for j in range(HISTORY))
-    hm0 = to_row(mixed_history, row, core, flip)
-    cot = to_row(cotangent, row, core, flip)
+    x0 = x0_chain.finish()
+    x0, late_weights, past = lax.optimization_barrier(
+        (x0, (input_weight, merge_weight, expand_weight, reduce_weight), history)
+    )
+    attn_w.append(Weight(*low_halves(merged(1, *late_weights[:2]), 1)))
+    expand_w.append(Weight(*low_halves(late_weights[2][1], 0)))
+    reduce_w.append(Weight(*low_halves(late_weights[3][1], 1), relay=False))
+    mixed_history = sum(depth_weights[0, j] * past[j] for j in range(HISTORY))
+    hm0 = Chain(row_steps(mixed_history, row, core, flip))
+    cot_chain = Chain(row_steps(cotangent, row, core, flip))
 
     saved = []
     mix = None
     for l in range(LAYERS):
         vec = vectors[l]
         outs = attention_forward(
-            mix, x0 if l == 0 else None, vec, attn_w[l], cos, sin, segments
+            mix, x0 if l == 0 else None, vec, attn_w[l].parts(), cos, sin, segments
         )
         if l == 0:
             x = x0
         else:
             y0, x = outs[:2]
             outs = outs[2:]
-        n1, st1, q, k, v, o, lse, left = outs
-        right = swap_core(left)
-        mid, n2, st2, u, act, left = mlp_forward(x, left, right, vec, expand_w[l], reduce_w[l])
-        right = swap_core(left)
+        n1, st1, q, k, v, o, lse = outs[:7]
+        left = list(outs[7:])
+        if l == 0:
+            left[0] = pin(left[0], expand_w[0].chain, reduce_w[0].chain, hm0)
+        else:
+            left[0] = pin(left[0], expand_w[1].chain, reduce_w[1].chain)
+        right = swap_pieces(left)
+        if l == 0:
+            mid, n2, st2, u, act = mlp_forward(x, left, right, vec, expand_w[0].parts(), None)
+            act = pin(act, attn_w[1].chain, reduce_w[0].chain)
+            left = reduce_forward(act, reduce_w[0].parts())
+            hm0 = hm0.finish()
+            right = swap_pieces(left)
+            right[0] = pin(right[0], attn_w[1].chain, expand_w[1].chain)
+        else:
+            mid, n2, st2, u, act, *left = mlp_forward(
+                x, left, right, vec, expand_w[1].parts(), reduce_w[1].parts()
+            )
+            left[0] = pin(left[0], cot_chain)
+            right = swap_pieces(left)
         saved.append((x, n1, st1, (q, k, v, o, lse), mid, n2, st2, u, act, left, right))
-        mix = (depth_weights, hm0, mid, left, right, vec)
-
+        mix = (depth_weights, hm0, mid, *left, *right, vec)
+
+    cot = cot_chain.finish()
     mid1, left1, right1 = saved[1][4], saved[1][9], saved[1][10]
 
+    def quarter_of(value, index):
+        return lax.dynamic_slice_in_dim(value, index * part, part, 0)
+
+    mine_at, sent_at = 2 * flip + core, 2 * (1 - flip) + core
+
     def tail_quarter(index):
-        cut = lambda item: lax.dynamic_slice_in_dim(item, index * part, part, 0).astype(F32)
-        bias = lax.dynamic_slice_in_dim(vectors[1, REDUCE_B], index * part, part, 0)
-        y1 = cut(mid1) + cut(left1) + cut(right1) + bias[:, None]
-        return depth_weights[1, last] * cut(y0) + depth_weights[1, last + 1] * y1
-
-    output = sum(depth_weights[1, j] * history[j + 1] for j in range(last)) + from_row(
-        tail_quarter, row, core, flip
-    )
-
-    totals = [None] * LAYERS
+        cut = lambda item: quarter_of(item, index).astype(F32)
+        pick = lambda items: jnp.where(
+            index < 2, jnp.where(index == 0, items[0], items[1]), jnp.where(index == 2, items[2], items[3])
+        ).astype(F32)
+        y1 = cut(mid1) + pick(left1) + pick(right1) + cut(vectors[1, REDUCE_B])[:, None]
+        return (depth_weights[1, last] * cut(y0) + depth_weights[1, last + 1] * y1).astype(BF)
+
+    chains = [{} for _ in range(LAYERS)]
     sums = [{} for _ in range(LAYERS)]
     for l in reversed(range(LAYERS)):
         x, n1, st1, heads, mid, n2, st2, u, act, y_left, y_right = saved[l]
         vec = vectors[l]
         aw, ew, rw = attn_w[l], expand_w[l], reduce_w[l]
+        natural = l == 1
+        count = 1 if natural else 2
         if l == 1:
-            opening = (depth_weights, cot, mid, y_left, y_right, y0, vec)
-            gyb, wide_sums, dots1, g1, be1, partial = mlp_backward(
-                "last", opening, None, n2, u, act, 1, rw[2:], ew[2:], None
+            opening = (depth_weights, cot, mid, *y_left, *y_right, y0, vec)
+            gyb, wide_sums, dots1, *grads = mlp_backward(
+                place, natural, "last", opening, None, n2, u, act, 1, rw.other(), ew.other(), None
             )
-            sums[1]["reduce_b"] = wide_sums[0]
         else:
-            opening = (depth_weights, cot, gmb, saved[1][0], saved[1][2], left, right, y0, vectors[1])
-            gyb, gx1, wide_sums, dots0, g1, be1, partial = mlp_backward(
-                "first", opening, None, n2, u, act, 1, rw[2:], ew[2:], None
+            right[0] = pin(right[0], chains[1]["attn"])
+            matrices = ("reduce", "expand", "attn")
+            for name in matrices:
+                chains[1][name].advance()
+            right[0], sums_1 = lax.optimization_barrier(
+                (right[0], [chains[1][name].held[0] for name in matrices])
             )
-            sums[0]["reduce_b"] = wide_sums[0]
+            sums_1 = lax.psum(sums_1, "dp")
+            opening = (
+                (depth_weights, cot, gmb, saved[1][0], saved[1][2], *left, *right, y0, vectors[1])
+            )
+            gyb, gx1, wide_sums, dots0, *grads = mlp_backward(
+                place, natural, "first", opening, None, n2, u, act, 1, rw.other(), ew.other(), None
+            )
             sums[1]["gain1"], sums[1]["shift1"] = wide_sums[8], wide_sums[16]
-        g0, be0, left = mlp_backward(
-            "own", None, gyb, n2, u, act, 0, rw[:2], ew[:2], partial
+            gx1_home = Chain(home_steps(quarter_of(gx1, mine_at), quarter_of(gx1, sent_at), row))
+        sums[l]["reduce_b"] = wide_sums[0]
+        e_other, r_other = grads[:count], grads[count : 2 * count]
+        be1, partial = grads[2 * count :]
+        *grads, be0, l0, l1, l2, l3 = mlp_backward(
+            place, natural, "own", None, gyb, n2, u, act, 0, rw.own, ew.own, partial
         )
-        right = swap_core(left)
-        shape_two = (2, 2 * units, half)
-        mlp_total = reduce_grad(g0.reshape(shape_two), g1.reshape(shape_two), bits)
-        opening = (gyb, left, right, mid, st2, vec)
-        gmb, wide_sums, a1, db1, partial = attention_backward(
-            opening, None, n1, aw[2:], cos, sin, segments, heads, 1, None
+        e_own, r_own, left = grads[:count], grads[count:], [l0, l1, l2, l3]
+        if natural:
+            right = swap_pieces(left)
+            chains[l]["reduce"] = Chain(whole_steps(r_own[0], r_other[0]))
+            chains[l]["expand"] = Chain(whole_steps(e_own[0], e_other[0]))
+            right[0] = pin(right[0], chains[l]["reduce"])
+        else:
+            chains[l]["reduce"] = Chain(reduce_steps(r_own, r_other, bits))
+            chains[l]["expand"] = Chain(reduce_steps(e_own, e_other, bits))
+            left[0] = pin(left[0], chains[l]["reduce"])
+            right = swap_pieces(left)
+            right[0] = pin(right[0], chains[l]["reduce"])
+        opening = (gyb, *left, *right, mid, st2, vec)
+        gmb, wide_sums, *grads, db1, partial = attention_backward(
+            place, natural, opening, None, n1, aw.other(), cos, sin, segments, heads, 1, None
         )
+        a_other = grads
         sums[l]["gain2"], sums[l]["shift2"], sums[l]["merge_b"] = (
             wide_sums[0],
             wide_sums[8],
             wide_sums[16],
         )
-        a0, db0, left = attention_backward(
-            None, gmb, n1, aw[:2], cos, sin, segments, heads, 0, partial
+        if l == 1:
+            gmb = pin(gmb, chains[l]["expand"])
+        else:
+            chains[0]["expand"].advance()
+            gmb = pin(gmb, chains[l]["reduce"], chains[l]["expand"])
+        *grads, db0, l0, l1, l2, l3 = attention_backward(
+            place, natural, None, gmb, n1, aw.own, cos, sin, segments, heads, 0, partial
         )
-        right = swap_core(left)
-        attn_total = reduce_grad(a0, a1, bits)
-        totals[l] = (mlp_total, attn_total)
+        left = [l0, l1, l2, l3]
+        if l == 0:
+            left[0] = pin(left[0], chains[0]["reduce"], chains[0]["expand"])
+        right = swap_pieces(left)
+        if natural:
+            chains[l]["attn"] = Chain(whole_steps(grads[0], a_other[0]))
+        else:
+            chains[l]["attn"] = Chain(reduce_steps(grads, a_other, bits))
         sums[l]["pair"] = ((db0[0], be0[0]), (db1[0], be1[0]))
-    gx0, wide_sums = final_backward(gmb, saved[0][0], saved[0][2], left, right, vectors[0])
+    chains[0]["attn"].advance()
+    right[0] = pin(
+        right[0], chains[0]["attn"], chains[0]["reduce"], chains[0]["expand"], gx1_home
+    )
+    gx0, wide_sums = final_backward(
+        gmb, saved[0][0], saved[0][2], *left, *right, vectors[0]
+    )
     sums[0]["gain1"], sums[0]["shift1"] = wide_sums[0], wide_sums[8]
 
-    def quarter_of(value):
-        return lambda index: lax.dynamic_slice_in_dim(value, index * part, part, 0)
-
-    g0_home = from_row(quarter_of(gx1), row, core, flip)
-    input_grad = from_row(quarter_of(gx0), row, core, flip)
-
+    final = chains[0]["attn"]
+
+    def onward(*others):
+        *waiting, chains_now = others
+        final.advance()
+        for chain in chains_now:
+            chain.advance()
+        final.held, held, waiting = lax.optimization_barrier(
+            (final.held, [chain.held for chain in chains_now], waiting)
+        )
+        for chain, value in zip(chains_now, held):
+            chain.held = value
+        return waiting
+
+    ahead = (chains[0]["reduce"], chains[0]["expand"])
+    gx0_home = Chain(home_steps(quarter_of(gx0, mine_at), quarter_of(gx0, sent_at), row))
+    past, late_cot = onward(history, cotangent, ahead + (gx0_home,))
+    g0_home = gx1_home.finish()
+    input_grad = gx0_home.finish()
     history_out = []
     for j in range(HISTORY):
         term = depth_weights[0, j] * g0_home
         if j >= 1:
-            term = term + depth_weights[1, j - 1] * cotangent
+            term = term + depth_weights[1, j - 1] * late_cot
         history_out.append(term)
+
+    past, late_cot, tail_mine, tail_sent = onward(
+        past, late_cot, tail_quarter(mine_at), tail_quarter(sent_at), ahead
+    )
 
     def by_core(value):
         return jnp.where(core == 0, jnp.sum(value), 0.0)
 
-    mix0 = [jnp.sum(g0_home * history[j]) for j in range(HISTORY)] + [by_core(dots0[0])]
-    mix1 = [jnp.sum(cotangent * history[j + 1]) for j in range(last)] + [
+    mix0 = [jnp.sum(g0_home * past[j]) for j in range(HISTORY)] + [by_core(dots0[0])]
+    mix1 = [jnp.sum(late_cot * past[j + 1]) for j in range(last)] + [
         by_core(dots1[0]),
         by_core(dots1[1]),
     ]
     mix_sum = jnp.concatenate([jnp.stack(mix0), jnp.stack(mix1)])
     mix_sum = mix_sum + swap_core(mix_sum)
+    output_home = Chain(home_steps(tail_mine, tail_sent, row))
+    (past,) = onward(past, ahead + (output_home,))
+    output = sum(depth_weights[1, j] * past[j + 1] for j in range(last)) + output_home.finish()
+    onward(ahead)
+    (sums_1,) = onward(sums_1, ahead)
 
     names = ("gain1", "shift1", "gain2", "shift2", "merge_b", "reduce_b")
     lines = []
-    for index, which in ((2 * flip + core, 0), (2 * (1 - flip) + core, 1)):
+    for index, which in ((mine_at, 0), (sent_at, 1)):
         line = []
         for l in range(LAYERS):
             stacked = jnp.stack([sums[l][name] for name in names])
@@ -945,30 +1263,35 @@
     per_layer = total[: -mix_sum.shape[0]].reshape(LAYERS, -1)
     wide_out = [per_layer[:, at + i * part : at + (i + 1) * part] for i in range(6)]
 
-    attn_t, expand_t, reduce_t = [], [], []
-    for l in range(LAYERS):
-        (near, far), (attn_near, attn_far) = totals[l]
-        attn_t.append(ordered(attn_near, attn_far, bit, 1))
-        expand_t.append(ordered(near[:units], far[:units], bit, 1).T)
-        reduce_t.append(ordered(near[units:], far[units:], bit, 1))
-    attn_t = jnp.stack(attn_t).astype(F32)
-    expand_t = jnp.stack(expand_t).astype(F32)
-    reduce_t = jnp.stack(reduce_t).astype(F32)
+    attn_t = expand_t = reduce_t = None
+    for l in reversed(range(LAYERS)):
+        total = [chains[l][name].finish() for name in matrices] if l == 0 else sums_1
+        reduce_t = assemble(total[0], place, l, [(LAYERS, units, width)], [units], False, reduce_t)
+        expand_t = assemble(total[1], place, l, [(LAYERS, width, units)], [units], True, expand_t)
+        attn_t = assemble(
+            total[2],
+            place,
+            l,
+            [(LAYERS, 3, part, width), (LAYERS, part, width)],
+            [3 * part, part],
+            False,
+            attn_t,
+        )
     return (
         output,
         input_grad,
         jnp.stack(history_out),
-        attn_t[:, : 3 * part].reshape(LAYERS, 3, part, width),
+        attn_t[0],
         per_layer[:, : 3 * part].reshape(LAYERS, 3, part),
-        attn_t[:, 3 * part :],
+        attn_t[1],
         wide_out[4],
         wide_out[0],
         wide_out[1],
         wide_out[2],
         wide_out[3],
-        expand_t,
+        expand_t[0],
         per_layer[:, 3 * part : at],
-        reduce_t,
+        reduce_t[0],
         wide_out[5],
         mix_grad,
     )

time: 679 us -> 560 us (0.82)
  waiting for transfers between devices: 261 us -> 123 us
  other arithmetic: 84.8 us -> 58.4 us
  Pallas kernels: 187 us -> 206 us
  local copies, waits for them, and re-layouts: 67.6 us -> 85.3 us
  between operations: 4.64 us -> 18 us
    ppermute x18 -> x24, waiting for transfers between devices: 114 us -> 36 us  [swap_row(): return lax.ppermute(value, 'mp', [(i, i ^ 2) for i in range(size)])]
    ppermute x33 -> x26, waiting for transfers between devices: 142 us -> 82.2 us  [swap_dp(): return lax.ppermute(value, 'dp', [(i, i ^ bit) for i in range(size)])]
    convert_element_type x26 -> x13, other arithmetic: 38.1 us -> 14.3 us  [the longest x2 8.14 us: tail_quarter(): (depth_weights[1, last] * cut(y0) + depth_weights[1, last + 1] * y1).asty...]
    pallas_call x13 -> x29, Pallas kernels: 187 us -> 206 us  [launch(): pl.pallas_call(kernel, grid=(steps,), in_specs=[spec for _, spec in ins],...]
    ppermute x33 -> x26, starting transfers between devices: 42.7 us -> 28.7 us  [swap_dp(): return lax.ppermute(value, 'dp', [(i, i ^ bit) for i in range(size)])]
    unnamed x237 -> x310, local copies, waits for them, and re-layouts: 28.1 us -> 37.1 us
    select_n x16 -> x10, other arithmetic: 14.7 us -> 6.89 us  [ordered(): jnp.where(which == 0, jnp.concatenate([mine, theirs], axis), jnp.concaten...]
    ppermute x13 -> x37, starting transfers between devices: 1.52 us -> 8.87 us  [swap_core(): return lax.ppermute(value, 'mp', [(i, i ^ 1) for i in range(size)])]
  transfers between devices with their start and end apart: 64 -> 88, of which waited for: 26 -> 31; matrix products, arithmetic and copies ran while one was open for 18% -> 18% of each run, Pallas kernels for 21% -> 31%
where the time goes in v2:
time: 560 us; the launch traced here: 554 us
  Pallas kernels  206 us (37%)
  waiting for transfers between devices  123 us (22%)
  local copies, waits for them, and re-layouts  85.3 us (15%)
  starting transfers between devices  63.3 us (11%)
  other arithmetic  58.4 us (10%)
  between operations  18 us (3%)
    pallas_call x29, Pallas kernels, launch(): pl.pallas_call(kernel, grid=(steps,), in_specs=[spec for _, spec in ins],...  206 us
    ppermute x26, waiting for transfers between devices, swap_dp(): return lax.ppermute(value, 'dp', [(i, i ^ bit) for i in range(size)])  82.2 us
    unnamed x310, local copies, waits for them, and re-layouts  37.1 us
    ppermute x24, waiting for transfers between devices, swap_row(): return lax.ppermute(value, 'mp', [(i, i ^ 2) for i in range(size)])  36 us
    ppermute x26, starting transfers between devices, swap_dp(): return lax.ppermute(value, 'dp', [(i, i ^ bit) for i in range(size)])  28.7 us
    ppermute x24, starting transfers between devices, swap_row(): return lax.ppermute(value, 'mp', [(i, i ^ 2) for i in range(size)])  25.7 us
    another operation x3, other arithmetic, shards(): jnp.stack(history_out)  12.4 us
  transfers between devices with their start and end apart: 88, of which 31 were waited for; matrix products, arithmetic and copies ran while one was open for 18% of the time, Pallas kernels for 31%

profile of v2, /device:TPU:0, one launch (start us, length us, event | category | flops | bytes accessed | tf_op | source)
XLA Modules:
  0.0 553.8 jit_solution(16543550664550849341)
XLA Ops:
  8.8 3.0 collective-permute-start
  19.2 2.6 collective-permute-done
  22.8 2.0 fusion.40
  24.9 8.9 %collective-permute-done.2.refs_4_.refs_14_ = bf16[768,384]{1,0:T(8,128)(2,1)} collective-permute-done((bf16[768,384]{1,0:T(8,128)(2,1)S(1)}, bf16[768,384]{1,0:T(8,128)(2,1)}, u32[]{:S(2)}, u32[]{:S(2)}) %collective-permute-start.2) | collective-permute-done | bytes 589856 | tf_op jit(solution)/shard_map/ppermute | solution.py:779
  55.9 6.1 %add_convert_fusion = bf16[1,192,2048]{2,1,0:T(8,128)(2,1)S(1)} fusion(f32[4,192,2048]{2,1,0:T(8,128)} %param.18, f32[]{:T(128)} %bitcast.9, f32[]{:T(128)} %bitcast.8, f32[]{:T(128)} %bitcast.7, f32[]{:T(128)} %bitcast.3), kind=kLoop, calls=%fused_computation.37 | loop fusion | flops 3145728 | bytes 7077904 | tf_op jit(solution)/shard_map/convert
  67.6 16.3 %attention_forward.2 = (bf16[768,1024]{1,0:T(8,128)(2,1)S(1)}, f32[8,1024]{1,0:T(8,128)S(1)}, bf16[6,64,1024]{2,1,0:T(8,128)(2,1)S(1)}, bf16[6,64,1024]{2,1,0:T(...) custom-call(bf16[768,1024]{1,0:T(8,128)(2,1)} %bitcast.94, ...), custom_call_target="tpu_custom_call" | custom-call | flops 20000000000 | bytes 1048576 | tf_op jit(solution)/shard_map/attention_forward/pallas_call | solution.py:52
  85.2 3.5 slice.314
  95.1 10.4 %mlp_forward.2 = (bf16[768,1024]{1,0:T(8,128)(2,1)S(1)}, bf16[768,1024]{1,0:T(8,128)(2,1)S(1)}, f32[8,1024]{1,0:T(8,128)S(1)}, bf16[1536,1024]{1,0:T(8,128)(2,1)}, bf16[1536,1024]{1,0:T(8,128)(2,1)}) custom-call(bf16[768,1024]{1,0:T(8,128)(2,1)S(1)} %bitcast.95, bf16[192,1024]{1,0:T(8,128)(2,1)S(1)} %get-tuple-element.218.refs_1_, ...), custom_call_target="tpu_custom_call" | custom-call | flops 10000000000 | bytes 1048576 | tf_op jit(solution)/shard_map/mlp_forward/pallas_call | solution.py:52
  112.5 3.7 reduce_forward.1
  120.0 3.5 collective-permute-done.18.refs_16_.refs_15_
  126.8 20.6 %attention_forward.3 = (bf16[768,1024]{1,0:T(8,128)(2,1)}, bf16[768,1024]{1,0:T(8,128)(2,1)}, bf16[768,1024]{1,0:T(8,128)(2,1)}, f32[8,1024]{1,0:T(8,128)S(1)}, ...) custom-call(f32[2,5]{1,0:T(2,128)S(1)} %copy-done.34, ...), custom_call_target="tpu_custom_call" | custom-call | flops 20000000000 | bytes 1048576 | tf_op jit(solution)/shard_map/attention_forward/pallas_call | solution.py:52
  151.0 14.2 %mlp_forward.3 = (bf16[768,1024]{1,0:T(8,128)(2,1)}, bf16[768,1024]{1,0:T(8,128)(2,1)}, f32[8,1024]{1,0:T(8,128)S(1)}, bf16[1536,1024]{1,0:T(8,128)(2,1)}, bf16[...) custom-call(bf16[768,1024]{1,0:T(8,128)(2,1)} %get-tuple-element.238, ...), custom_call_target="tpu_custom_call" | custom-call | flops 14000000000 | bytes 1048576 | tf_op jit(solution)/shard_map/mlp_forward/pallas_call | solution.py:52
  170.7 4.1 add_convert_fusion.1
  178.2 15.0 %mlp_backward.4 = (bf16[768,1024]{1,0:T(8,128)(2,1)S(1)}, f32[24,768]{1,0:T(8,128)S(1)}, f32[8,1024]{1,0:T(8,128)S(1)}, bf16[768,768]{1,0:T(8,128)(2,1)S(1)}, bf...) custom-call(s32[1,1]{1,0:T(1,128)} %bitcast.1.refs_0_, f32[2,5]{1,0:T(2,128)S(1)} %copy-done.34, ...), custom_call_target="tpu_custom_call" | custom-call | flops 12999999488 | bytes 1048576 | tf_op jit(solution)/shard_map/mlp_backward/pallas_call | solution.py:52
  195.3 12.2 %mlp_backward.5 = (bf16[768,768]{1,0:T(8,128)(2,1)S(1)}, bf16[768,768]{1,0:T(8,128)(2,1)S(1)}, f32[8,768]{1,0:T(8,128)S(1)}, bf16[192,1024]{1,0:T(8,128)(2,1)}, ...) custom-call(s32[1,1]{1,0:T(1,128)} %bitcast.1.refs_0_, ...), custom_call_target="tpu_custom_call" | custom-call | flops 12999999488 | bytes 1048576 | tf_op jit(solution)/shard_map/mlp_backward/pallas_call | solution.py:52
  208.6 4.1 add_convert_fusion.2
  217.0 6.9 %collective-permute-done.37.refs_1_ = bf16[768,768]{1,0:T(8,128)(2,1)} collective-permute-done((bf16[768,768]{1,0:T(8,128)(2,1)}, bf16[768,768]{1,0:T(8,128)(2,1)}, u32[]{:S(2)}, u32[]{:S(2)}) %collective-permute-start.37) | collective-permute-done | bytes 1179680 | tf_op jit(solution)/shard_map/ppermute | solution.py:779
  232.2 18.1 %attention_backward.4 = (bf16[768,1024]{1,0:T(8,128)(2,1)}, f32[24,768]{1,0:T(8,128)S(1)}, bf16[768,768]{1,0:T(8,128)(2,1)S(1)}, f32[8,576]{1,0:T(8,128)S(1)}, f32[768,1024]{1,0:T(8,128)}) custom-call(s32[1,1]{1,0:T(1,128)} %bitcast.1.refs_0_, bf16[768,1024]{1,0:T(8,128)(2,1)} %copy-done.94, bf16[192,1024]{1,0:T(8,128)(2,1)} %get-tuple-element.261.refs_2_, ...), custom_call_target="tpu_custom_call" | custom-call | flops 14000000000 | bytes 1048576 | tf_op jit(solution)/shard_map/attention_backward/pallas_call | solution.py:52
  252.2 13.0 %attention_backward.5 = (bf16[768,768]{1,0:T(8,128)(2,1)S(1)}, f32[8,576]{1,0:T(8,128)S(1)}, bf16[192,1024]{1,0:T(8,128)(2,1)S(1)}, bf16[192,1024]{1,0:T(8,128)(...) custom-call(s32[1,1]{1,0:T(1,128)} %bitcast.1.refs_0_, bf16[768,1024]{1,0:T(8,128)(2,1)S(1)} %copy-done.91, ...), custom_call_target="tpu_custom_call" | custom-call | flops 14000000000 | bytes 1048576 | tf_op jit(solution)/shard_map/attention_backward/pallas_call | solution.py:52
  266.2 2.8 add.285
  271.5 5.2 collective-permute-done.43.refs_1_
  282.2 20.6 %mlp_backward.6 = (bf16[768,1024]{1,0:T(8,128)(2,1)S(1)}, bf16[768,1024]{1,0:T(8,128)(2,1)}, f32[24,768]{1,0:T(8,128)S(1)}, f32[8,1024]{1,0:T(8,128)S(1)}, bf16[...) custom-call(s32[1,1]{1,0:T(1,128)} %bitcast.1.refs_0_, ...), custom_call_target="tpu_custom_call" | custom-call | flops 12999999488 | bytes 1048576 | tf_op jit(solution)/shard_map/mlp_backward/pallas_call | solution.py:52
  306.4 10.7 %mlp_backward.7 = (bf16[768,384]{1,0:T(8,128)(2,1)S(1)}, bf16[768,384]{1,0:T(8,128)(2,1)S(1)}, bf16[768,384]{1,0:T(8,128)(2,1)S(1)}, bf16[768,384]{1,0:T(8,128)(...) custom-call(s32[1,1]{1,0:T(1,128)} %bitcast.1.refs_0_, ...), custom_call_target="tpu_custom_call" | custom-call | flops 12999999488 | bytes 1048576 | tf_op jit(solution)/shard_map/mlp_backward/pallas_call | solution.py:52
  327.3 1.9 constant_dynamic-slice_fusion.2
  337.1 17.6 %attention_backward.6 = (bf16[768,1024]{1,0:T(8,128)(2,1)}, f32[24,768]{1,0:T(8,128)S(1)}, bf16[768,384]{1,0:T(8,128)(2,1)S(1)}, bf16[768,384]{1,0:T(8,128)(2,1)...) custom-call(s32[1,1]{1,0:T(1,128)} %bitcast.1.refs_0_, bf16[768,1024]{1,0:T(8,128)(2,1)} %copy-done.90, ...), custom_call_target="tpu_custom_call" | custom-call | flops 14000000000 | bytes 1048576 | tf_op jit(solution)/shard_map/attention_backward/pallas_call | solution.py:52
  356.8 2.3 collective-permute-done.55.refs_3_
  362.7 12.3 %attention_backward.7 = (bf16[768,384]{1,0:T(8,128)(2,1)S(1)}, bf16[768,384]{1,0:T(8,128)(2,1)S(1)}, f32[8,576]{1,0:T(8,128)S(1)}, bf16[192,1024]{1,0:T(8,128)(2...) custom-call(s32[1,1]{1,0:T(1,128)} %bitcast.1.refs_0_, ...), custom_call_target="tpu_custom_call" | custom-call | flops 14000000000 | bytes 1048576 | tf_op jit(solution)/shard_map/attention_backward/pallas_call | solution.py:52
  375.0 3.4 collective-permute-done.56
  379.2 1.9 collective-permute-start.62
  381.8 9.1 %collective-permute-done.60.refs_3_ = bf16[768,384]{1,0:T(8,128)(2,1)S(1)} collective-permute-done((bf16[768,384]{1,0:T(8,128)(2,1)S(1)}, bf16[768,384]{1,0:T(8,128)(2,1)S(1)}, u32[]{:S(2)}, u32[]{:S(2)}) %collective-permute-start.60) | collective-permute-done | bytes 589856 | tf_op jit(solution)/shard_map/ppermute | solution.py:779
  392.6 7.7 %collective-permute-done.62 = bf16[384,384]{1,0:T(8,128)(2,1)S(1)} collective-permute-done((bf16[384,384]{1,0:T(8,128)(2,1)S(1)}, bf16[384,384]{1,0:T(8,128)(2,1)S(1)}, u32[]{:S(2)}, u32[]{:S(2)}) %collective-permute-start.62) | collective-permute-done | bytes 294944 | tf_op jit(solution)/shard_map/ppermute | solution.py:784
  401.0 3.8 norm_backward.1
  412.7 2.9 collective-permute-start.65
  416.5 8.5 %collective-permute-done.66 = bf16[192,384]{1,0:T(8,128)(2,1)S(1)} collective-permute-done((bf16[192,384]{1,0:T(8,128)(2,1)S(1)}, bf16[192,384]{1,0:T(8,128)(2,1)S(1)}, u32[]{:S(2)}, u32[]{:S(2)}) %collective-permute-start.66) | collective-permute-done | bytes 147488 | tf_op jit(solution)/shard_map/ppermute | solution.py:784
  424.9 6.8 %collective-permute-done.65 = bf16[192,384]{1,0:T(8,128)(2,1)S(1)} collective-permute-done((bf16[192,384]{1,0:T(8,128)(2,1)S(1)}, bf16[192,384]{1,0:T(8,128)(2,1)S(1)}, u32[]{:S(2)}, u32[]{:S(2)}) %collective-permute-start.65) | collective-permute-done | bytes 147488 | tf_op jit(solution)/shard_map/ppermute | solution.py:784
  434.7 4.9 fusion.1
  439.7 2.7 fusion.3
  442.3 15.9 %collective-permute-done.71 = bf16[384,384]{1,0:T(8,128)(2,1)S(1)} collective-permute-done((bf16[384,384]{1,0:T(8,128)(2,1)S(1)}, bf16[384,384]{1,0:T(8,128)(2,1)S(1)}, u32[]{:S(2)}, u32[]{:S(2)}) %collective-permute-start.71) | collective-permute-done | bytes 294944 | tf_op jit(solution)/shard_map/ppermute | solution.py:784
  458.2 17.7 %collective-permute-done.72 = bf16[384,384]{1,0:T(8,128)(2,1)S(1)} collective-permute-done((bf16[384,384]{1,0:T(8,128)(2,1)S(1)}, bf16[384,384]{1,0:T(8,128)(2,1)S(1)}, u32[]{:S(2)}, u32[]{:S(2)}) %collective-permute-start.72) | collective-permute-done | bytes 294944 | tf_op jit(solution)/shard_map/ppermute | solution.py:784
  477.7 4.6 concatenate.155
  488.1 2.1 collective-permute-start.77
  492.6 2.6 collective-permute-start.76
  495.2 4.6 collective-permute-done.84
  499.9 4.8 pad_maximum_fusion
  505.4 2.3 collective-permute-start.86
  515.5 7.3 %collective-permute-done.78 = bf16[192,384]{1,0:T(8,128)(2,1)S(1)} collective-permute-done((bf16[192,384]{1,0:T(8,128)(2,1)S(1)}, bf16[192,384]{1,0:T(8,128)(2,1)S(1)}, u32[]{:S(2)}, u32[]{:S(2)}) %collective-permute-start.78) | collective-permute-done | bytes 147488 | tf_op jit(solution)/shard_map/ppermute | solution.py:784
  524.2 6.2 %bitcast_add_fusion = f32[192,2048]{1,0:T(8,128)} fusion(f32[4,192,2048]{2,1,0:T(8,128)} %param.18, bf16[192,1024]{1,0:T(8,128)(2,1)} %collective-permute-done.77, bf16[192,1024]{1,0:T(8,128)(2,1)S(1)} %copy-done.132, f32[]{:T(128)} %bitcast.38, f32[]{:T(128)} %bitcast.37, f32[]{:T(128)} %bitcast, pred[]{:T(512)S(6)} %eq.28), kind=kLoop, calls=%fused_computation.35 | loop fusion | flops 6291456 | bytes 7077901 | tf_op jit(solution)/shard_map/add | solution.py:1246
  542.4 2.9 collective-permute-done.81.refs_2_
  (591 shorter events, 171.6 us)
Async XLA Ops:
  7.2 523.2 %all-reduce.3.cloned.1.call-start = ((), (), s32[]{:S(2)}) async-start(), calls=%async_computation | async-start | bytes 7077888 | tf_op jit(solution)/shard_map/psum | solution.py:1141
  14.8 19.0 %collective-permute-start.2 = (bf16[768,384]{1,0:T(8,128)(2,1)S(1)}, bf16[768,384]{1,0:T(8,128)(2,1)}, u32[]{:S(2)}, u32[]{:S(2)}) collective-permute-start(bf16[768,384]{1,0:T(8,128)(2,1)S(1)} %get-tuple-element.453.refs_2_.refs_3_), channel_id=1, source_target_pairs={{0,2},{1,3},{2,0},{3,1},{4,6},{5,7},{6,4},{7,5},{8,10},{9,11},{10,... | collective-permute-start | bytes 1769480 | tf_op jit(solution)/shard_map/ppermute | solution.py:779
  22.8 30.2 %collective-permute-start.1 = (bf16[2,192,1024]{2,1,0:T(8,128)(2,1)}, bf16[2,192,1024]{2,1,0:T(8,128)(2,1)}, u32[]{:S(2)}, u32[]{:S(2)}) collective-permute-start(bf16[2,192,1024]{2,1,0:T(8,128)(2,1)} %maximum_select_fusion.3), channel_id=1, source_target_pairs={{0,1},{1,0},{2,3},{3,2},{4,5},{5,4},{6,7},{7,6},{8,9},{9,8},{10,11... | collective-permute-start | bytes 2359304 | tf_op jit(solution)/shard_map/ppermute | solution.py:774
  36.3 31.3 %collective-permute-start.5 = (bf16[768,384]{1,0:T(8,128)(2,1)}, bf16[768,384]{1,0:T(8,128)(2,1)}, u32[]{:S(2)}, u32[]{:S(2)}) collective-permute-start(bf16[768,384]{1,0:T(8,128)(2,1)} %collective-permute-done.2.refs_4_.refs_14_), channel_id=1, source_target_pairs={{0,4},{4,0},{8,12},{12,8},{16,20},{20,16},{24,28},{28,24},{1,5},{5... | collective-permute-start | bytes 1769480 | tf_op jit(solution)/shard_map/ppermute | solution.py:784
  39.7 27.4 %collective-permute-start.6 = (bf16[384,768]{1,0:T(8,128)(2,1)S(1)}, bf16[384,768]{1,0:T(8,128)(2,1)}, u32[]{:S(2)}, u32[]{:S(2)}) collective-permute-start(bf16[384,768]{1,0:T(8,128)(2,1)S(1)} %get-tuple-element.451.refs_10_.refs_7_), channel_id=1, source_target_pairs={{0,2},{1,3},{2,0},{3,1},{4,6},{5,7},{6,4},{7,5},{8,10},{9,11},{10,... | collective-permute-start | bytes 1769480 | tf_op jit(solution)/shard_map/ppermute | solution.py:779
  42.3 48.4 %collective-permute-start.8 = (bf16[768,384]{1,0:T(8,128)(2,1)S(1)}, bf16[768,384]{1,0:T(8,128)(2,1)}, u32[]{:S(2)}, u32[]{:S(2)}) collective-permute-start(bf16[768,384]{1,0:T(8,128)(2,1)S(1)} %get-tuple-element.449.refs_0_.refs_5_), channel_id=1, source_target_pairs={{0,2},{1,3},{2,0},{3,1},{4,6},{5,7},{6,4},{7,5},{8,10},{9,11},{10,... | collective-permute-start | bytes 1769480 | tf_op jit(solution)/shard_map/ppermute | solution.py:779
  62.1 29.2 %collective-permute-start.9 = (bf16[192,1024]{1,0:T(8,128)(2,1)S(1)}, bf16[192,1024]{1,0:T(8,128)(2,1)S(1)}, u32[]{:S(2)}, u32[]{:S(2)}) collective-permute-start(bf16[192,1024]{1,0:T(8,128)(2,1)S(1)} %get-tuple-element.465), channel_id=1, source_target_pairs={{0,2},{1,3},{2,0},{3,1},{4,6},{5,7},{6,4},{7,5},{8,10},{9,11},{10,... | collective-permute-start | bytes 1179656 | tf_op jit(solution)/shard_map/ppermute | solution.py:779
  65.6 42.3 %collective-permute-start.15 = (bf16[768,384]{1,0:T(8,128)(2,1)S(1)}, bf16[768,384]{1,0:T(8,128)(2,1)S(1)}, u32[]{:S(2)}, u32[]{:S(2)}) collective-permute-start(bf16[768,384]{1,0:T(8,128)(2,1)S(1)} %get-tuple-element.447.refs_13_.refs_3_), channel_id=1, source_target_pairs={{0,2},{1,3},{2,0},{3,1},{4,6},{5,7},{6,4},{7,5},{8,10},{9,11},{10,... | collective-permute-start | bytes 1769480 | tf_op jit(solution)/shard_map/ppermute | solution.py:779
  67.2 24.2 %collective-permute-start.7 = (bf16[384,768]{1,0:T(8,128)(2,1)}, bf16[384,768]{1,0:T(8,128)(2,1)S(1)}, u32[]{:S(2)}, u32[]{:S(2)}) collective-permute-start(bf16[384,768]{1,0:T(8,128)(2,1)} %collective-permute-done.6.refs_12_.refs_21_), channel_id=1, source_target_pairs={{0,4},{4,0},{8,12},{12,8},{16,20},{20,16},{24,28},{28,24},{1,5},{5... | collective-permute-start | bytes 1769480 | tf_op jit(solution)/shard_map/ppermute | solution.py:784
  92.3 24.5 %collective-permute-start.19 = (bf16[384,768]{1,0:T(8,128)(2,1)S(1)}, bf16[384,768]{1,0:T(8,128)(2,1)S(1)}, u32[]{:S(2)}, u32[]{:S(2)}) collective-permute-start(bf16[384,768]{1,0:T(8,128)(2,1)S(1)} %get-tuple-element.445.refs_10_.refs_7_), channel_id=1, source_target_pairs={{0,2},{1,3},{2,0},{3,1},{4,6},{5,7},{6,4},{7,5},{8,10},{9,11},{10,... | collective-permute-start | bytes 1769480 | tf_op jit(solution)/shard_map/ppermute | solution.py:779
  92.9 24.0 %collective-permute-start.10 = (bf16[2,192,1024]{2,1,0:T(8,128)(2,1)S(1)}, bf16[2,192,1024]{2,1,0:T(8,128)(2,1)S(1)}, u32[]{:S(2)}, u32[]{:S(2)}) collective-permute-start(bf16[2,192,1024]{2,1,0:T(8,128)(2,1)S(1)} %maximum_select_fusion.4), channel_id=1, source_target_pairs={{0,1},{1,0},{2,3},{3,2},{4,5},{5,4},{6,7},{7,6},{8,9},{9,8},{10,11... | collective-permute-start | bytes 2359304 | tf_op jit(solution)/shard_map/ppermute | solution.py:774
  93.5 15.6 %collective-permute-start.16 = (bf16[768,384]{1,0:T(8,128)(2,1)}, bf16[768,384]{1,0:T(8,128)(2,1)S(1)}, u32[]{:S(2)}, u32[]{:S(2)}) collective-permute-start(bf16[768,384]{1,0:T(8,128)(2,1)} %collective-permute-done.8.refs_2_.refs_19_), channel_id=1, source_target_pairs={{0,4},{4,0},{8,12},{12,8},{16,20},{20,16},{24,28},{28,24},{1,5},{5... | collective-permute-start | bytes 1769480 | tf_op jit(solution)/shard_map/ppermute | solution.py:784
  109.0 14.5 %collective-permute-start.18 = (bf16[768,384]{1,0:T(8,128)(2,1)S(1)}, bf16[768,384]{1,0:T(8,128)(2,1)S(1)}, u32[]{:S(2)}, u32[]{:S(2)}) collective-permute-start(bf16[768,384]{1,0:T(8,128)(2,1)S(1)} %collective-permute-done.15.refs_15_.refs_14_), channel_id=1, source_target_pairs={{0,4},{4,0},{8,12},{12,8},{16,20},{20,16},{24,28},{28,24},{1,5},{5... | collective-permute-start | bytes 1769480 | tf_op jit(solution)/shard_map/ppermute | solution.py:784
  118.8 30.1 %collective-permute-start.29 = (bf16[768,384]{1,0:T(8,128)(2,1)S(1)}, bf16[768,384]{1,0:T(8,128)(2,1)S(1)}, u32[]{:S(2)}, u32[]{:S(2)}) collective-permute-start(bf16[768,384]{1,0:T(8,128)(2,1)S(1)} %get-tuple-element.442.refs_15_.refs_6_), channel_id=1, source_target_pairs={{0,2},{1,3},{2,0},{3,1},{4,6},{5,7},{6,4},{7,5},{8,10},{9,11},{10,... | collective-permute-start | bytes 1769480 | tf_op jit(solution)/shard_map/ppermute | solution.py:779
  123.6 24.4 %collective-permute-start.24 = (bf16[768,384]{1,0:T(8,128)(2,1)S(1)}, bf16[768,384]{1,0:T(8,128)(2,1)S(1)}, u32[]{:S(2)}, u32[]{:S(2)}) collective-permute-start(bf16[768,384]{1,0:T(8,128)(2,1)S(1)} %get-tuple-element.443.refs_14_.refs_5_), channel_id=1, source_target_pairs={{0,2},{1,3},{2,0},{3,1},{4,6},{5,7},{6,4},{7,5},{8,10},{9,11},{10,... | collective-permute-start | bytes 1769480 | tf_op jit(solution)/shard_map/ppermute | solution.py:779
  125.2 22.9 %collective-permute-start.23 = (bf16[384,768]{1,0:T(8,128)(2,1)S(1)}, bf16[384,768]{1,0:T(8,128)(2,1)S(1)}, u32[]{:S(2)}, u32[]{:S(2)}) collective-permute-start(bf16[384,768]{1,0:T(8,128)(2,1)S(1)} %collective-permute-done.19.refs_12_.refs_19_), channel_id=1, source_target_pairs={{0,4},{4,0},{8,12},{12,8},{16,20},{20,16},{24,28},{28,24},{1,5},{5... | collective-permute-start | bytes 1769480 | tf_op jit(solution)/shard_map/ppermute | solution.py:784
  148.8 16.3 %collective-permute-start.30 = (bf16[192,1024]{1,0:T(8,128)(2,1)S(1)}, bf16[192,1024]{1,0:T(8,128)(2,1)S(1)}, u32[]{:S(2)}, u32[]{:S(2)}) collective-permute-start(bf16[192,1024]{1,0:T(8,128)(2,1)S(1)} %get-tuple-element.459), channel_id=1, source_target_pairs={{0,2},{1,3},{2,0},{3,1},{4,6},{5,7},{6,4},{7,5},{8,10},{9,11},{10,... | collective-permute-start | bytes 1179656 | tf_op jit(solution)/shard_map/ppermute | solution.py:779
  194.9 29.1 %collective-permute-start.37 = (bf16[768,768]{1,0:T(8,128)(2,1)}, bf16[768,768]{1,0:T(8,128)(2,1)}, u32[]{:S(2)}, u32[]{:S(2)}) collective-permute-start(bf16[768,768]{1,0:T(8,128)(2,1)} %get-tuple-element.265), channel_id=1, source_target_pairs={{0,2},{1,3},{2,0},{3,1},{4,6},{5,7},{6,4},{7,5},{8,10},{9,11},{10,... | collective-permute-start | bytes 3538952 | tf_op jit(solution)/shard_map/ppermute | solution.py:779
  207.6 16.4 %collective-permute-start.38 = (bf16[192,1024]{1,0:T(8,128)(2,1)}, bf16[192,1024]{1,0:T(8,128)(2,1)}, u32[]{:S(2)}, u32[]{:S(2)}) collective-permute-start(bf16[192,1024]{1,0:T(8,128)(2,1)} %get-tuple-element.262.refs_3_), channel_id=1, source_target_pairs={{0,1},{1,0},{2,3},{3,2},{4,5},{5,4},{6,7},{7,6},{8,9},{9,8},{10,11... | collective-permute-start | bytes 1179656 | tf_op jit(solution)/shard_map/ppermute | solution.py:774
  208.0 15.9 %collective-permute-start.39 = (bf16[192,1024]{1,0:T(8,128)(2,1)}, bf16[192,1024]{1,0:T(8,128)(2,1)}, u32[]{:S(2)}, u32[]{:S(2)}) collective-permute-start(bf16[192,1024]{1,0:T(8,128)(2,1)} %get-tuple-element.263.refs_4_), channel_id=1, source_target_pairs={{0,1},{1,0},{2,3},{3,2},{4,5},{5,4},{6,7},{7,6},{8,9},{9,8},{10,11... | collective-permute-start | bytes 1179656 | tf_op jit(solution)/shard_map/ppermute | solution.py:774
  208.1 15.9 %collective-permute-start.40 = (bf16[192,1024]{1,0:T(8,128)(2,1)}, bf16[192,1024]{1,0:T(8,128)(2,1)}, u32[]{:S(2)}, u32[]{:S(2)}) collective-permute-start(bf16[192,1024]{1,0:T(8,128)(2,1)} %get-tuple-element.264.refs_5_), channel_id=1, source_target_pairs={{0,1},{1,0},{2,3},{3,2},{4,5},{5,4},{6,7},{7,6},{8,9},{9,8},{10,11... | collective-permute-start | bytes 1179656 | tf_op jit(solution)/shard_map/ppermute | solution.py:774
  215.4 35.4 %collective-permute-start.41 = (bf16[768,768]{1,0:T(8,128)(2,1)}, bf16[768,768]{1,0:T(8,128)(2,1)S(1)}, u32[]{:S(2)}, u32[]{:S(2)}) collective-permute-start(bf16[768,768]{1,0:T(8,128)(2,1)} %copy-done.39), channel_id=1, source_target_pairs={{0,2},{1,3},{2,0},{3,1},{4,6},{5,7},{6,4},{7,5},{8,10},{9,11},{10,... | collective-permute-start | bytes 3538952 | tf_op jit(solution)/shard_map/ppermute | solution.py:779
  250.3 26.4 %collective-permute-start.43 = (bf16[768,768]{1,0:T(8,128)(2,1)S(1)}, bf16[768,768]{1,0:T(8,128)(2,1)S(1)}, u32[]{:S(2)}, u32[]{:S(2)}) collective-permute-start(bf16[768,768]{1,0:T(8,128)(2,1)S(1)} %get-tuple-element.283), channel_id=1, source_target_pairs={{0,2},{1,3},{2,0},{3,1},{4,6},{5,7},{6,4},{7,5},{8,10},{9,11},{10,... | collective-permute-start | bytes 3538952 | tf_op jit(solution)/shard_map/ppermute | solution.py:779
  304.4 19.7 %collective-permute-start.47 = (bf16[768,384]{1,0:T(8,128)(2,1)}, bf16[768,384]{1,0:T(8,128)(2,1)S(1)}, u32[]{:S(2)}, u32[]{:S(2)}) collective-permute-start(bf16[768,384]{1,0:T(8,128)(2,1)} %get-tuple-element.297), channel_id=1, source_target_pairs={{0,2},{1,3},{2,0},{3,1},{4,6},{5,7},{6,4},{7,5},{8,10},{9,11},{10,... | collective-permute-start | bytes 1769480 | tf_op jit(solution)/shard_map/ppermute | solution.py:779
  304.8 25.4 %collective-permute-start.49 = (bf16[768,384]{1,0:T(8,128)(2,1)}, bf16[768,384]{1,0:T(8,128)(2,1)}, u32[]{:S(2)}, u32[]{:S(2)}) collective-permute-start(bf16[768,384]{1,0:T(8,128)(2,1)} %get-tuple-element.303), channel_id=1, source_target_pairs={{0,2},{1,3},{2,0},{3,1},{4,6},{5,7},{6,4},{7,5},{8,10},{9,11},{10,... | collective-permute-start | bytes 1769480 | tf_op jit(solution)/shard_map/ppermute | solution.py:779
  330.2 26.2 %collective-permute-start.54 = (bf16[768,384]{1,0:T(8,128)(2,1)S(1)}, bf16[768,384]{1,0:T(8,128)(2,1)S(1)}, u32[]{:S(2)}, u32[]{:S(2)}) collective-permute-start(bf16[768,384]{1,0:T(8,128)(2,1)S(1)} %copy-done.59), channel_id=1, source_target_pairs={{0,2},{1,3},{2,0},{3,1},{4,6},{5,7},{6,4},{7,5},{8,10},{9,11},{10,... | collective-permute-start | bytes 1769480 | tf_op jit(solution)/shard_map/ppermute | solution.py:779
  330.6 28.5 %collective-permute-start.55 = (bf16[768,384]{1,0:T(8,128)(2,1)S(1)}, bf16[768,384]{1,0:T(8,128)(2,1)S(1)}, u32[]{:S(2)}, u32[]{:S(2)}) collective-permute-start(bf16[768,384]{1,0:T(8,128)(2,1)S(1)} %copy-done.57), channel_id=1, source_target_pairs={{0,2},{1,3},{2,0},{3,1},{4,6},{5,7},{6,4},{7,5},{8,10},{9,11},{10,... | collective-permute-start | bytes 1769480 | tf_op jit(solution)/shard_map/ppermute | solution.py:779
  335.9 45.3 %collective-permute-start.63 = (bf16[192,1024]{1,0:T(8,128)(2,1)S(1)}, bf16[192,1024]{1,0:T(8,128)(2,1)S(1)}, u32[]{:S(2)}, u32[]{:S(2)}) collective-permute-start(bf16[192,1024]{1,0:T(8,128)(2,1)S(1)} %get-tuple-element.439), channel_id=1, source_target_pairs={{0,2},{1,3},{2,0},{3,1},{4,6},{5,7},{6,4},{7,5},{8,10},{9,11},{10,... | collective-permute-start | bytes 1179656 | tf_op jit(solution)/shard_map/ppermute | solution.py:779
  336.6 22.5 %collective-permute-start.53 = (bf16[768,384]{1,0:T(8,128)(2,1)S(1)}, bf16[768,384]{1,0:T(8,128)(2,1)S(1)}, u32[]{:S(2)}, u32[]{:S(2)}) collective-permute-start(bf16[768,384]{1,0:T(8,128)(2,1)S(1)} %get-tuple-element.317), channel_id=1, source_target_pairs={{0,4},{4,0},{8,12},{12,8},{16,20},{20,16},{24,28},{28,24},{1,5},{5... | collective-permute-start | bytes 1769480 | tf_op jit(solution)/shard_map/ppermute | solution.py:784
  354.8 26.4 %collective-permute-start.59 = (bf16[768,384]{1,0:T(8,128)(2,1)S(1)}, bf16[768,384]{1,0:T(8,128)(2,1)S(1)}, u32[]{:S(2)}, u32[]{:S(2)}) collective-permute-start(bf16[768,384]{1,0:T(8,128)(2,1)S(1)} %get-tuple-element.333), channel_id=1, source_target_pairs={{0,2},{1,3},{2,0},{3,1},{4,6},{5,7},{6,4},{7,5},{8,10},{9,11},{10,... | collective-permute-start | bytes 1769480 | tf_op jit(solution)/shard_map/ppermute | solution.py:779
  356.4 34.4 %collective-permute-start.60 = (bf16[768,384]{1,0:T(8,128)(2,1)S(1)}, bf16[768,384]{1,0:T(8,128)(2,1)S(1)}, u32[]{:S(2)}, u32[]{:S(2)}) collective-permute-start(bf16[768,384]{1,0:T(8,128)(2,1)S(1)} %get-tuple-element.334), channel_id=1, source_target_pairs={{0,2},{1,3},{2,0},{3,1},{4,6},{5,7},{6,4},{7,5},{8,10},{9,11},{10,... | collective-permute-start | bytes 1769480 | tf_op jit(solution)/shard_map/ppermute | solution.py:779
  359.3 19.1 %collective-permute-start.56 = (bf16[384,384]{1,0:T(8,128)(2,1)S(1)}, bf16[384,384]{1,0:T(8,128)(2,1)S(1)}, u32[]{:S(2)}, u32[]{:S(2)}) collective-permute-start(bf16[384,384]{1,0:T(8,128)(2,1)S(1)} %constant_dynamic-slice_fusion.15), channel_id=1, source_target_pairs={{0,8},{4,12},{8,0},{12,4},{16,24},{20,28},{24,16},{28,20},{1,9},{5... | collective-permute-start | bytes 884744 | tf_op jit(solution)/shard_map/ppermute | solution.py:784
  361.3 17.1 %collective-permute-start.57 = (bf16[768,384]{1,0:T(8,128)(2,1)S(1)}, bf16[768,384]{1,0:T(8,128)(2,1)S(1)}, u32[]{:S(2)}, u32[]{:S(2)}) collective-permute-start(bf16[768,384]{1,0:T(8,128)(2,1)S(1)} %get-tuple-element.331), channel_id=1, source_target_pairs={{0,4},{4,0},{8,12},{12,8},{16,20},{20,16},{24,28},{28,24},{1,5},{5... | collective-permute-start | bytes 1769480 | tf_op jit(solution)/shard_map/ppermute | solution.py:784
  379.2 21.0 %collective-permute-start.62 = (bf16[384,384]{1,0:T(8,128)(2,1)S(1)}, bf16[384,384]{1,0:T(8,128)(2,1)S(1)}, u32[]{:S(2)}, u32[]{:S(2)}) collective-permute-start(bf16[384,384]{1,0:T(8,128)(2,1)S(1)} %constant_dynamic-slice_fusion.13), channel_id=1, source_target_pairs={{0,8},{4,12},{8,0},{12,4},{16,24},{20,28},{24,16},{28,20},{1,9},{5... | collective-permute-start | bytes 884744 | tf_op jit(solution)/shard_map/ppermute | solution.py:784
  381.2 19.0 %collective-permute-start.58 = (bf16[192,1024]{1,0:T(8,128)(2,1)S(1)}, bf16[192,1024]{1,0:T(8,128)(2,1)S(1)}, u32[]{:S(2)}, u32[]{:S(2)}) collective-permute-start(bf16[192,1024]{1,0:T(8,128)(2,1)S(1)} %get-tuple-element.332.refs_3_), channel_id=1, source_target_pairs={{0,1},{1,0},{2,3},{3,2},{4,5},{5,4},{6,7},{7,6},{8,9},{9,8},{10,11... | collective-permute-start | bytes 1179656 | tf_op jit(solution)/shard_map/ppermute | solution.py:774
  381.2 19.8 %collective-permute-start.67 = (bf16[192,1024]{1,0:T(8,128)(2,1)S(1)}, bf16[192,1024]{1,0:T(8,128)(2,1)S(1)}, u32[]{:S(2)}, u32[]{:S(2)}) collective-permute-start(bf16[192,1024]{1,0:T(8,128)(2,1)S(1)} %get-tuple-element.346.refs_4_), channel_id=1, source_target_pairs={{0,1},{1,0},{2,3},{3,2},{4,5},{5,4},{6,7},{7,6},{8,9},{9,8},{10,11... | collective-permute-start | bytes 1179656 | tf_op jit(solution)/shard_map/ppermute | solution.py:774
  407.4 17.6 %collective-permute-start.66 = (bf16[192,384]{1,0:T(8,128)(2,1)S(1)}, bf16[192,384]{1,0:T(8,128)(2,1)S(1)}, u32[]{:S(2)}, u32[]{:S(2)}) collective-permute-start(bf16[192,384]{1,0:T(8,128)(2,1)S(1)} %constant_dynamic-slice_fusion.11), channel_id=1, source_target_pairs={{0,16},{4,20},{8,24},{12,28},{16,0},{20,4},{24,8},{28,12},{1,17},{... | collective-permute-start | bytes 442376 | tf_op jit(solution)/shard_map/ppermute | solution.py:784
  408.9 22.9 %collective-permute-start.64 = (bf16[768,384]{1,0:T(8,128)(2,1)S(1)}, bf16[768,384]{1,0:T(8,128)(2,1)S(1)}, u32[]{:S(2)}, u32[]{:S(2)}) collective-permute-start(bf16[768,384]{1,0:T(8,128)(2,1)S(1)} %get-tuple-element.342), channel_id=1, source_target_pairs={{0,4},{4,0},{8,12},{12,8},{16,20},{20,16},{24,28},{28,24},{1,5},{5... | collective-permute-start | bytes 1769480 | tf_op jit(solution)/shard_map/ppermute | solution.py:784
  411.2 20.6 %collective-permute-start.70 = (bf16[192,1024]{1,0:T(8,128)(2,1)S(1)}, bf16[192,1024]{1,0:T(8,128)(2,1)S(1)}, u32[]{:S(2)}, u32[]{:S(2)}) collective-permute-start(bf16[192,1024]{1,0:T(8,128)(2,1)S(1)} %get-tuple-element.441), channel_id=1, source_target_pairs={{0,2},{1,3},{2,0},{3,1},{4,6},{5,7},{6,4},{7,5},{8,10},{9,11},{10,... | collective-permute-start | bytes 1179656 | tf_op jit(solution)/shard_map/ppermute | solution.py:779
  412.7 19.0 %collective-permute-start.65 = (bf16[192,384]{1,0:T(8,128)(2,1)S(1)}, bf16[192,384]{1,0:T(8,128)(2,1)S(1)}, u32[]{:S(2)}, u32[]{:S(2)}) collective-permute-start(bf16[192,384]{1,0:T(8,128)(2,1)S(1)} %add_convert_fusion.8), channel_id=1, source_target_pairs={{0,16},{4,20},{8,24},{12,28},{16,0},{20,4},{24,8},{28,12},{1,17},{... | collective-permute-start | bytes 442376 | tf_op jit(solution)/shard_map/ppermute | solution.py:784
  432.5 25.7 %collective-permute-start.71 = (bf16[384,384]{1,0:T(8,128)(2,1)S(1)}, bf16[384,384]{1,0:T(8,128)(2,1)S(1)}, u32[]{:S(2)}, u32[]{:S(2)}) collective-permute-start(bf16[384,384]{1,0:T(8,128)(2,1)S(1)} %constant_dynamic-slice_fusion.9), channel_id=1, source_target_pairs={{0,8},{4,12},{8,0},{12,4},{16,24},{20,28},{24,16},{28,20},{1,9},{5... | collective-permute-start | bytes 884744 | tf_op jit(solution)/shard_map/ppermute | solution.py:784
  434.2 41.6 %collective-permute-start.72 = (bf16[384,384]{1,0:T(8,128)(2,1)S(1)}, bf16[384,384]{1,0:T(8,128)(2,1)S(1)}, u32[]{:S(2)}, u32[]{:S(2)}) collective-permute-start(bf16[384,384]{1,0:T(8,128)(2,1)S(1)} %maximum_select_fusion.13), channel_id=1, source_target_pairs={{0,8},{4,12},{8,0},{12,4},{16,24},{20,28},{24,16},{28,20},{1,9},{5... | collective-permute-start | bytes 884744 | tf_op jit(solution)/shard_map/ppermute | solution.py:784
  483.6 24.1 %collective-permute-start.75 = (bf16[768,384]{1,0:T(8,128)(2,1)S(1)}, bf16[768,384]{1,0:T(8,128)(2,1)S(1)}, u32[]{:S(2)}, u32[]{:S(2)}) collective-permute-start(bf16[768,384]{1,0:T(8,128)(2,1)S(1)} %maximum_select_fusion.10.refs_1_), channel_id=1, source_target_pairs={{0,4},{4,0},{8,12},{12,8},{16,20},{20,16},{24,28},{28,24},{1,5},{5... | collective-permute-start | bytes 1769480 | tf_op jit(solution)/shard_map/ppermute | solution.py:784
  488.1 19.6 %collective-permute-start.77 = (bf16[192,1024]{1,0:T(8,128)(2,1)}, bf16[192,1024]{1,0:T(8,128)(2,1)}, u32[]{:S(2)}, u32[]{:S(2)}) collective-permute-start(bf16[192,1024]{1,0:T(8,128)(2,1)} %add_convert_fusion.1), channel_id=1, source_target_pairs={{0,2},{1,3},{2,0},{3,1},{4,6},{5,7},{6,4},{7,5},{8,10},{9,11},{10,... | collective-permute-start | bytes 1179656 | tf_op jit(solution)/shard_map/ppermute | solution.py:779
  492.6 15.1 %collective-permute-start.74 = (bf16[192,384]{1,0:T(8,128)(2,1)S(1)}, bf16[192,384]{1,0:T(8,128)(2,1)S(1)}, u32[]{:S(2)}, u32[]{:S(2)}) collective-permute-start(bf16[192,384]{1,0:T(8,128)(2,1)S(1)} %constant_dynamic-slice_fusion.4), channel_id=1, source_target_pairs={{0,16},{4,20},{8,24},{12,28},{16,0},{20,4},{24,8},{28,12},{1,17},{... | collective-permute-start | bytes 442376 | tf_op jit(solution)/shard_map/ppermute | solution.py:784
  492.6 15.1 %collective-permute-start.76 = (bf16[384,384]{1,0:T(8,128)(2,1)S(1)}, bf16[384,384]{1,0:T(8,128)(2,1)S(1)}, u32[]{:S(2)}, u32[]{:S(2)}) collective-permute-start(bf16[384,384]{1,0:T(8,128)(2,1)S(1)} %maximum_select_fusion.14), channel_id=1, source_target_pairs={{0,8},{4,12},{8,0},{12,4},{16,24},{20,28},{24,16},{28,20},{1,9},{5... | collective-permute-start | bytes 884744 | tf_op jit(solution)/shard_map/ppermute | solution.py:784
  509.0 14.8 %collective-permute-start.79 = (bf16[768,384]{1,0:T(8,128)(2,1)S(1)}, bf16[768,384]{1,0:T(8,128)(2,1)S(1)}, u32[]{:S(2)}, u32[]{:S(2)}) collective-permute-start(bf16[768,384]{1,0:T(8,128)(2,1)S(1)} %maximum_select_fusion.11.refs_1_), channel_id=1, source_target_pairs={{0,4},{4,0},{8,12},{12,8},{16,20},{20,16},{24,28},{28,24},{1,5},{5... | collective-permute-start | bytes 1769480 | tf_op jit(solution)/shard_map/ppermute | solution.py:784
  532.0 13.3 %collective-permute-start.81 = (bf16[768,384]{1,0:T(8,128)(2,1)S(1)}, bf16[768,384]{1,0:T(8,128)(2,1)S(1)}, u32[]{:S(2)}, u32[]{:S(2)}) collective-permute-start(bf16[768,384]{1,0:T(8,128)(2,1)S(1)} %maximum_select_fusion.12.refs_1_), channel_id=1, source_target_pairs={{0,4},{4,0},{8,12},{12,8},{16,20},{20,16},{24,28},{28,24},{1,5},{5... | collective-permute-start | bytes 1769480 | tf_op jit(solution)/shard_map/ppermute | solution.py:784
  (194 other events, 2225.7 us)
Sparse Core Ops, SparseCore 0:
  326.2 157.9 all-reduce.2

commit v3 on v2

--- a/solution.py
+++ b/solution.py
@@ -21,7 +21,10 @@
 F32 = jnp.float32
 GELU_A = 0.7978845608028654
 GELU_B = 0.044715
-GAIN1, SHIFT1, GAIN2, SHIFT2, MERGE_B, REDUCE_B, INPUT_B, EXPAND_B = 0, 1, 2, 3, 4, 5, 6, 8
+INPUT_ROWS, EXPAND_ROWS = (0, 3), (3, 7)
+GAIN1, SHIFT1, GAIN2, SHIFT2, MERGE_B, REDUCE_B = 7, 8, 9, 10, 11, 12
+TABLE_ROWS, TABLE_LANES = 16, 256
+BIT, ROW, FLIP, CORE = 0, 1, 2, 3
 
 
 def dot(a, b, on):
@@ -48,14 +51,69 @@
     return jax.ShapeDtypeStruct(dims, kind)
 
 
+LATE, EARLY = "late", "early"
+
+
 def launch(kernel, name, steps, ins, outs, scratch, micros, vmem, aliases=None):
+    if steps == 1:
+        ins = [(item, full(item.shape) if spec is LATE else spec) for item, spec in ins]
+        outs = [(item, full(item.shape) if spec is EARLY else spec) for item, spec in outs]
+    late = [i for i, (_, spec) in enumerate(ins) if spec is LATE]
+    early = [i for i, (_, spec) in enumerate(outs) if spec is EARLY]
+    anywhere = pl.BlockSpec(memory_space=pl.ANY)
+    held = [pltpu.VMEM(ins[i][0].shape, ins[i][0].dtype) for i in late]
+    held += [pltpu.VMEM(outs[i][0].shape, outs[i][0].dtype) for i in early]
+    moves = len(held)
+
+    def body(*refs):
+        if not moves:
+            kernel(*refs)
+            return
+        refs = list(refs)
+        extra = refs[len(ins) + len(outs) + len(scratch) :]
+        del refs[len(ins) + len(outs) + len(scratch) :]
+        buffers, sems = extra[:moves], extra[moves]
+        incoming, outgoing = [], []
+        for slot, index in enumerate(late):
+            incoming.append(pltpu.make_async_copy(refs[index], buffers[slot], sems.at[slot]))
+            refs[index] = buffers[slot]
+        for slot, index in enumerate(early, len(late)):
+            index = len(ins) + index
+            outgoing.append(pltpu.make_async_copy(buffers[slot], refs[index], sems.at[slot]))
+            refs[index] = buffers[slot]
+        step = pl.program_id(0)
+
+        @pl.when(step == 0)
+        def _():
+            for move in incoming:
+                move.start()
+
+        @pl.when(step == steps - 1)
+        def _():
+            for move in incoming:
+                move.wait()
+
+        kernel(*refs)
+
+        @pl.when(step == 0)
+        def _():
+            for move in outgoing:
+                move.start()
+
+        @pl.when(step == steps - 1)
+        def _():
+            for move in outgoing:
+                move.wait()
+
+    if moves:
+        held.append(pltpu.SemaphoreType.DMA((moves,)))
     return pl.pallas_call(
-        kernel,
+        body,
         grid=(steps,),
-        in_specs=[spec for _, spec in ins],
-        out_specs=[spec for _, spec in outs],
+        in_specs=[anywhere if spec is LATE else spec for _, spec in ins],
+        out_specs=[anywhere if spec is EARLY else spec for _, spec in outs],
         out_shape=[struct for struct, _ in outs],
-        scratch_shapes=scratch,
+        scratch_shapes=list(scratch) + held,
         compiler_params=pltpu.CompilerParams(
             dimension_semantics=("arbitrary",), vmem_limit_bytes=vmem * 1024 * 1024
         ),
@@ -67,6 +125,14 @@
     )(*[operand for operand, _ in ins])
 
 
+def late(*operands):
+    return [(operand, LATE) for operand in operands]
+
+
+def out_early(dims, kind=BF):
+    return (shape(dims, kind), EARLY)
+
+
 def whole(*operands):
     return [(operand, full(operand.shape)) for operand in operands]
 
@@ -96,6 +162,38 @@
 
 def out_pieces(width, length):
     return [out_full((width // 4, length)) for _ in range(4)]
+
+
+def choose(place, index, four, read):
+    mine, theirs, core_mine, core_theirs = four
+    here, side = divmod(index, 2)
+    own = jnp.where(place[0, FLIP] == here, read(mine), read(theirs))
+    other = jnp.where(place[0, FLIP] == here, read(core_mine), read(core_theirs))
+    return jnp.where(place[0, CORE] == side, own, other)
+
+
+class RowParts:
+    def __init__(self, place, refs):
+        self.place = place
+        self.refs = refs
+        self.size = refs[0].shape[0]
+
+    def __getitem__(self, index):
+        rows = index[0]
+        at = rows.start // self.size
+        cut = slice(rows.start - at * self.size, rows.stop - at * self.size)
+        return choose(self.place, at, self.refs, lambda ref: ref[cut, :].astype(F32))
+
+
+def columns_of(place, four, layer, part):
+    return jnp.concatenate(
+        [choose(place, q, four, lambda ref: ref[layer]).T[:part] for q in range(4)], 0
+    )
+
+
+def stacked_rows(ref, layer, rows, part):
+    table = ref[layer].T[:part]
+    return jnp.concatenate([table[:, row : row + 1] for row in range(*rows)], 0)
 
 
 def strips(size):
@@ -167,19 +265,20 @@
     return nt(jnp.ones((8, value.shape[1]), BF), value)
 
 
-def attention_forward_kernel(mixing, heads, length, width, *refs):
+def attention_forward_kernel(mixing, layer, heads, length, width, *refs):
     refs = list(refs)
+    place = refs.pop(0)
     if mixing:
-        coef, history_i, mid_i = refs[:3]
-        left, right, before = Pieces(refs[3:7]), Pieces(refs[7:11]), refs[11]
-        del refs[:12]
-    else:
-        x_i = refs.pop(0)
-    vectors, a0d, a0r, a1d, a1r, cos, sin, segments = refs[:8]
-    del refs[:8]
+        coef, mid_i = refs[:2]
+        left, right = Pieces(refs[2:6]), Pieces(refs[6:10])
+        del refs[:10]
+    incoming = RowParts(place, refs[:4])
+    vectors = refs[4:8]
+    a0d, a0r, a1d, a1r, cos, sin, segments = refs[8:15]
+    del refs[:15]
     if mixing:
-        y_o, x_o = refs[:2]
-        del refs[:2]
+        y_o = refs.pop(0)
+    x_o = refs.pop(0)
     n1_o, st_o, q_o, k_o, v_o, o_o, lse_o = refs[:7]
     part_o = Pieces(refs[7:11])
     lin, mask, o_all = refs[11:]
@@ -189,9 +288,9 @@
 
     @pl.when(head == 0)
     def _():
-        columns = vectors[...].T
+        columns = columns_of(place, vectors, layer, width // 4)
         if mixing:
-            bias = before[...].T
+            bias = columns_of(place, vectors, layer - 1, width // 4)
             weight = coef[0, HISTORY]
             for rows in strips(width):
                 y = (
@@ -201,10 +300,11 @@
                     + bias[rows, REDUCE_B : REDUCE_B + 1]
                 )
                 y_o[rows, :] = y.astype(BF)
-                x_o[rows, :] = (history_i[rows, :].astype(F32) + weight * y).astype(BF)
-            source = x_o
+                x_o[rows, :] = (incoming[rows, :] + weight * y).astype(BF)
         else:
-            source = x_i
+            for rows in strips(width):
+                x_o[rows, :] = incoming[rows, :].astype(BF)
+        source = x_o
         mean, scale = normalise(
             lambda rows: source[rows, :].astype(F32), None, st_o, None, None, None, width, length
         )
@@ -217,7 +317,7 @@
             lin[at : at + 3 * quarter, :] = (
                 nn(d[: 3 * quarter, :], n1_o[:half, :])
                 + nn(r[: 3 * quarter, :], n1_o[half:, :])
-                + columns[: 3 * quarter, INPUT_B + index : INPUT_B + index + 1]
+                + stacked_rows(vectors[index], layer, INPUT_ROWS, width // 4)
             )
         fill_mask(mask, segments, length)
 
@@ -258,23 +358,22 @@
             )
 
 
-def attention_forward(mix, x, vectors, weights, cos, sin, segments):
+def attention_forward(place, mix, incoming, vectors, layer, weights, cos, sin, segments):
     length = segments.shape[1]
     rows, half = weights[0].shape
     width = 2 * half
     quarter = rows // 4
     heads = 2 * quarter // HEAD
+    ins = scalars(place)
+    outs = [out_early((width, length))]
     if mix is not None:
-        ins = scalars(mix[0]) + whole(*mix[1:])
-        outs = [out_full((width, length)), out_full((width, length))]
-    else:
-        ins = whole(x)
-        outs = []
-    ins = ins + whole(vectors, *weights, cos, sin, segments)
+        ins = ins + scalars(mix[0]) + whole(*mix[1:])
+        outs = outs * 2
+    ins = ins + whole(*incoming, *vectors, *weights, cos, sin, segments)
     per_head = lambda size: pl.BlockSpec((1, size, length), lambda h: (h, 0, 0))
     heads_out = (shape((heads, HEAD, length)), per_head(HEAD))
     outs = outs + [
-        out_full((width, length)),
+        out_early((width, length)),
         out_full((8, length), F32),
         heads_out,
         heads_out,
@@ -284,7 +383,9 @@
     ]
     outs = outs + out_pieces(width, length)
     return launch(
-        functools.partial(attention_forward_kernel, mix is not None, heads, length, width),
+        functools.partial(
+            attention_forward_kernel, mix is not None, layer, heads, length, width
+        ),
         "attention_forward",
         heads,
         ins,
@@ -295,7 +396,7 @@
             pltpu.VMEM((2 * quarter, length), BF),
         ],
         20,
-        44,
+        58,
     )
 
 
@@ -314,13 +415,13 @@
     return [at(0), at(1)]
 
 
-def attention_backward_kernel(opening, natural, heads, length, width, *refs):
+def attention_backward_kernel(opening, layer, natural, heads, length, width, *refs):
     refs = list(refs)
     place = refs.pop(0)
     if opening:
-        grad_i, mid, st, vectors = refs[0], refs[9], refs[10], refs[11]
+        grad_i, mid, st, vectors = refs[0], refs[9], refs[10], refs[11:15]
         left, right = Pieces(refs[1:5]), Pieces(refs[5:9])
-        del refs[:12]
+        del refs[:15]
     else:
         gmb = refs.pop(0)
     n1, ad, ar, cos, sin, segments, q_i, k_i, v_i, o_i, lse_i = refs[:11]
@@ -349,7 +450,7 @@
     def _():
         if opening:
             grad_n, grad_gain = refs
-            columns = vectors[...].T
+            columns = columns_of(place, vectors, layer, width // 4)
             norm_back(
                 mid,
                 st,
@@ -413,12 +514,12 @@
         for at, w in ((0, ad), (half, ar)):
             value = tn(w[: 3 * quarter, :], gl_all[...])
             if opening:
-                part_o[at : at + half, :] = value
+                part_o[at : at + half, :] = value.astype(BF)
             else:
-                part_o.store(at, value + add[at : at + half, :])
-
-
-def attention_backward(place, natural, opening, gmb, n1, weights, cos, sin, segments, saved, group, add):
+                part_o.store(at, value + add[at : at + half, :].astype(F32))
+
+
+def attention_backward(place, layer, natural, opening, gmb, n1, weights, cos, sin, segments, saved, group, add):
     length = segments.shape[1]
     rows, half = weights[0].shape
     width = 2 * half
@@ -427,7 +528,7 @@
     q, key, v, o, lse = saved
     if opening is not None:
         ins = scalars(place) + whole(*opening)
-        outs = [out_full((width, length)), out_full((24, width), F32)]
+        outs = [out_early((width, length)), out_full((24, width), F32)]
         scratch = [pltpu.VMEM((width, length), BF), pltpu.VMEM((width, length), BF)]
     else:
         ins = scalars(place) + whole(gmb)
@@ -435,17 +536,17 @@
         scratch = []
     at = group * heads
     per_head = lambda size: pl.BlockSpec((1, size, length), lambda h: (at + h, 0, 0))
-    ins = ins + whole(n1, *weights, cos, sin, segments)
+    ins = ins + late(n1) + whole(*weights, cos, sin, segments)
     ins = ins + [(item, per_head(HEAD)) for item in (q, key, v)]
     ins = ins + [(o, pl.BlockSpec((heads, HEAD, length), lambda h: (group, 0, 0))), (lse, per_head(1))]
     if add is not None:
-        ins = ins + whole(add)
+        ins = ins + late(add)
     outs = outs + ([out_full((rows, width))] if natural else [out_full((rows, half))] * 2)
     outs = outs + [out_full((8, 3 * quarter), F32)]
-    outs = outs + (out_pieces(width, length) if add is not None else [out_full((width, length), F32)])
+    outs = outs + (out_pieces(width, length) if add is not None else [out_full((width, length))])
     return launch(
         functools.partial(
-            attention_backward_kernel, opening is not None, natural, heads, length, width
+            attention_backward_kernel, opening is not None, layer, natural, heads, length, width
         ),
         "attention_backward",
         heads,
@@ -460,15 +561,16 @@
         ]
         + scratch,
         14,
-        44,
-    )
-
-
-def mlp_forward_kernel(merged, tiles, length, width, *refs):
+        58,
+    )
+
+
+def mlp_forward_kernel(merged, layer, tiles, length, width, *refs):
     refs = list(refs)
-    x, left, right, vectors = refs[0], Pieces(refs[1:5]), Pieces(refs[5:9]), refs[9]
-    e0d, e0r, e1d, e1r = refs[10:14]
-    del refs[:14]
+    place = refs.pop(0)
+    x, left, right, vectors = refs[0], Pieces(refs[1:5]), Pieces(refs[5:9]), refs[9:13]
+    e0d, e0r, e1d, e1r = refs[13:17]
+    del refs[:17]
     if merged:
         r0d, r0r, r1d, r1r = refs[:4]
         del refs[:4]
@@ -483,8 +585,11 @@
 
     @pl.when(t == 0)
     def _():
-        columns = vectors[...].T
-        columns_s[:, : columns.shape[1]] = columns
+        columns = columns_of(place, vectors, layer, width // 4)
+        for index in range(2):
+            columns_s[:, index : index + 1] = stacked_rows(
+                vectors[index], layer, EXPAND_ROWS, width // 4
+            )
         for rows in strips(width):
             mid_o[rows, :] = (
                 x[rows, :].astype(F32)
@@ -502,7 +607,7 @@
 
     def expand(group, d, r):
         at = pl.multiple_of((t - group * tiles) * TILE, TILE)
-        bias = columns_s[pl.ds(at, TILE), EXPAND_B + group : EXPAND_B + group + 1]
+        bias = columns_s[pl.ds(at, TILE), group : group + 1]
         u = tn(d[...], n2_o[:half, :]) + tn(r[...], n2_o[half:, :]) + bias
         act = (0.5 * u * (1.0 + jnp.tanh(GELU_A * (u + GELU_B * (u * u * u))))).astype(BF)
         u_o[...] = u.astype(BF)
@@ -526,37 +631,37 @@
                 part_o.store(at, tn(own[...], acts[:units, :]) + tn(other[...], acts[units:, :]))
 
 
-def mlp_forward(x, left, right, vectors, expand, reduce):
+def mlp_forward(place, x, left, right, vectors, layer, expand, reduce):
     width, length = x.shape
     half, units = expand[0].shape
     tiles = units // TILE
     merged = reduce is not None
     first = pl.BlockSpec((half, TILE), lambda t: (0, jnp.minimum(t, tiles - 1)))
     second = pl.BlockSpec((half, TILE), lambda t: (0, jnp.maximum(t - tiles, 0)))
-    ins = whole(x, *left, *right, vectors)
+    ins = scalars(place) + whole(x, *left, *right, *vectors)
     ins = ins + list(zip(expand, (first, first, second, second)))
     per_tile = (shape((2 * units, length)), pl.BlockSpec((TILE, length), lambda t: (t, 0)))
     outs = [
-        out_full((width, length)),
-        out_full((width, length)),
+        out_early((width, length)),
+        out_early((width, length)),
         out_full((8, length), F32),
         per_tile,
         per_tile,
     ]
-    scratch = [pltpu.VMEM((width, 128), F32)]
+    scratch = [pltpu.VMEM((units, 128), F32)]
     if merged:
-        ins = ins + whole(*reduce)
+        ins = ins + late(*reduce)
         outs = outs + out_pieces(width, length)
         scratch = scratch + [pltpu.VMEM((2 * units, length), BF)]
     return launch(
-        functools.partial(mlp_forward_kernel, merged, tiles, length, width),
+        functools.partial(mlp_forward_kernel, merged, layer, tiles, length, width),
         "mlp_forward",
         2 * tiles,
         ins,
         outs,
         scratch,
         14 if merged else 10,
-        44,
+        58,
     )
 
 
@@ -582,21 +687,22 @@
     )
 
 
-def mlp_backward_kernel(mode, natural, tiles, length, width, *refs):
+def mlp_backward_kernel(mode, layer, natural, tiles, length, width, *refs):
     refs = list(refs)
     place = refs.pop(0)
     half = width // 2
     units = tiles * TILE
     if mode == "last":
-        coef, cot, mid = refs[:3]
-        left, right = Pieces(refs[3:7]), Pieces(refs[7:11])
-        y0, vectors = refs[11:13]
-        del refs[:13]
+        coef, mid = refs[:2]
+        left, right = Pieces(refs[2:6]), Pieces(refs[6:10])
+        y0, vectors = refs[10], refs[11:15]
+        cot = RowParts(place, refs[15:19])
+        del refs[:19]
     elif mode == "first":
         coef, cot, gmid, x, st = refs[:5]
         left, right = Pieces(refs[5:9]), Pieces(refs[9:13])
-        y0, vectors = refs[13:15]
-        del refs[:15]
+        y0, vectors = refs[13], refs[14:18]
+        del refs[:18]
     else:
         gyb = refs.pop(0)
     n2, u_i, act, rd, rr, ed, er = refs[:7]
@@ -607,6 +713,9 @@
         gyb = refs.pop(0)
         if mode == "first":
             gx_o = refs.pop(0)
+        else:
+            cot_o, tail_o = refs[:2]
+            del refs[:2]
         sums_o, dots_o = refs[:2]
         del refs[:2]
     count = 1 if natural else 2
@@ -626,11 +735,12 @@
 
         @pl.when(t == 0)
         def _():
-            columns = vectors[...].T
+            columns = columns_of(place, vectors, layer, width // 4)
             dots_o[...] = jnp.zeros_like(dots_o)
             if mode == "last":
                 for rows in strips(width):
-                    value = cot[rows, :].astype(F32)
+                    value = cot[rows, :]
+                    cot_o[rows, :] = value.astype(BF)
                     gyb[rows, :] = (coef[1, HISTORY] * value).astype(BF)
                     y1 = (
                         mid[rows, :].astype(F32)
@@ -638,7 +748,9 @@
                         + right[rows, :].astype(F32)
                         + columns[rows, REDUCE_B : REDUCE_B + 1]
                     )
-                    dots_o[0:1, :] += jnp.sum(value * y0[rows, :].astype(F32), 0, keepdims=True)
+                    first = y0[rows, :].astype(F32)
+                    tail_o[rows, :] = (coef[1, HISTORY - 1] * first + coef[1, HISTORY] * y1).astype(BF)
+                    dots_o[0:1, :] += jnp.sum(value * first, 0, keepdims=True)
                     dots_o[1:2, :] += jnp.sum(value * y1, 0, keepdims=True)
                 sums_o[0:8, :] = row_sums(gyb[...])
             else:
@@ -686,12 +798,12 @@
         for at, w in ((0, ed), (half, er)):
             value = nn(w[...], gubs[...])
             if mode == "own":
-                part_o.store(at, value + add[at : at + half, :])
+                part_o.store(at, value + add[at : at + half, :].astype(F32))
             else:
-                part_o[at : at + half, :] = value
-
-
-def mlp_backward(place, natural, mode, opening, gyb, n2, u, act, group, reduce, expand, add):
+                part_o[at : at + half, :] = value.astype(BF)
+
+
+def mlp_backward(place, layer, natural, mode, opening, gyb, n2, u, act, group, reduce, expand, add):
     width, length = n2.shape
     half, units = expand[0].shape
     tiles = units // TILE
@@ -701,18 +813,19 @@
         ins = scalars(place) + whole(gyb)
     else:
         ins = scalars(place) + scalars(opening[0]) + whole(*opening[1:])
-        outs = outs + [out_full((width, length))]
+        outs = outs + [out_early((width, length)), out_early((width, length))]
+        if mode == "last":
+            outs = outs + [out_early((width, length))]
         if mode == "first":
-            outs = outs + [out_full((width, length))]
             scratch = scratch + [pltpu.VMEM((width, length), BF), pltpu.VMEM((width, length), BF)]
         outs = outs + [out_full((24, width), F32), out_full((8, length), F32)]
     at = group * tiles
     per_tile = pl.BlockSpec((TILE, length), lambda t: (at + t, 0))
     reduce_tile = pl.BlockSpec((TILE, half), lambda t: (t, 0))
     ins = ins + whole(n2) + [(u, per_tile), (act, per_tile)]
-    ins = ins + [(item, reduce_tile) for item in reduce] + whole(*expand)
+    ins = ins + [(item, reduce_tile) for item in reduce] + late(*expand)
     if add is not None:
-        ins = ins + whole(add)
+        ins = ins + late(add)
     if natural:
         outs = outs + [(shape((units, width)), pl.BlockSpec((TILE, width), lambda t: (t, 0)))] * 2
     else:
@@ -720,24 +833,25 @@
     outs = outs + [
         (shape((8, units), F32), pl.BlockSpec((8, TILE), lambda t: (0, t))),
     ]
-    outs = outs + (out_pieces(width, length) if add is not None else [out_full((width, length), F32)])
+    outs = outs + (out_pieces(width, length) if add is not None else [out_full((width, length))])
     return launch(
-        functools.partial(mlp_backward_kernel, mode, natural, tiles, length, width),
+        functools.partial(mlp_backward_kernel, mode, layer, natural, tiles, length, width),
         "mlp_backward",
         tiles,
         ins,
         outs,
         scratch,
         13,
-        44,
-    )
-
-
-def final_kernel(length, width, *refs):
+        58,
+    )
+
+
+def final_kernel(length, width, place, *refs):
     gmid, x, st = refs[:3]
     left, right = Pieces(refs[3:7]), Pieces(refs[7:11])
-    vectors, gx_o, sums_o, grad_n, grad_gain = refs[11:]
-    columns = vectors[...].T
+    vectors = refs[11:15]
+    gx_o, sums_o, grad_n, grad_gain = refs[15:]
+    columns = columns_of(place, vectors, 0, width // 4)
     norm_back(
         x,
         st,
@@ -755,17 +869,108 @@
     sums_o[8:16, :] = row_sums(grad_n[...])
 
 
-def final_backward(*operands):
+def final_backward(place, *operands):
     width, length = operands[0].shape
     return launch(
         functools.partial(final_kernel, length, width),
         "norm_backward",
         1,
-        whole(*operands),
+        scalars(place) + whole(*operands),
         [out_full((width, length)), out_full((16, width), F32)],
         [pltpu.VMEM((width, length), BF), pltpu.VMEM((width, length), BF)],
         5,
         32,
+    )
+
+
+def finish_kernel(entries, place, coef, history, cot, *refs):
+    tail, g0, gx0 = refs[0:2], refs[2:4], refs[4:6]
+    output, input_grad, history_grad, dots, total = refs[6:]
+    step = pl.program_id(0)
+    length = tail[0].shape[1]
+    halves = [
+        pl.ds(pl.multiple_of((place[0, ROW] ^ which) * length, length), length)
+        for which in range(2)
+    ]
+    behind = coef[1, jnp.maximum(step - 1, 0)]
+    carried = jnp.where(step == 0, 0.0, behind)
+
+    @pl.when(step == 0)
+    def _():
+        total[...] = jnp.zeros_like(total)
+        for cols, part in zip(halves, gx0):
+            input_grad[:, cols] = part[...].astype(F32)
+
+    entry = history[0]
+    total[...] += carried * entry
+    dots[0, 4:8, :] = jnp.broadcast_to(jnp.sum(cot[...] * entry, 0, keepdims=True), (4, 2 * length))
+    for cols, part in zip(halves, g0):
+        grad = part[...].astype(F32)
+        history_grad[0, :, cols] = coef[0, step] * grad + carried * cot[:, cols]
+        dots[0, 0:4, cols] = jnp.broadcast_to(
+            jnp.sum(grad * history[0, :, cols], 0, keepdims=True), (4, length)
+        )
+
+    @pl.when(step == entries - 1)
+    def _():
+        for cols, part in zip(halves, tail):
+            output[:, cols] = total[:, cols] + part[...].astype(F32)
+
+
+def finish(place, coef, history, cot, tail, g0, gx0):
+    entries, part, tokens = history.shape
+    block = pl.BlockSpec((1, part, tokens), lambda t: (t, 0, 0))
+    return launch(
+        functools.partial(finish_kernel, entries),
+        "finish",
+        entries,
+        scalars(place) + scalars(coef) + [(history, block)] + whole(cot, *tail, *g0, *gx0),
+        [
+            out_full((part, tokens), F32),
+            out_full((part, tokens), F32),
+            (shape((entries, part, tokens), F32), block),
+            (
+                shape((entries, 8, tokens), F32),
+                pl.BlockSpec((1, 8, tokens), lambda t: (t, 0, 0)),
+            ),
+        ],
+        [pltpu.VMEM((part, tokens), F32)],
+        6,
+        40,
+    )
+
+
+def lines_kernel(wide, part, mine_at, sent_at, place, *refs):
+    count = len(wide)
+    sums, pairs = refs[:count], refs[count : count + 8]
+    mix, mine_o, sent_o = refs[count + 8 :]
+    for out, which, index in ((mine_o, 0, place[0, mine_at]), (sent_o, 1, place[0, sent_at])):
+        out[...] = jnp.zeros_like(out)
+        for at, (ref, row) in enumerate(zip(sums, wide)):
+            line = ref[row : row + 1, :]
+            cut = line[:, :part]
+            for q in range(1, 4):
+                cut = jnp.where(index == q, line[:, q * part : (q + 1) * part], cut)
+            out[at : at + 1, :part] = cut
+        for l in range(LAYERS):
+            for k in range(2):
+                line = pairs[4 * l + 2 * which + k][0:1, :]
+                out[count + 2 * l + k : count + 2 * l + k + 1, : line.shape[1]] = line
+        at = count + 2 * LAYERS
+        out[at : at + 1, : mix.shape[1]] = mix[0:1, :]
+
+
+def vector_lines(place, wide, pairs, mix, width, part):
+    rows = -(-(len(wide) + 2 * LAYERS + 1) // 8) * 8
+    return launch(
+        functools.partial(lines_kernel, [row for _, row in wide], part, 4, 5),
+        "vector_lines",
+        1,
+        scalars(place) + whole(*[item for item, _ in wide], *pairs, mix),
+        [out_full((rows, width), F32)] * 2,
+        [],
+        2,
+        16,
     )
 
 
@@ -797,38 +1002,112 @@
     )
 
 
-def spread(mine, flip, core):
-    theirs = swap_row(mine)
-    pair = ordered(mine[None], theirs[None], flip)
-    other = swap_core(pair)
-    return (
-        jnp.where(
-            core == 0,
-            jnp.stack([pair[0], other[0], pair[1], other[1]]),
-            jnp.stack([other[0], pair[0], other[1], pair[1]]),
-        ),
-        theirs,
-    )
-
-
-def row_steps(value, row, core, flip):
-    length = value.shape[1] // 2
-    low = value.astype(BF)
-    mine = lax.dynamic_slice_in_dim(low, row * length, length, 1)
-    (theirs,) = yield [swap_row(lax.dynamic_slice_in_dim(low, (1 - row) * length, length, 1))]
-    pair = ordered(mine[None], theirs[None], flip)
-    other = swap_core(pair)
-    gathered = jnp.where(
-        core == 0,
-        jnp.stack([pair[0], other[0], pair[1], other[1]]),
-        jnp.stack([other[0], pair[0], other[1], pair[1]]),
-    )
-    yield gathered.reshape(4 * value.shape[0], length)
+def cast_kernel(kinds, place, *refs):
+    refs = list(refs)
+    outs = refs[-2 * len(kinds) :]
+    for index, kind in enumerate(kinds):
+        near_o, far_o = outs[2 * index : 2 * index + 2]
+        for out, which in ((near_o, 0), (far_o, 1)):
+            if kind == "expand":
+                half = out.shape[0]
+                rows = pl.ds(pl.multiple_of((place[0, BIT] ^ which) * half, half), half)
+                out[...] = refs[0][0, rows, :].astype(BF)
+                continue
+            half = out.shape[1]
+            cols = pl.ds(pl.multiple_of((place[0, BIT] ^ which) * half, half), half)
+            if kind == "reduce":
+                out[...] = refs[0][0, :, cols].astype(BF)
+                continue
+            part = refs[1].shape[1]
+            for k in range(3):
+                out[k * part : (k + 1) * part, :] = refs[0][0, k, :, cols].astype(BF)
+            out[3 * part :, :] = refs[1][0, :, cols].astype(BF)
+        del refs[: 2 if kind == "attn" else 1]
+
+
+def cast_weights(place, layer, kinds, operands):
+    ins = scalars(place)
+    for item in operands:
+        block = (1,) + item.shape[1:]
+        ins.append(
+            (item, pl.BlockSpec(block, lambda t, n=len(block): (layer,) + (0,) * (n - 1)))
+        )
+    outs = []
+    for kind in kinds:
+        if kind == "attn":
+            dims = (4 * operands[0].shape[2], operands[0].shape[3] // 2)
+        elif kind == "expand":
+            dims = (operands[-2].shape[1] // 2, operands[-2].shape[2])
+        else:
+            dims = (operands[-1].shape[1], operands[-1].shape[2] // 2)
+        outs += [out_full(dims), out_full(dims)]
+    found = launch(
+        functools.partial(cast_kernel, kinds), "cast", 1, ins, outs, [], 2 * len(kinds), 40
+    )
+    return [tuple(found[i : i + 2]) for i in range(0, len(found), 2)]
+
+
+def split_rows_kernel(entries, place, *refs):
+    if entries:
+        coef, value, mine, sent, total = refs
+        step = pl.program_id(0)
+
+        @pl.when(step == 0)
+        def _():
+            total[...] = coef[0, 0] * value[0]
+
+        @pl.when(step > 0)
+        def _():
+            total[...] += coef[0, step] * value[0]
+
+        source = total
+    else:
+        source, mine, sent = refs
+    length = mine.shape[1]
+    for out, which in ((mine, 0), (sent, 1)):
+        cols = pl.ds(pl.multiple_of((place[0, ROW] ^ which) * length, length), length)
+        if entries:
+
+            @pl.when(step == entries - 1)
+            def _():
+                out[...] = source[:, cols].astype(BF)
+
+        else:
+            out[...] = source[:, cols].astype(BF)
+
+
+def split_rows(place, value, coef=None):
+    part, tokens = value.shape[-2:]
+    ins = scalars(place)
+    if coef is None:
+        steps, entries = 1, 0
+        ins = ins + whole(value)
+        scratch = []
+    else:
+        steps = entries = value.shape[0]
+        ins = ins + scalars(coef) + [(value, pl.BlockSpec((1, part, tokens), lambda t: (t, 0, 0)))]
+        scratch = [pltpu.VMEM((part, tokens), F32)]
+    return launch(
+        functools.partial(split_rows_kernel, entries),
+        "split_rows",
+        steps,
+        ins,
+        [out_full((part, tokens // 2))] * 2,
+        scratch,
+        2,
+        24,
+    )
+
+
+def gather_steps(mine, sent):
+    theirs, core_mine = yield [swap_row(sent), swap_core(mine)]
+    (core_theirs,) = yield [swap_core(theirs)]
+    yield [mine, theirs, core_mine, core_theirs]
 
 
 def home_steps(mine, sent, row):
     (theirs,) = yield [swap_row(sent)]
-    yield ordered(mine, theirs, row, 1).astype(F32)
+    yield mine, theirs
 
 
 def fetch_steps(near, far, relay):
@@ -875,7 +1154,7 @@
     return (mine.astype(F32) + theirs.astype(F32)).astype(BF)
 
 
-def assemble_kernel(turned, counts, halves, *refs):
+def assemble_kernel(turned, counts, halves, pick, *refs):
     if halves:
         place, near, far = refs[:3]
         scratch = refs[-1]
@@ -886,8 +1165,9 @@
         scratch[:, :half] = jnp.where(first, a, b)
         scratch[:, half:] = jnp.where(first, b, a)
     else:
-        scratch = refs[0]
+        place, near, far = refs[:3]
         outs = refs[len(refs) - len(counts) :]
+        scratch = jnp.where(place[0, BIT] == pick, near[...].astype(F32), far[...].astype(F32))
     at = 0
     for out, count in zip(outs, counts):
         value = scratch[at : at + count, :].astype(F32)
@@ -896,8 +1176,13 @@
 
 
 def assemble(total, place, layer, shapes, counts, turned, held):
-    halves = isinstance(total, tuple)
-    ins = scalars(place) + whole(*total) if halves else whole(total)
+    halves = not isinstance(total[1], int)
+    pick = 0
+    if halves:
+        ins = scalars(place) + whole(*total)
+    else:
+        total, pick = total
+        ins = scalars(place) + whole(*total)
     aliases = {}
     if held is not None:
         for index, item in enumerate(held):
@@ -910,7 +1195,7 @@
     rows = sum(counts)
     scratch = [pltpu.VMEM((rows, 2 * total[0].shape[1]), F32)] if halves else []
     return launch(
-        functools.partial(assemble_kernel, turned, counts, halves),
+        functools.partial(assemble_kernel, turned, counts, halves, pick),
         "assemble",
         1,
         ins,
@@ -939,9 +1224,50 @@
     yield value, got[0]
 
 
-def whole_steps(own, other):
-    (got,) = yield [swap_row(other)]
-    yield add_all((own,), (got,))
+def half_steps(items):
+    got = []
+    for item in items:
+        *got, last = yield got + [swap_row(item)]
+        got = got + [last]
+
+
+def reversed_bits(index, count):
+    return sum(((index >> k) & 1) << (count - 1 - k) for k in range(count))
+
+
+def add_stack_kernel(count, bits, place, *refs):
+    out = refs[-1]
+    size, half = refs[0].shape
+    block = out.shape[0] >> bits
+    for index in range(count):
+        a, b = refs[index], refs[count + index]
+        cols = pl.ds(pl.multiple_of((place[0, BIT] ^ (index % 2)) * half, half), half)
+        for start in range(0, size, block):
+            to = reversed_bits(((index // 2) * size + start) // block, bits) * block
+            value = a[start : start + block, :].astype(F32) + b[start : start + block, :].astype(F32)
+            out[to : to + block, cols] = value.astype(BF)
+
+
+def add_stack(place, mine, theirs, bits):
+    rows, half = mine[0].shape
+    return launch(
+        functools.partial(add_stack_kernel, len(mine), bits),
+        "add",
+        1,
+        scalars(place) + whole(*mine, *theirs),
+        [out_full((rows * len(mine) // 2, 2 * half))],
+        [],
+        4,
+        32,
+    )[0]
+
+
+def spread_steps(value, bits):
+    for step in reversed(range(1, len(bits))):
+        got = yield [swap_dp(value, 1 << step)]
+        value = ordered(value, got[0], bits[step])
+    got = yield [swap_dp(value, 1)]
+    yield value, got[0]
 
 
 class Chain:
@@ -1011,261 +1337,259 @@
     angles = frequency[:, None] * jnp.arange(length, dtype=F32)[None, :]
     cos, sin = jnp.cos(angles), jnp.sin(angles)
 
-    place = bit.reshape(1, 1).astype(jnp.int32)
-    x0_chain = Chain(row_steps(inputs, row, core, flip))
-    x0_chain.advance()
-
+    mine_at, sent_at = 2 * flip + core, 2 * (1 - flip) + core
+    place = jnp.stack([bit, row, flip, core, mine_at, sent_at]).reshape(1, 6).astype(jnp.int32)
+    attn_low = cast_weights(place, 0, ("attn",), (input_weight, merge_weight))
+    attn_near, first_inputs = lax.optimization_barrier((attn_low[0][0], inputs))
+    attn_w = [Weight(attn_near, attn_low[0][1])]
+    attn_w[0].chain.advance()
+    x0_low = split_rows(place, first_inputs)
     small = jnp.concatenate(
-        [
-            item.reshape(LAYERS, -1)
-            for item in (
-                input_bias,
-                expand_bias,
-                first_gain,
-                first_shift,
-                second_gain,
-                second_shift,
-                merge_bias,
-                reduce_bias,
-            )
+        [item.reshape(LAYERS, -1, part) for item in (input_bias, expand_bias)]
+        + [
+            item.reshape(LAYERS, 1, part)
+            for item in (first_gain, first_shift, second_gain, second_shift, merge_bias, reduce_bias)
         ],
         1,
     )
-    def low_halves(source, axis):
-        return half_of(source, bit, axis).astype(BF), half_of(source, 1 - bit, axis).astype(BF)
-
-    def merged(l, first, second):
-        return jnp.concatenate([first[l].reshape(3 * part, width), second[l]], 0)
-
-    attn_w = [Weight(*low_halves(merged(0, input_weight, merge_weight), 1))]
-    attn_w[0].chain.advance()
-    attn_w[0].chain.held, early, small = lax.optimization_barrier(
-        (attn_w[0].chain.held, (expand_weight, reduce_weight), small)
-    )
-    expand_w = [Weight(*low_halves(early[0][0], 0))]
+    small = jnp.pad(
+        small, ((0, 0), (0, TABLE_ROWS - small.shape[1]), (0, TABLE_LANES - part))
+    )
+    feed_low = cast_weights(place, 0, ("expand", "reduce"), (expand_weight, reduce_weight))
+    x0_low, small = lax.optimization_barrier((x0_low, small))
+    x0_chain = Chain(gather_steps(*x0_low))
+    x0_chain.advance()
+    vector_chain = Chain(gather_steps(small, small))
+    attn_w[0].chain.held, feed_near = lax.optimization_barrier(
+        (attn_w[0].chain.held, [feed_low[0][0], feed_low[1][0]])
+    )
+    expand_w = [Weight(feed_near[0], feed_low[0][1])]
     expand_w[0].chain.advance()
-    reduce_w = [Weight(*low_halves(early[1][0], 1))]
-    quarters, small_other = spread(small, flip, core)
+    reduce_w = [Weight(feed_near[1], feed_low[1][1])]
+    vectors = vector_chain.finish()
+    x0_chain.advance()
+    x0_chain.held, late_weights, late_history = lax.optimization_barrier(
+        (x0_chain.held, (input_weight, merge_weight, expand_weight, reduce_weight), history)
+    )
+    later = cast_weights(place, 1, ("attn", "expand", "reduce"), late_weights)
+    hm_low = split_rows(place, late_history, depth_weights)
+    x0 = x0_chain.finish()
+    x0[0], later, hm_low = lax.optimization_barrier((x0[0], later, hm_low))
+    attn_w.append(Weight(*later[0]))
+    expand_w.append(Weight(*later[1]))
+    reduce_w.append(Weight(*later[2], relay=False))
+    hm0 = Chain(gather_steps(*hm_low))
+    cot_chain = Chain(gather_steps(*split_rows(place, cotangent)))
     at = 3 * part + units
-    wide = quarters[:, :, at:].reshape(4, LAYERS, 6, part).transpose(1, 2, 0, 3)
-    wide = wide.reshape(LAYERS, 6, width)
-    pair = jnp.stack([small, small_other], 1)
-    input_rows = jnp.pad(pair[:, :, : 3 * part], ((0, 0), (0, 0), (0, width - 3 * part)))
-    vectors = jnp.concatenate(
-        [wide, input_rows, pair[:, :, 3 * part : at], jnp.zeros((LAYERS, 6, width), F32)], 1
-    )
-
-    x0 = x0_chain.finish()
-    x0, late_weights, past = lax.optimization_barrier(
-        (x0, (input_weight, merge_weight, expand_weight, reduce_weight), history)
-    )
-    attn_w.append(Weight(*low_halves(merged(1, *late_weights[:2]), 1)))
-    expand_w.append(Weight(*low_halves(late_weights[2][1], 0)))
-    reduce_w.append(Weight(*low_halves(late_weights[3][1], 1), relay=False))
-    mixed_history = sum(depth_weights[0, j] * past[j] for j in range(HISTORY))
-    hm0 = Chain(row_steps(mixed_history, row, core, flip))
-    cot_chain = Chain(row_steps(cotangent, row, core, flip))
 
     saved = []
     mix = None
     for l in range(LAYERS):
-        vec = vectors[l]
         outs = attention_forward(
-            mix, x0 if l == 0 else None, vec, attn_w[l].parts(), cos, sin, segments
+            place, mix, x0 if l == 0 else hm0, vectors, l, attn_w[l].parts(), cos, sin, segments
         )
-        if l == 0:
-            x = x0
-        else:
-            y0, x = outs[:2]
-            outs = outs[2:]
+        if l == 1:
+            y0 = outs[0]
+            outs = outs[1:]
+        x = outs[0]
+        outs = outs[1:]
         n1, st1, q, k, v, o, lse = outs[:7]
         left = list(outs[7:])
         if l == 0:
-            left[0] = pin(left[0], expand_w[0].chain, reduce_w[0].chain, hm0)
+            left[0] = pin(left[0], expand_w[0].chain, reduce_w[0].chain)
         else:
             left[0] = pin(left[0], expand_w[1].chain, reduce_w[1].chain)
         right = swap_pieces(left)
         if l == 0:
-            mid, n2, st2, u, act = mlp_forward(x, left, right, vec, expand_w[0].parts(), None)
-            act = pin(act, attn_w[1].chain, reduce_w[0].chain)
-            left = reduce_forward(act, reduce_w[0].parts())
+            right[0] = pin(right[0], attn_w[1].chain)
+            mid, n2, st2, u, act = mlp_forward(
+                place, x, left, right, vectors, l, expand_w[0].parts(), None
+            )
+            act = pin(act, reduce_w[0].chain, hm0)
+            left = list(reduce_forward(act, reduce_w[0].parts()))
+            left[0] = pin(left[0], attn_w[1].chain)
             hm0 = hm0.finish()
             right = swap_pieces(left)
-            right[0] = pin(right[0], attn_w[1].chain, expand_w[1].chain)
+            right[0] = pin(right[0], expand_w[1].chain)
         else:
             mid, n2, st2, u, act, *left = mlp_forward(
-                x, left, right, vec, expand_w[1].parts(), reduce_w[1].parts()
+                place, x, left, right, vectors, l, expand_w[1].parts(), reduce_w[1].parts()
             )
             left[0] = pin(left[0], cot_chain)
             right = swap_pieces(left)
         saved.append((x, n1, st1, (q, k, v, o, lse), mid, n2, st2, u, act, left, right))
-        mix = (depth_weights, hm0, mid, *left, *right, vec)
+        mix = (depth_weights, mid, *left, *right)
 
     cot = cot_chain.finish()
-    mid1, left1, right1 = saved[1][4], saved[1][9], saved[1][10]
-
     def quarter_of(value, index):
         return lax.dynamic_slice_in_dim(value, index * part, part, 0)
-
-    mine_at, sent_at = 2 * flip + core, 2 * (1 - flip) + core
-
-    def tail_quarter(index):
-        cut = lambda item: quarter_of(item, index).astype(F32)
-        pick = lambda items: jnp.where(
-            index < 2, jnp.where(index == 0, items[0], items[1]), jnp.where(index == 2, items[2], items[3])
-        ).astype(F32)
-        y1 = cut(mid1) + pick(left1) + pick(right1) + cut(vectors[1, REDUCE_B])[:, None]
-        return (depth_weights[1, last] * cut(y0) + depth_weights[1, last + 1] * y1).astype(BF)
 
     chains = [{} for _ in range(LAYERS)]
     sums = [{} for _ in range(LAYERS)]
     for l in reversed(range(LAYERS)):
         x, n1, st1, heads, mid, n2, st2, u, act, y_left, y_right = saved[l]
-        vec = vectors[l]
         aw, ew, rw = attn_w[l], expand_w[l], reduce_w[l]
-        natural = l == 1
-        count = 1 if natural else 2
+        count = 2
         if l == 1:
-            opening = (depth_weights, cot, mid, *y_left, *y_right, y0, vec)
-            gyb, wide_sums, dots1, *grads = mlp_backward(
-                place, natural, "last", opening, None, n2, u, act, 1, rw.other(), ew.other(), None
+            opening = (depth_weights, mid, *y_left, *y_right, y0, *vectors, *cot)
+            gyb, cot, tail, wide_sums, dots1, *grads = mlp_backward(
+                place, 1, False, "last", opening, None, n2, u, act, 1, rw.other(), ew.other(), None
             )
         else:
-            right[0] = pin(right[0], chains[1]["attn"])
-            matrices = ("reduce", "expand", "attn")
-            for name in matrices:
-                chains[1][name].advance()
-            right[0], sums_1 = lax.optimization_barrier(
-                (right[0], [chains[1][name].held[0] for name in matrices])
-            )
-            sums_1 = lax.psum(sums_1, "dp")
             opening = (
-                (depth_weights, cot, gmb, saved[1][0], saved[1][2], *left, *right, y0, vectors[1])
+                (depth_weights, cot, gmb, saved[1][0], saved[1][2], *left, *right, y0, *vectors)
             )
             gyb, gx1, wide_sums, dots0, *grads = mlp_backward(
-                place, natural, "first", opening, None, n2, u, act, 1, rw.other(), ew.other(), None
+                place, 1, False, "first", opening, None, n2, u, act, 1, rw.other(), ew.other(), None
             )
-            sums[1]["gain1"], sums[1]["shift1"] = wide_sums[8], wide_sums[16]
-            gx1_home = Chain(home_steps(quarter_of(gx1, mine_at), quarter_of(gx1, sent_at), row))
-        sums[l]["reduce_b"] = wide_sums[0]
+            chains[1]["attn"].advance()
+            gyb = pin(gyb, chains[1]["attn"])
+            sums[1]["gain1"], sums[1]["shift1"] = (wide_sums, 8), (wide_sums, 16)
+        sums[l]["reduce_b"] = (wide_sums, 0)
         e_other, r_other = grads[:count], grads[count : 2 * count]
         be1, partial = grads[2 * count :]
         *grads, be0, l0, l1, l2, l3 = mlp_backward(
-            place, natural, "own", None, gyb, n2, u, act, 0, rw.own, ew.own, partial
+            place, l, False, "own", None, gyb, n2, u, act, 0, rw.own, ew.own, partial
         )
         e_own, r_own, left = grads[:count], grads[count:], [l0, l1, l2, l3]
-        if natural:
+        if l == 1:
             right = swap_pieces(left)
-            chains[l]["reduce"] = Chain(whole_steps(r_own[0], r_other[0]))
-            chains[l]["expand"] = Chain(whole_steps(e_own[0], e_other[0]))
-            right[0] = pin(right[0], chains[l]["reduce"])
+            feed_own = r_own + e_own
+            chains[1]["feed"] = Chain(half_steps(r_other + e_other))
+            right[0] = pin(right[0], chains[1]["feed"])
         else:
             chains[l]["reduce"] = Chain(reduce_steps(r_own, r_other, bits))
             chains[l]["expand"] = Chain(reduce_steps(e_own, e_other, bits))
-            left[0] = pin(left[0], chains[l]["reduce"])
+            left[0] = pin(left[0], chains[l]["reduce"], chains[1]["attn"])
             right = swap_pieces(left)
             right[0] = pin(right[0], chains[l]["reduce"])
-        opening = (gyb, *left, *right, mid, st2, vec)
+        opening = (gyb, *left, *right, mid, st2, *vectors)
         gmb, wide_sums, *grads, db1, partial = attention_backward(
-            place, natural, opening, None, n1, aw.other(), cos, sin, segments, heads, 1, None
+            place, l, False, opening, None, n1, aw.other(), cos, sin, segments, heads, 1, None
         )
         a_other = grads
         sums[l]["gain2"], sums[l]["shift2"], sums[l]["merge_b"] = (
-            wide_sums[0],
-            wide_sums[8],
-            wide_sums[16],
+            (wide_sums, 0),
+            (wide_sums, 8),
+            (wide_sums, 16),
         )
         if l == 1:
-            gmb = pin(gmb, chains[l]["expand"])
+            gmb = pin(gmb, chains[1]["feed"])
         else:
             chains[0]["expand"].advance()
-            gmb = pin(gmb, chains[l]["reduce"], chains[l]["expand"])
+            gmb = pin(gmb, chains[l]["reduce"], chains[l]["expand"], chains[1]["attn"])
+            gmb, sums_1 = lax.optimization_barrier((gmb, sums_1))
+            chains[1]["feed"] = Chain(spread_steps(sums_1, bits))
         *grads, db0, l0, l1, l2, l3 = attention_backward(
-            place, natural, None, gmb, n1, aw.own, cos, sin, segments, heads, 0, partial
+            place, l, False, None, gmb, n1, aw.own, cos, sin, segments, heads, 0, partial
         )
         left = [l0, l1, l2, l3]
+        chains[l]["attn"] = Chain(reduce_steps(grads, a_other, bits))
         if l == 0:
-            left[0] = pin(left[0], chains[0]["reduce"], chains[0]["expand"])
-        right = swap_pieces(left)
-        if natural:
-            chains[l]["attn"] = Chain(whole_steps(grads[0], a_other[0]))
+            chains[0]["attn"].advance()
+            left[0] = pin(
+                left[0],
+                chains[0]["reduce"],
+                chains[0]["expand"],
+                chains[1]["attn"],
+                chains[0]["attn"],
+                chains[1]["feed"],
+            )
         else:
-            chains[l]["attn"] = Chain(reduce_steps(grads, a_other, bits))
-        sums[l]["pair"] = ((db0[0], be0[0]), (db1[0], be1[0]))
-    chains[0]["attn"].advance()
-    right[0] = pin(
-        right[0], chains[0]["attn"], chains[0]["reduce"], chains[0]["expand"], gx1_home
-    )
+            right = swap_pieces(left)
+            chains[1]["feed"].advance()
+            right[0] = pin(right[0], chains[1]["feed"])
+            sums_1 = add_stack(place, feed_own, chains[1]["feed"].held, len(bits))
+            sums_1 = lax.psum_scatter(sums_1, "dp", scatter_dimension=0, tiled=True)
+        sums[l]["pair"] = ((db0, be0), (db1, be1))
+    final = chains[0]["attn"]
+    ahead = (chains[0]["reduce"], chains[0]["expand"], chains[1]["attn"], chains[1]["feed"])
+
+    def onward(*passing):
+        final.advance()
+        for chain in ahead:
+            chain.advance()
+        final.held, held, passing = lax.optimization_barrier(
+            (final.held, [chain.held for chain in ahead], passing)
+        )
+        for chain, value in zip(ahead, held):
+            chain.held = value
+        return passing
+
+    right = swap_pieces(left)
+    gx1, tail = lax.optimization_barrier((left[0], (gx1, tail)))[1]
+    homes = [
+        Chain(home_steps(quarter_of(item, mine_at), quarter_of(item, sent_at), row))
+        for item in (gx1, tail)
+    ]
+    for home in homes:
+        home.advance()
+    final.advance()
+    chains[0]["reduce"].advance()
+    chains[1]["attn"].advance()
+    chains[1]["feed"].advance()
     gx0, wide_sums = final_backward(
-        gmb, saved[0][0], saved[0][2], *left, *right, vectors[0]
-    )
-    sums[0]["gain1"], sums[0]["shift1"] = wide_sums[0], wide_sums[8]
-
-    final = chains[0]["attn"]
-
-    def onward(*others):
-        *waiting, chains_now = others
-        final.advance()
-        for chain in chains_now:
-            chain.advance()
-        final.held, held, waiting = lax.optimization_barrier(
-            (final.held, [chain.held for chain in chains_now], waiting)
-        )
-        for chain, value in zip(chains_now, held):
-            chain.held = value
-        return waiting
-
-    ahead = (chains[0]["reduce"], chains[0]["expand"])
-    gx0_home = Chain(home_steps(quarter_of(gx0, mine_at), quarter_of(gx0, sent_at), row))
-    past, late_cot = onward(history, cotangent, ahead + (gx0_home,))
-    g0_home = gx1_home.finish()
-    input_grad = gx0_home.finish()
-    history_out = []
-    for j in range(HISTORY):
-        term = depth_weights[0, j] * g0_home
-        if j >= 1:
-            term = term + depth_weights[1, j - 1] * late_cot
-        history_out.append(term)
-
-    past, late_cot, tail_mine, tail_sent = onward(
-        past, late_cot, tail_quarter(mine_at), tail_quarter(sent_at), ahead
-    )
+        place, gmb, saved[0][0], saved[0][2], *left, *right, *vectors
+    )
+    sums[0]["gain1"], sums[0]["shift1"] = (wide_sums, 0), (wide_sums, 8)
+
+    final.held, held, homes[0].held, homes[1].held, gx0 = lax.optimization_barrier(
+        (final.held, [chain.held for chain in ahead], homes[0].held, homes[1].held, gx0)
+    )
+    for chain, value in zip(ahead, held):
+        chain.held = value
+    homes.append(Chain(home_steps(quarter_of(gx0, mine_at), quarter_of(gx0, sent_at), row)))
+    homes[2].advance()
+    pairs = [found.pop("pair") for found in sums]
+    row_at = [{name: at for name, (_, at) in found.items()} for found in sums]
+    held_sums = [{name: item for name, (item, _) in found.items()} for found in sums]
+    late_cot, past, held_sums, pairs, dots0, dots1, homes[2].held = onward(
+        cotangent, history, held_sums, pairs, dots0, dots1, homes[2].held
+    )
+    output, input_grad, history_out, dots = finish(
+        place, depth_weights, past, late_cot, *[home.finish() for home in (homes[1], homes[0], homes[2])]
+    )
+    output, input_grad, history_out, dots = onward(output, input_grad, history_out, dots)
+    entry_dots = jnp.sum(dots[:, ::4], 2)
 
     def by_core(value):
         return jnp.where(core == 0, jnp.sum(value), 0.0)
 
-    mix0 = [jnp.sum(g0_home * past[j]) for j in range(HISTORY)] + [by_core(dots0[0])]
-    mix1 = [jnp.sum(late_cot * past[j + 1]) for j in range(last)] + [
-        by_core(dots1[0]),
-        by_core(dots1[1]),
-    ]
-    mix_sum = jnp.concatenate([jnp.stack(mix0), jnp.stack(mix1)])
+    mix_sum = jnp.concatenate(
+        [
+            entry_dots[:, 0],
+            by_core(dots0[0])[None],
+            entry_dots[1:, 1],
+            by_core(dots1[0])[None],
+            by_core(dots1[1])[None],
+        ]
+    )
     mix_sum = mix_sum + swap_core(mix_sum)
-    output_home = Chain(home_steps(tail_mine, tail_sent, row))
-    (past,) = onward(past, ahead + (output_home,))
-    output = sum(depth_weights[1, j] * past[j + 1] for j in range(last)) + output_home.finish()
-    onward(ahead)
-    (sums_1,) = onward(sums_1, ahead)
 
     names = ("gain1", "shift1", "gain2", "shift2", "merge_b", "reduce_b")
-    lines = []
-    for index, which in ((mine_at, 0), (sent_at, 1)):
-        line = []
-        for l in range(LAYERS):
-            stacked = jnp.stack([sums[l][name] for name in names])
-            cut = lax.dynamic_slice_in_dim(stacked, index * part, part, 1)
-            line += [sums[l]["pair"][which][0], sums[l]["pair"][which][1], cut.reshape(-1)]
-        lines.append(jnp.concatenate(line + [mix_sum]))
+
+    wide = [(held_sums[l][name], row_at[l][name]) for l in range(LAYERS) for name in names]
+    flat_pairs = [pairs[l][which][k] for l in range(LAYERS) for which in range(2) for k in range(2)]
+    lines = vector_lines(
+        place, wide, flat_pairs, jnp.pad(mix_sum, (0, 128 - mix_sum.shape[0]))[None], width, part
+    )
     total = lines[0] + swap_row(lines[1])
+    (total,) = onward(total)
     for step in range(len(bits)):
         total = total + swap_dp(total, 1 << step)
-    mix_grad = total[-mix_sum.shape[0] :].reshape(LAYERS, HISTORY + 1)
-    per_layer = total[: -mix_sum.shape[0]].reshape(LAYERS, -1)
-    wide_out = [per_layer[:, at + i * part : at + (i + 1) * part] for i in range(6)]
+    at = LAYERS * 6
+    mix_grad = total[at + 2 * LAYERS, : mix_sum.shape[0]].reshape(LAYERS, HISTORY + 1)
+    wide_out = [total[i:at:6, :part] for i in range(6)]
+    input_out = total[at : at + 2 * LAYERS : 2, : 3 * part].reshape(LAYERS, 3, part)
+    expand_out = total[at + 1 : at + 2 * LAYERS : 2, :units]
 
     attn_t = expand_t = reduce_t = None
     for l in reversed(range(LAYERS)):
-        total = [chains[l][name].finish() for name in matrices] if l == 0 else sums_1
+        if l == 0:
+            total = [chains[l][name].finish() for name in ("reduce", "expand", "attn")]
+        else:
+            feed = chains[1]["feed"].finish()
+            total = [(feed, 0), (feed, 1), chains[1]["attn"].finish()]
         reduce_t = assemble(total[0], place, l, [(LAYERS, units, width)], [units], False, reduce_t)
         expand_t = assemble(total[1], place, l, [(LAYERS, width, units)], [units], True, expand_t)
         attn_t = assemble(
@@ -1280,9 +1604,9 @@
     return (
         output,
         input_grad,
-        jnp.stack(history_out),
+        history_out,
         attn_t[0],
-        per_layer[:, : 3 * part].reshape(LAYERS, 3, part),
+        input_out,
         attn_t[1],
         wide_out[4],
         wide_out[0],
@@ -1290,7 +1614,7 @@
         wide_out[2],
         wide_out[3],
         expand_t[0],
-        per_layer[:, 3 * part : at],
+        expand_out,
         reduce_t[0],
         wide_out[5],
         mix_grad,

time: 560 us -> 503 us (0.90)
  other arithmetic: 58.4 us -> 13.5 us
  local copies, waits for them, and re-layouts: 85.3 us -> 42.6 us
  Pallas kernels: 206 us -> 240 us
  waiting for transfers between devices: 123 us -> 89.1 us
  starting transfers between devices: 63.3 us -> 96.3 us
    pallas_call x29 -> x37, Pallas kernels: 206 us -> 240 us  [launch(): pl.pallas_call(body, grid=(steps,), in_specs=[anywhere if spec is LATE el...]
    ppermute x26 -> x35, waiting for transfers between devices: 82.2 us -> 49.6 us  [swap_dp(): return lax.ppermute(value, 'dp', [(i, i ^ bit) for i in range(size)])]
    ppermute x26 -> x35, starting transfers between devices: 28.7 us -> 55.9 us  [swap_dp(): return lax.ppermute(value, 'dp', [(i, i ^ bit) for i in range(size)])]
    slice x33 -> x12, local copies, waits for them, and re-layouts: 25.3 us -> 4.83 us  [the longest x6 3.55 us: shards(): wide_out = [total[i:at:6, :part] for i in range(6)]]
    another operation x4 -> x0, other arithmetic: 18.5 us -> none  [the longest x3 12.4 us: shards(): jnp.stack(history_out)]
    convert_element_type x7 -> x0, other arithmetic: 11.5 us -> none  [the longest x2 8.14 us: tail_quarter(): (depth_weights[1, last] * cut(y0) + depth_weights[1, last + 1] * y1).asty...]
    concatenate x5 -> x2, local copies, waits for them, and re-layouts: 7.02 us -> 0.14 us  [the longest x1 0.09 us: shards(): jnp.concatenate([entry_dots[:, 0], by_core(dots0[0])[None], entry_dots[1:...]
    add x1 -> x0, other arithmetic: 6.21 us -> none  [shards(): sum((depth_weights[1, j] * past[j + 1] for j in range(last)))]
  transfers between devices with their start and end apart: 88 -> 104, of which waited for: 31 -> 33; matrix products, arithmetic and copies ran while one was open for 18% -> 4% of each run, Pallas kernels for 31% -> 44%
where the time goes in v3:
time: 503 us; the launch traced here: 499 us
  Pallas kernels  240 us (48%)
  starting transfers between devices  96.3 us (19%)
  waiting for transfers between devices  89.1 us (18%)
  local copies, waits for them, and re-layouts  42.6 us (8%)
  between operations  18.1 us (4%)
  other arithmetic  13.5 us (3%)
    pallas_call x37, Pallas kernels, launch(): pl.pallas_call(body, grid=(steps,), in_specs=[anywhere if spec is LATE el...  240 us
    ppermute x35, starting transfers between devices, swap_dp(): return lax.ppermute(value, 'dp', [(i, i ^ bit) for i in range(size)])  55.9 us
    ppermute x35, waiting for transfers between devices, swap_dp(): return lax.ppermute(value, 'dp', [(i, i ^ bit) for i in range(size)])  49.6 us
    ppermute x27, waiting for transfers between devices, swap_row(): return lax.ppermute(value, 'mp', [(i, i ^ 2) for i in range(size)])  33.6 us
    unnamed x296, local copies, waits for them, and re-layouts  32.5 us
    ppermute x27, starting transfers between devices, swap_row(): return lax.ppermute(value, 'mp', [(i, i ^ 2) for i in range(size)])  30.5 us
  transfers between devices with their start and end apart: 104, of which 33 were waited for; matrix products, arithmetic and copies ran while one was open for 4% of the time, Pallas kernels for 44%

profile of v3, /device:TPU:0, one launch (start us, length us, event | category | flops | bytes accessed | tf_op | source)
XLA Modules:
  0.0 499.2 jit_solution(18140411399966009386)
XLA Ops:
  13.9 3.0 collective-permute-start
  19.2 2.3 copy-done.9
  21.5 2.3 copy-done.11
  29.6 10.1 %collective-permute-done.6.refs_11_.refs_17_ = bf16[768,384]{1,0:T(8,128)(2,1)} collective-permute-done((bf16[768,384]{1,0:T(8,128)(2,1)S(1)}, bf16[768,384]{1,0:T(8,128)(2,1)}, u32[]{:S(2)}, u32[]{:S(2)}) %collective-permute-start.6) | collective-permute-done | bytes 589856 | tf_op jit(solution)/shard_map/ppermute | solution.py:984
  42.9 2.3 copy-done.10
  54.6 2.6 collective-permute-done.8.refs_16_.refs_24_
  57.6 19.3 %attention_forward.2 = (bf16[768,1024]{1,0:T(8,128)(2,1)}, bf16[768,1024]{1,0:T(8,128)(2,1)}, f32[8,1024]{1,0:T(8,128)}, bf16[6,64,1024]{2,1,0:T(8,128)(2,1)}, b...) custom-call(s32[1,6]{1,0:T(1,128)} %bitcast.17, ...), custom_call_target="tpu_custom_call" | custom-call | flops 20000000000 | bytes 1048576 | tf_op jit(solution)/shard_map/attention_forward/pallas_call | solution.py:110
  78.1 2.7 collective-permute-done.12.refs_21_.refs_17_
  86.0 13.5 %mlp_forward.2 = (bf16[768,1024]{1,0:T(8,128)(2,1)}, bf16[768,1024]{1,0:T(8,128)(2,1)}, f32[8,1024]{1,0:T(8,128)}, bf16[1536,1024]{1,0:T(8,128)(2,1)}, bf16[1536,1024]{1,0:T(8,128)(2,1)}) custom-call(s32[1,6]{1,0:T(1,128)} %bitcast.18, bf16[768,1024]{1,0:T(8,128)(2,1)} %get-tuple-element.322.refs_1_.refs_2_, bf16[192,1024]{1,0:T(8,128)(2,1)} %get-tuple-element.326.refs_2_, ...), custom_call_target="tpu_custom_call" | custom-call | flops 10000000000 | bytes 1048576 | tf_op jit(solution)/shard_map/mlp_forward/pallas_call | solution.py:110
  103.2 2.6 reduce_forward.1
  105.9 6.5 %collective-permute-done.19.refs_22_.refs_18_ = bf16[768,384]{1,0:T(8,128)(2,1)} collective-permute-done((bf16[768,384]{1,0:T(8,128)(2,1)}, bf16[768,384]{1,0:T(8,128)(2,1)}, u32[]{:S(2)}, u32[]{:S(2)}) %collective-permute-start.19) | collective-permute-done | bytes 589856 | tf_op jit(solution)/shard_map/ppermute | solution.py:989
  118.7 22.6 %attention_forward.3 = (bf16[768,1024]{1,0:T(8,128)(2,1)}, bf16[768,1024]{1,0:T(8,128)(2,1)}, bf16[768,1024]{1,0:T(8,128)(2,1)}, f32[8,1024]{1,0:T(8,128)}, bf16...) custom-call(s32[1,6]{1,0:T(1,128)} %bitcast.19, ...), custom_call_target="tpu_custom_call" | custom-call | flops 20000000000 | bytes 1048576 | tf_op jit(solution)/shard_map/attention_forward/pallas_call | solution.py:110
  145.4 16.8 %mlp_forward.3 = (bf16[768,1024]{1,0:T(8,128)(2,1)}, bf16[768,1024]{1,0:T(8,128)(2,1)}, f32[8,1024]{1,0:T(8,128)}, bf16[1536,1024]{1,0:T(8,128)(2,1)}, bf16[1536...) custom-call(s32[1,6]{1,0:T(1,128)} %bitcast.20, ...), custom_call_target="tpu_custom_call" | custom-call | flops 14000000000 | bytes 1048576 | tf_op jit(solution)/shard_map/mlp_forward/pallas_call | solution.py:110
  167.2 17.1 %mlp_backward.4 = (bf16[768,1024]{1,0:T(8,128)(2,1)}, bf16[768,1024]{1,0:T(8,128)(2,1)}, bf16[768,1024]{1,0:T(8,128)(2,1)}, f32[24,768]{1,0:T(8,128)}, f32[8,102...) custom-call(s32[1,6]{1,0:T(1,128)} %bitcast.21, ...), custom_call_target="tpu_custom_call" | custom-call | flops 12999999488 | bytes 1048576 | tf_op jit(solution)/shard_map/mlp_backward/pallas_call | solution.py:110
  185.4 12.9 %mlp_backward.5 = (bf16[768,384]{1,0:T(8,128)(2,1)}, bf16[768,384]{1,0:T(8,128)(2,1)}, bf16[768,384]{1,0:T(8,128)(2,1)}, bf16[768,384]{1,0:T(8,128)(2,1)}, f32[8...) custom-call(s32[1,6]{1,0:T(1,128)} %bitcast.22, ...), custom_call_target="tpu_custom_call" | custom-call | flops 12999999488 | bytes 1048576 | tf_op jit(solution)/shard_map/mlp_backward/pallas_call | solution.py:110
  204.4 17.8 %attention_backward.4 = (bf16[768,1024]{1,0:T(8,128)(2,1)}, f32[24,768]{1,0:T(8,128)}, bf16[768,384]{1,0:T(8,128)(2,1)}, bf16[768,384]{1,0:T(8,128)(2,1)}, f32[8,576]{1,0:T(8,128)}, /*index=5*/bf16[768,1024]{1,0:T(8,128)(2,1)}) custom-call(s32[1,6]{1,0:T(1,128)} %bitcast.23, bf16[768,1024]{1,0:T(8,128)(2,1)} %get-tuple-element.381.refs_1_, ...), custom_call_target="tpu_custom_call" | custom-call | flops 14000000000 | bytes 1048576 | tf_op jit(solution)/shard_map/attention_backward/pallas_call | solution.py:110
  222.3 13.7 %attention_backward.5 = (bf16[768,384]{1,0:T(8,128)(2,1)}, bf16[768,384]{1,0:T(8,128)(2,1)}, f32[8,576]{1,0:T(8,128)}, bf16[192,1024]{1,0:T(8,128)(2,1)}, bf16[1...) custom-call(s32[1,6]{1,0:T(1,128)} %bitcast.24, ...), custom_call_target="tpu_custom_call" | custom-call | flops 14000000000 | bytes 1048576 | tf_op jit(solution)/shard_map/attention_backward/pallas_call | solution.py:110
  237.0 4.0 collective-permute-done.48.refs_8_
  244.1 2.5 add.142
  246.7 19.8 %mlp_backward.6 = (bf16[768,1024]{1,0:T(8,128)(2,1)}, bf16[768,1024]{1,0:T(8,128)(2,1)}, f32[24,768]{1,0:T(8,128)}, f32[8,1024]{1,0:T(8,128)}, bf16[768,384]{1,0...) custom-call(s32[1,6]{1,0:T(1,128)} %bitcast.25, ...), custom_call_target="tpu_custom_call" | custom-call | flops 12999999488 | bytes 1048576 | tf_op jit(solution)/shard_map/mlp_backward/pallas_call | solution.py:110
  270.5 12.8 %mlp_backward.7 = (bf16[768,384]{1,0:T(8,128)(2,1)}, bf16[768,384]{1,0:T(8,128)(2,1)}, bf16[768,384]{1,0:T(8,128)(2,1)}, bf16[768,384]{1,0:T(8,128)(2,1)}, f32[8...) custom-call(s32[1,6]{1,0:T(1,128)} %bitcast.26, ...), custom_call_target="tpu_custom_call" | custom-call | flops 12999999488 | bytes 1048576 | tf_op jit(solution)/shard_map/mlp_backward/pallas_call | solution.py:110
  283.3 4.0 collective-permute-done.55.refs_1_
  288.6 5.1 %collective-permute-done.57.refs_3_ = bf16[768,384]{1,0:T(8,128)(2,1)S(1)} collective-permute-done((bf16[768,384]{1,0:T(8,128)(2,1)}, bf16[768,384]{1,0:T(8,128)(2,1)S(1)}, u32[]{:S(2)}, u32[]{:S(2)}) %collective-permute-start.57) | collective-permute-done | bytes 589856 | tf_op jit(solution)/shard_map/ppermute | solution.py:984
  300.7 18.1 %attention_backward.6 = (bf16[768,1024]{1,0:T(8,128)(2,1)}, f32[24,768]{1,0:T(8,128)}, bf16[768,384]{1,0:T(8,128)(2,1)}, bf16[768,384]{1,0:T(8,128)(2,1)}, f32[8,576]{1,0:T(8,128)}, /*index=5*/bf16[768,1024]{1,0:T(8,128)(2,1)}) custom-call(s32[1,6]{1,0:T(1,128)} %bitcast.27, bf16[768,1024]{1,0:T(8,128)(2,1)} %get-tuple-element.416.refs_1_, ...), custom_call_target="tpu_custom_call" | custom-call | flops 14000000000 | bytes 1048576 | tf_op jit(solution)/shard_map/attention_backward/pallas_call | solution.py:110
  322.0 2.6 collective-permute-start.67
  325.7 2.6 collective-permute-start.66
  330.7 4.6 collective-permute-done.68.refs_2_
  335.3 2.6 collective-permute-start.70
  337.9 13.5 %attention_backward.7 = (bf16[768,384]{1,0:T(8,128)(2,1)}, bf16[768,384]{1,0:T(8,128)(2,1)}, f32[8,576]{1,0:T(8,128)}, bf16[192,1024]{1,0:T(8,128)(2,1)}, bf16[1...) custom-call(s32[1,6]{1,0:T(1,128)} %bitcast.28, ...), custom_call_target="tpu_custom_call" | custom-call | flops 14000000000 | bytes 1048576 | tf_op jit(solution)/shard_map/attention_backward/pallas_call | solution.py:110
  361.0 9.2 %collective-permute-done.73 = bf16[192,384]{1,0:T(8,128)(2,1)S(1)} collective-permute-done((bf16[192,384]{1,0:T(8,128)(2,1)S(1)}, bf16[192,384]{1,0:T(8,128)(2,1)S(1)}, u32[]{:S(2)}, u32[]{:S(2)}) %collective-permute-start.73) | collective-permute-done | bytes 147488 | tf_op jit(solution)/shard_map/ppermute | solution.py:989
  371.2 3.4 collective-permute-start.72
  374.7 4.3 norm_backward.1
  387.0 3.2 collective-permute-start.82
  392.2 7.7 %collective-permute-done.82 = bf16[192,384]{1,0:T(8,128)(2,1)S(1)} collective-permute-done((bf16[192,384]{1,0:T(8,128)(2,1)S(1)}, bf16[192,384]{1,0:T(8,128)(2,1)S(1)}, u32[]{:S(2)}, u32[]{:S(2)}) %collective-permute-start.82) | collective-permute-done | bytes 147488 | tf_op jit(solution)/shard_map/ppermute | solution.py:989
  400.6 3.7 collective-permute-start.81
  404.4 4.7 collective-permute-done.81
  416.9 2.7 collective-permute-start.87
  419.7 2.8 copy-done.8
  422.5 7.0 %finish.1 = (f32[192,2048]{1,0:T(8,128)}, f32[192,2048]{1,0:T(8,128)}, f32[4,192,2048]{2,1,0:T(8,128)}, f32[4,8,2048]{2,1,0:T(8,128)S(1)}) custom-call(s32[1,6]{1,0:T(1,128)S(1)} %bitcast.32, f32[2,5]{1,0:T(2,128)S(1)} %copy-done.51, f32[4,192,2048]{2,1,0:T(8,128)S(1)} %copy-done.8, f32[192,2048]{1,0:T(8,128)S(1)} %copy-done.16, ...), custom_call_target="tpu_custom_call" | custom-call | flops 6000000000 | bytes 1048576 | tf_op jit(solution)/shard_map/finish/pallas_call | solution.py:110
  439.6 2.4 collective-permute-start.91
  443.9 3.4 collective-permute-done.95
  448.8 2.9 collective-permute-done.91
  455.4 2.9 assemble.10.refs_3_
  458.3 3.1 assemble.8.refs_3_
  467.1 3.7 collective-permute-done.99
  473.7 2.6 assemble.6
  482.5 2.4 assemble.9
  484.9 5.2 %collective-permute-done.97.refs_2_ = bf16[768,384]{1,0:T(8,128)(2,1)S(1)} collective-permute-done((bf16[768,384]{1,0:T(8,128)(2,1)S(1)}, bf16[768,384]{1,0:T(8,128)(2,1)S(1)}, u32[]{:S(2)}, u32[]{:S(2)}) %collective-permute-start.97) | collective-permute-done | bytes 589856 | tf_op jit(solution)/shard_map/ppermute | solution.py:989
  (560 shorter events, 143.3 us)
Async XLA Ops:
  7.2 323.5 %reduce-scatter.2.cloned.1.call-start = ((), (), s32[]{:S(2)}) async-start(), calls=%async_computation.1 | async-start | bytes 2654208 | tf_op jit(solution)/shard_map/reduce_scatter | solution.py:1503
  17.0 35.4 %collective-permute-start.4 = (f32[2,16,256]{2,1,0:T(8,128)S(1)}, f32[2,16,256]{2,1,0:T(8,128)S(1)}, u32[]{:S(2)}, u32[]{:S(2)}) collective-permute-start(f32[2,16,256]{2,1,0:T(8,128)S(1)} %pad.8.refs_5_.refs_10_.refs_15_.refs_12_), channel_id=1, source_target_pairs={{0,1},{1,0},{2,3},{3,2},{4,5},{5,4},{6,7},{7,6},{8,9},{9,8},{10,11... | collective-permute-start | bytes 98312 | tf_op jit(solution)/shard_map/ppermute | solution.py:979
  17.0 22.7 %collective-permute-start.6 = (bf16[768,384]{1,0:T(8,128)(2,1)S(1)}, bf16[768,384]{1,0:T(8,128)(2,1)}, u32[]{:S(2)}, u32[]{:S(2)}) collective-permute-start(bf16[768,384]{1,0:T(8,128)(2,1)S(1)} %get-tuple-element.317.refs_9_.refs_3_), channel_id=1, source_target_pairs={{0,2},{1,3},{2,0},{3,1},{4,6},{5,7},{6,4},{7,5},{8,10},{9,11},{10,... | collective-permute-start | bytes 1769480 | tf_op jit(solution)/shard_map/ppermute | solution.py:984
  19.0 38.6 %collective-permute-start.2 = (bf16[192,1024]{1,0:T(8,128)(2,1)}, bf16[192,1024]{1,0:T(8,128)(2,1)}, u32[]{:S(2)}, u32[]{:S(2)}) collective-permute-start(bf16[192,1024]{1,0:T(8,128)(2,1)} %get-tuple-element.314.refs_1_), channel_id=1, source_target_pairs={{0,1},{1,0},{2,3},{3,2},{4,5},{5,4},{6,7},{7,6},{8,9},{9,8},{10,11... | collective-permute-start | bytes 1179656 | tf_op jit(solution)/shard_map/ppermute | solution.py:979
  29.1 23.9 %collective-permute-start.5 = (f32[2,16,256]{2,1,0:T(8,128)S(1)}, f32[2,16,256]{2,1,0:T(8,128)S(1)}, u32[]{:S(2)}, u32[]{:S(2)}) collective-permute-start(f32[2,16,256]{2,1,0:T(8,128)S(1)} %collective-permute-done.3.refs_6_.refs_11_.refs_16_.refs_13_), channel_id=1, source_target_pairs={{0,1},{1,0},{2,3},{3,2},{4,5},{5,4},{6,7},{7,6},{8,9},{9,8},{10,11... | collective-permute-start | bytes 98312 | tf_op jit(solution)/shard_map/ppermute | solution.py:979
  39.7 17.9 %collective-permute-start.7 = (bf16[768,384]{1,0:T(8,128)(2,1)}, bf16[768,384]{1,0:T(8,128)(2,1)}, u32[]{:S(2)}, u32[]{:S(2)}) collective-permute-start(bf16[768,384]{1,0:T(8,128)(2,1)} %collective-permute-done.6.refs_11_.refs_17_), channel_id=1, source_target_pairs={{0,4},{4,0},{8,12},{12,8},{16,20},{20,16},{24,28},{28,24},{1,5},{5... | collective-permute-start | bytes 1769480 | tf_op jit(solution)/shard_map/ppermute | solution.py:989
  52.4 24.5 %collective-permute-start.10 = (bf16[768,384]{1,0:T(8,128)(2,1)S(1)}, bf16[768,384]{1,0:T(8,128)(2,1)S(1)}, u32[]{:S(2)}, u32[]{:S(2)}) collective-permute-start(bf16[768,384]{1,0:T(8,128)(2,1)S(1)} %get-tuple-element.325.refs_1_.refs_5_), channel_id=1, source_target_pairs={{0,2},{1,3},{2,0},{3,1},{4,6},{5,7},{6,4},{7,5},{8,10},{9,11},{10,... | collective-permute-start | bytes 1769480 | tf_op jit(solution)/shard_map/ppermute | solution.py:984
  53.0 27.7 %collective-permute-start.12 = (bf16[768,384]{1,0:T(8,128)(2,1)S(1)}, bf16[768,384]{1,0:T(8,128)(2,1)}, u32[]{:S(2)}, u32[]{:S(2)}) collective-permute-start(bf16[768,384]{1,0:T(8,128)(2,1)S(1)} %get-tuple-element.330.refs_19_.refs_3_), channel_id=1, source_target_pairs={{0,2},{1,3},{2,0},{3,1},{4,6},{5,7},{6,4},{7,5},{8,10},{9,11},{10,... | collective-permute-start | bytes 1769480 | tf_op jit(solution)/shard_map/ppermute | solution.py:984
  57.2 19.7 %collective-permute-start.9 = (bf16[384,768]{1,0:T(8,128)(2,1)}, bf16[384,768]{1,0:T(8,128)(2,1)S(1)}, u32[]{:S(2)}, u32[]{:S(2)}) collective-permute-start(bf16[384,768]{1,0:T(8,128)(2,1)} %collective-permute-done.8.refs_16_.refs_24_), channel_id=1, source_target_pairs={{0,4},{4,0},{8,12},{12,8},{16,20},{20,16},{24,28},{28,24},{1,5},{5... | collective-permute-start | bytes 1769480 | tf_op jit(solution)/shard_map/ppermute | solution.py:989
  80.7 18.7 %collective-permute-start.17 = (bf16[192,1024]{1,0:T(8,128)(2,1)S(1)}, bf16[192,1024]{1,0:T(8,128)(2,1)S(1)}, u32[]{:S(2)}, u32[]{:S(2)}) collective-permute-start(bf16[192,1024]{1,0:T(8,128)(2,1)S(1)} %get-tuple-element.337), channel_id=1, source_target_pairs={{0,2},{1,3},{2,0},{3,1},{4,6},{5,7},{6,4},{7,5},{8,10},{9,11},{10,... | collective-permute-start | bytes 1179656 | tf_op jit(solution)/shard_map/ppermute | solution.py:984
  82.2 17.2 %collective-permute-start.18 = (bf16[192,1024]{1,0:T(8,128)(2,1)S(1)}, bf16[192,1024]{1,0:T(8,128)(2,1)S(1)}, u32[]{:S(2)}, u32[]{:S(2)}) collective-permute-start(bf16[192,1024]{1,0:T(8,128)(2,1)S(1)} %get-tuple-element.338.refs_11_), channel_id=1, source_target_pairs={{0,1},{1,0},{2,3},{3,2},{4,5},{5,4},{6,7},{7,6},{8,9},{9,8},{10,11... | collective-permute-start | bytes 1179656 | tf_op jit(solution)/shard_map/ppermute | solution.py:979
  82.3 31.0 %collective-permute-start.21 = (bf16[384,768]{1,0:T(8,128)(2,1)S(1)}, bf16[384,768]{1,0:T(8,128)(2,1)}, u32[]{:S(2)}, u32[]{:S(2)}) collective-permute-start(bf16[384,768]{1,0:T(8,128)(2,1)S(1)} %get-tuple-element.348.refs_14_.refs_7_), channel_id=1, source_target_pairs={{0,2},{1,3},{2,0},{3,1},{4,6},{5,7},{6,4},{7,5},{8,10},{9,11},{10,... | collective-permute-start | bytes 1769480 | tf_op jit(solution)/shard_map/ppermute | solution.py:984
  84.5 27.9 %collective-permute-start.19 = (bf16[768,384]{1,0:T(8,128)(2,1)}, bf16[768,384]{1,0:T(8,128)(2,1)}, u32[]{:S(2)}, u32[]{:S(2)}) collective-permute-start(bf16[768,384]{1,0:T(8,128)(2,1)} %collective-permute-done.12.refs_21_.refs_17_), channel_id=1, source_target_pairs={{0,4},{4,0},{8,12},{12,8},{16,20},{20,16},{24,28},{28,24},{1,5},{5... | collective-permute-start | bytes 1769480 | tf_op jit(solution)/shard_map/ppermute | solution.py:989
  114.6 27.3 %collective-permute-start.27 = (bf16[768,384]{1,0:T(8,128)(2,1)S(1)}, bf16[768,384]{1,0:T(8,128)(2,1)S(1)}, u32[]{:S(2)}, u32[]{:S(2)}) collective-permute-start(bf16[768,384]{1,0:T(8,128)(2,1)S(1)} %copy-done.27), channel_id=1, source_target_pairs={{0,2},{1,3},{2,0},{3,1},{4,6},{5,7},{6,4},{7,5},{8,10},{9,11},{10,... | collective-permute-start | bytes 1769480 | tf_op jit(solution)/shard_map/ppermute | solution.py:984
  115.7 27.4 %collective-permute-start.32 = (bf16[768,384]{1,0:T(8,128)(2,1)S(1)}, bf16[768,384]{1,0:T(8,128)(2,1)S(1)}, u32[]{:S(2)}, u32[]{:S(2)}) collective-permute-start(bf16[768,384]{1,0:T(8,128)(2,1)S(1)} %copy-done.29), channel_id=1, source_target_pairs={{0,2},{1,3},{2,0},{3,1},{4,6},{5,7},{6,4},{7,5},{8,10},{9,11},{10,... | collective-permute-start | bytes 1769480 | tf_op jit(solution)/shard_map/ppermute | solution.py:984
  116.7 25.3 %collective-permute-start.26 = (bf16[384,768]{1,0:T(8,128)(2,1)}, bf16[384,768]{1,0:T(8,128)(2,1)S(1)}, u32[]{:S(2)}, u32[]{:S(2)}) collective-permute-start(bf16[384,768]{1,0:T(8,128)(2,1)} %collective-permute-done.21.refs_16_.refs_25_), channel_id=1, source_target_pairs={{0,4},{4,0},{8,12},{12,8},{16,20},{20,16},{24,28},{28,24},{1,5},{5... | collective-permute-start | bytes 1769480 | tf_op jit(solution)/shard_map/ppermute | solution.py:989
  143.1 19.1 %collective-permute-start.33 = (bf16[192,1024]{1,0:T(8,128)(2,1)S(1)}, bf16[192,1024]{1,0:T(8,128)(2,1)S(1)}, u32[]{:S(2)}, u32[]{:S(2)}) collective-permute-start(bf16[192,1024]{1,0:T(8,128)(2,1)S(1)} %get-tuple-element.368), channel_id=1, source_target_pairs={{0,2},{1,3},{2,0},{3,1},{4,6},{5,7},{6,4},{7,5},{8,10},{9,11},{10,... | collective-permute-start | bytes 1179656 | tf_op jit(solution)/shard_map/ppermute | solution.py:984
  144.2 18.0 %collective-permute-start.34 = (bf16[192,1024]{1,0:T(8,128)(2,1)S(1)}, bf16[192,1024]{1,0:T(8,128)(2,1)S(1)}, u32[]{:S(2)}, u32[]{:S(2)}) collective-permute-start(bf16[192,1024]{1,0:T(8,128)(2,1)S(1)} %get-tuple-element.369.refs_16_), channel_id=1, source_target_pairs={{0,1},{1,0},{2,3},{3,2},{4,5},{5,4},{6,7},{7,6},{8,9},{9,8},{10,11... | collective-permute-start | bytes 1179656 | tf_op jit(solution)/shard_map/ppermute | solution.py:979
  184.3 17.0 %collective-permute-start.41 = (bf16[768,384]{1,0:T(8,128)(2,1)}, bf16[768,384]{1,0:T(8,128)(2,1)S(1)}, u32[]{:S(2)}, u32[]{:S(2)}) collective-permute-start(bf16[768,384]{1,0:T(8,128)(2,1)} %get-tuple-element.387), channel_id=1, source_target_pairs={{0,2},{1,3},{2,0},{3,1},{4,6},{5,7},{6,4},{7,5},{8,10},{9,11},{10,... | collective-permute-start | bytes 1769480 | tf_op jit(solution)/shard_map/ppermute | solution.py:984
  200.4 21.9 %collective-permute-start.45 = (bf16[768,384]{1,0:T(8,128)(2,1)S(1)}, bf16[768,384]{1,0:T(8,128)(2,1)S(1)}, u32[]{:S(2)}, u32[]{:S(2)}) collective-permute-start(bf16[768,384]{1,0:T(8,128)(2,1)S(1)} %copy-done.118), channel_id=1, source_target_pairs={{0,2},{1,3},{2,0},{3,1},{4,6},{5,7},{6,4},{7,5},{8,10},{9,11},{10,... | collective-permute-start | bytes 1769480 | tf_op jit(solution)/shard_map/ppermute | solution.py:984
  201.4 35.2 %collective-permute-start.47 = (bf16[768,384]{1,0:T(8,128)(2,1)S(1)}, bf16[768,384]{1,0:T(8,128)(2,1)S(1)}, u32[]{:S(2)}, u32[]{:S(2)}) collective-permute-start(bf16[768,384]{1,0:T(8,128)(2,1)S(1)} %copy-done.117), channel_id=1, source_target_pairs={{0,2},{1,3},{2,0},{3,1},{4,6},{5,7},{6,4},{7,5},{8,10},{9,11},{10,... | collective-permute-start | bytes 1769480 | tf_op jit(solution)/shard_map/ppermute | solution.py:984
  202.4 38.6 %collective-permute-start.48 = (bf16[768,384]{1,0:T(8,128)(2,1)S(1)}, bf16[768,384]{1,0:T(8,128)(2,1)S(1)}, u32[]{:S(2)}, u32[]{:S(2)}) collective-permute-start(bf16[768,384]{1,0:T(8,128)(2,1)S(1)} %copy-done.116), channel_id=1, source_target_pairs={{0,2},{1,3},{2,0},{3,1},{4,6},{5,7},{6,4},{7,5},{8,10},{9,11},{10,... | collective-permute-start | bytes 1769480 | tf_op jit(solution)/shard_map/ppermute | solution.py:984
  241.0 27.6 %collective-permute-start.52 = (bf16[768,384]{1,0:T(8,128)(2,1)}, bf16[768,384]{1,0:T(8,128)(2,1)S(1)}, u32[]{:S(2)}, u32[]{:S(2)}) collective-permute-start(bf16[768,384]{1,0:T(8,128)(2,1)} %get-tuple-element.414), channel_id=1, source_target_pairs={{0,2},{1,3},{2,0},{3,1},{4,6},{5,7},{6,4},{7,5},{8,10},{9,11},{10,... | collective-permute-start | bytes 1769480 | tf_op jit(solution)/shard_map/ppermute | solution.py:984
  242.0 26.6 %collective-permute-start.53 = (bf16[768,384]{1,0:T(8,128)(2,1)}, bf16[768,384]{1,0:T(8,128)(2,1)S(1)}, u32[]{:S(2)}, u32[]{:S(2)}) collective-permute-start(bf16[768,384]{1,0:T(8,128)(2,1)} %get-tuple-element.415), channel_id=1, source_target_pairs={{0,2},{1,3},{2,0},{3,1},{4,6},{5,7},{6,4},{7,5},{8,10},{9,11},{10,... | collective-permute-start | bytes 1769480 | tf_op jit(solution)/shard_map/ppermute | solution.py:984
  266.5 16.8 %collective-permute-start.54 = (bf16[768,384]{1,0:T(8,128)(2,1)}, bf16[768,384]{1,0:T(8,128)(2,1)S(1)}, u32[]{:S(2)}, u32[]{:S(2)}) collective-permute-start(bf16[768,384]{1,0:T(8,128)(2,1)} %get-tuple-element.419), channel_id=1, source_target_pairs={{0,2},{1,3},{2,0},{3,1},{4,6},{5,7},{6,4},{7,5},{8,10},{9,11},{10,... | collective-permute-start | bytes 1769480 | tf_op jit(solution)/shard_map/ppermute | solution.py:984
  267.6 26.1 %collective-permute-start.57 = (bf16[768,384]{1,0:T(8,128)(2,1)}, bf16[768,384]{1,0:T(8,128)(2,1)S(1)}, u32[]{:S(2)}, u32[]{:S(2)}) collective-permute-start(bf16[768,384]{1,0:T(8,128)(2,1)} %get-tuple-element.430), channel_id=1, source_target_pairs={{0,2},{1,3},{2,0},{3,1},{4,6},{5,7},{6,4},{7,5},{8,10},{9,11},{10,... | collective-permute-start | bytes 1769480 | tf_op jit(solution)/shard_map/ppermute | solution.py:984
  268.9 18.5 %collective-permute-start.55 = (bf16[768,384]{1,0:T(8,128)(2,1)S(1)}, bf16[768,384]{1,0:T(8,128)(2,1)S(1)}, u32[]{:S(2)}, u32[]{:S(2)}) collective-permute-start(bf16[768,384]{1,0:T(8,128)(2,1)S(1)} %get-tuple-element.424), channel_id=1, source_target_pairs={{0,4},{4,0},{8,12},{12,8},{16,20},{20,16},{24,28},{28,24},{1,5},{5... | collective-permute-start | bytes 1769480 | tf_op jit(solution)/shard_map/ppermute | solution.py:989
  293.7 26.1 %collective-permute-start.62 = (bf16[768,384]{1,0:T(8,128)(2,1)}, bf16[768,384]{1,0:T(8,128)(2,1)S(1)}, u32[]{:S(2)}, u32[]{:S(2)}) collective-permute-start(bf16[768,384]{1,0:T(8,128)(2,1)} %get-tuple-element.445), channel_id=1, source_target_pairs={{0,2},{1,3},{2,0},{3,1},{4,6},{5,7},{6,4},{7,5},{8,10},{9,11},{10,... | collective-permute-start | bytes 1769480 | tf_op jit(solution)/shard_map/ppermute | solution.py:984
  294.7 26.5 %collective-permute-start.63 = (bf16[768,384]{1,0:T(8,128)(2,1)}, bf16[768,384]{1,0:T(8,128)(2,1)S(1)}, u32[]{:S(2)}, u32[]{:S(2)}) collective-permute-start(bf16[768,384]{1,0:T(8,128)(2,1)} %get-tuple-element.446), channel_id=1, source_target_pairs={{0,2},{1,3},{2,0},{3,1},{4,6},{5,7},{6,4},{7,5},{8,10},{9,11},{10,... | collective-permute-start | bytes 1769480 | tf_op jit(solution)/shard_map/ppermute | solution.py:984
  296.8 24.3 %collective-permute-start.64 = (bf16[384,384]{1,0:T(8,128)(2,1)S(1)}, bf16[384,384]{1,0:T(8,128)(2,1)S(1)}, u32[]{:S(2)}, u32[]{:S(2)}) collective-permute-start(bf16[384,384]{1,0:T(8,128)(2,1)S(1)} %constant_dynamic-slice_fusion.13), channel_id=1, source_target_pairs={{0,8},{4,12},{8,0},{12,4},{16,24},{20,28},{24,16},{28,20},{1,9},{5... | collective-permute-start | bytes 884744 | tf_op jit(solution)/shard_map/ppermute | solution.py:989
  298.4 22.7 %collective-permute-start.61 = (bf16[768,384]{1,0:T(8,128)(2,1)S(1)}, bf16[768,384]{1,0:T(8,128)(2,1)S(1)}, u32[]{:S(2)}, u32[]{:S(2)}) collective-permute-start(bf16[768,384]{1,0:T(8,128)(2,1)S(1)} %get-tuple-element.444), channel_id=1, source_target_pairs={{0,4},{4,0},{8,12},{12,8},{16,20},{20,16},{24,28},{28,24},{1,5},{5... | collective-permute-start | bytes 1769480 | tf_op jit(solution)/shard_map/ppermute | solution.py:989
  319.8 31.7 %collective-permute-start.69 = (bf16[768,384]{1,0:T(8,128)(2,1)}, bf16[768,384]{1,0:T(8,128)(2,1)S(1)}, u32[]{:S(2)}, u32[]{:S(2)}) collective-permute-start(bf16[768,384]{1,0:T(8,128)(2,1)} %get-tuple-element.472), channel_id=1, source_target_pairs={{0,2},{1,3},{2,0},{3,1},{4,6},{5,7},{6,4},{7,5},{8,10},{9,11},{10,... | collective-permute-start | bytes 1769480 | tf_op jit(solution)/shard_map/ppermute | solution.py:984
  322.0 29.6 %collective-permute-start.67 = (bf16[192,384]{1,0:T(8,128)(2,1)}, bf16[192,384]{1,0:T(8,128)(2,1)}, u32[]{:S(2)}, u32[]{:S(2)}) collective-permute-start(bf16[192,384]{1,0:T(8,128)(2,1)} %constant_dynamic-slice_fusion.11), channel_id=1, source_target_pairs={{0,16},{4,20},{8,24},{12,28},{16,0},{20,4},{24,8},{28,12},{1,17},{... | collective-permute-start | bytes 442376 | tf_op jit(solution)/shard_map/ppermute | solution.py:989
  325.7 26.5 %collective-permute-start.66 = (bf16[768,384]{1,0:T(8,128)(2,1)S(1)}, bf16[768,384]{1,0:T(8,128)(2,1)S(1)}, u32[]{:S(2)}, u32[]{:S(2)}) collective-permute-start(bf16[768,384]{1,0:T(8,128)(2,1)S(1)} %get-tuple-element.469), channel_id=1, source_target_pairs={{0,4},{4,0},{8,12},{12,8},{16,20},{20,16},{24,28},{28,24},{1,5},{5... | collective-permute-start | bytes 1769480 | tf_op jit(solution)/shard_map/ppermute | solution.py:989
  328.6 23.5 %collective-permute-start.65 = (bf16[384,384]{1,0:T(8,128)(2,1)S(1)}, bf16[384,384]{1,0:T(8,128)(2,1)S(1)}, u32[]{:S(2)}, u32[]{:S(2)}) collective-permute-start(bf16[384,384]{1,0:T(8,128)(2,1)S(1)} %constant_dynamic-slice_fusion.12), channel_id=1, source_target_pairs={{0,8},{4,12},{8,0},{12,4},{16,24},{20,28},{24,16},{28,20},{1,9},{5... | collective-permute-start | bytes 884744 | tf_op jit(solution)/shard_map/ppermute | solution.py:989
  335.3 16.9 %collective-permute-start.70 = (bf16[192,768]{1,0:T(8,128)(2,1)}, bf16[192,768]{1,0:T(8,128)(2,1)S(1)}, u32[]{:S(2)}, u32[]{:S(2)}) collective-permute-start(bf16[192,768]{1,0:T(8,128)(2,1)} %reduce-scatter.2.cloned.1.call-done), channel_id=1, source_target_pairs={{0,16},{4,20},{8,24},{12,28},{16,0},{20,4},{24,8},{28,12},{1,17},{... | collective-permute-start | bytes 884744 | tf_op jit(solution)/shard_map/ppermute | solution.py:989
  352.2 19.0 %collective-permute-start.77 = (bf16[192,1024]{1,0:T(8,128)(2,1)}, bf16[192,1024]{1,0:T(8,128)(2,1)S(1)}, u32[]{:S(2)}, u32[]{:S(2)}) collective-permute-start(bf16[192,1024]{1,0:T(8,128)(2,1)} %get-tuple-element.482.refs_4_), channel_id=1, source_target_pairs={{0,1},{1,0},{2,3},{3,2},{4,5},{5,4},{6,7},{7,6},{8,9},{9,8},{10,11... | collective-permute-start | bytes 1179656 | tf_op jit(solution)/shard_map/ppermute | solution.py:979
  352.8 28.0 %collective-permute-start.74 = (bf16[384,768]{1,0:T(8,128)(2,1)S(1)}, bf16[384,768]{1,0:T(8,128)(2,1)S(1)}, u32[]{:S(2)}, u32[]{:S(2)}) collective-permute-start(bf16[384,768]{1,0:T(8,128)(2,1)S(1)} %maximum_select_fusion.1), channel_id=1, source_target_pairs={{0,8},{4,12},{8,0},{12,4},{16,24},{20,28},{24,16},{28,20},{1,9},{5... | collective-permute-start | bytes 1769480 | tf_op jit(solution)/shard_map/ppermute | solution.py:989
  357.1 23.7 %collective-permute-start.71 = (bf16[768,384]{1,0:T(8,128)(2,1)S(1)}, bf16[768,384]{1,0:T(8,128)(2,1)S(1)}, u32[]{:S(2)}, u32[]{:S(2)}) collective-permute-start(bf16[768,384]{1,0:T(8,128)(2,1)S(1)} %get-tuple-element.477), channel_id=1, source_target_pairs={{0,4},{4,0},{8,12},{12,8},{16,20},{20,16},{24,28},{28,24},{1,5},{5... | collective-permute-start | bytes 1769480 | tf_op jit(solution)/shard_map/ppermute | solution.py:989
  359.9 20.8 %collective-permute-start.76 = (bf16[192,1024]{1,0:T(8,128)(2,1)S(1)}, bf16[192,1024]{1,0:T(8,128)(2,1)S(1)}, u32[]{:S(2)}, u32[]{:S(2)}) collective-permute-start(bf16[192,1024]{1,0:T(8,128)(2,1)S(1)} %get-tuple-element.645), channel_id=1, source_target_pairs={{0,2},{1,3},{2,0},{3,1},{4,6},{5,7},{6,4},{7,5},{8,10},{9,11},{10,... | collective-permute-start | bytes 1179656 | tf_op jit(solution)/shard_map/ppermute | solution.py:984
  381.2 28.1 %collective-permute-start.85 = (bf16[768,768]{1,0:T(8,128)(2,1)S(1)}, bf16[768,768]{1,0:T(8,128)(2,1)}, u32[]{:S(2)}, u32[]{:S(2)}) collective-permute-start(bf16[768,768]{1,0:T(8,128)(2,1)S(1)} %maximum_select_fusion.refs_1_), channel_id=1, source_target_pairs={{0,4},{4,0},{8,12},{12,8},{16,20},{20,16},{24,28},{28,24},{1,5},{5... | collective-permute-start | bytes 3538952 | tf_op jit(solution)/shard_map/ppermute | solution.py:989
  384.0 20.4 %collective-permute-start.84 = (bf16[384,384]{1,0:T(8,128)(2,1)}, bf16[384,384]{1,0:T(8,128)(2,1)}, u32[]{:S(2)}, u32[]{:S(2)}) collective-permute-start(bf16[384,384]{1,0:T(8,128)(2,1)} %maximum_select_fusion.6), channel_id=1, source_target_pairs={{0,8},{4,12},{8,0},{12,4},{16,24},{20,28},{24,16},{28,20},{1,9},{5... | collective-permute-start | bytes 884744 | tf_op jit(solution)/shard_map/ppermute | solution.py:989
  386.0 18.4 %collective-permute-start.83 = (bf16[384,384]{1,0:T(8,128)(2,1)}, bf16[384,384]{1,0:T(8,128)(2,1)}, u32[]{:S(2)}, u32[]{:S(2)}) collective-permute-start(bf16[384,384]{1,0:T(8,128)(2,1)} %constant_dynamic-slice_fusion.6), channel_id=1, source_target_pairs={{0,8},{4,12},{8,0},{12,4},{16,24},{20,28},{24,16},{28,20},{1,9},{5... | collective-permute-start | bytes 884744 | tf_op jit(solution)/shard_map/ppermute | solution.py:989
  391.0 18.0 %collective-permute-start.86 = (bf16[192,1024]{1,0:T(8,128)(2,1)}, bf16[192,1024]{1,0:T(8,128)(2,1)}, u32[]{:S(2)}, u32[]{:S(2)}) collective-permute-start(bf16[192,1024]{1,0:T(8,128)(2,1)} %get-tuple-element.641), channel_id=1, source_target_pairs={{0,2},{1,3},{2,0},{3,1},{4,6},{5,7},{6,4},{7,5},{8,10},{9,11},{10,... | collective-permute-start | bytes 1179656 | tf_op jit(solution)/shard_map/ppermute | solution.py:984
  411.3 21.8 %collective-permute-start.90 = (bf16[768,384]{1,0:T(8,128)(2,1)S(1)}, bf16[768,384]{1,0:T(8,128)(2,1)}, u32[]{:S(2)}, u32[]{:S(2)}) collective-permute-start(bf16[768,384]{1,0:T(8,128)(2,1)S(1)} %maximum_select_fusion.2.refs_1_), channel_id=1, source_target_pairs={{0,4},{4,0},{8,12},{12,8},{16,20},{20,16},{24,28},{28,24},{1,5},{5... | collective-permute-start | bytes 1769480 | tf_op jit(solution)/shard_map/ppermute | solution.py:989
  414.4 18.7 %collective-permute-start.89 = (bf16[192,384]{1,0:T(8,128)(2,1)}, bf16[192,384]{1,0:T(8,128)(2,1)}, u32[]{:S(2)}, u32[]{:S(2)}) collective-permute-start(bf16[192,384]{1,0:T(8,128)(2,1)} %constant_dynamic-slice_fusion.3), channel_id=1, source_target_pairs={{0,16},{4,20},{8,24},{12,28},{16,0},{20,4},{24,8},{28,12},{1,17},{... | collective-permute-start | bytes 442376 | tf_op jit(solution)/shard_map/ppermute | solution.py:989
  463.8 18.7 %collective-permute-start.102 = (bf16[768,384]{1,0:T(8,128)(2,1)S(1)}, bf16[768,384]{1,0:T(8,128)(2,1)S(1)}, u32[]{:S(2)}, u32[]{:S(2)}) collective-permute-start(bf16[768,384]{1,0:T(8,128)(2,1)S(1)} %maximum_select_fusion.5.refs_1_), channel_id=1, source_target_pairs={{0,4},{4,0},{8,12},{12,8},{16,20},{20,16},{24,28},{28,24},{1,5},{5... | collective-permute-start | bytes 1769480 | tf_op jit(solution)/shard_map/ppermute | solution.py:989
  472.7 17.3 %collective-permute-start.97 = (bf16[768,384]{1,0:T(8,128)(2,1)S(1)}, bf16[768,384]{1,0:T(8,128)(2,1)S(1)}, u32[]{:S(2)}, u32[]{:S(2)}) collective-permute-start(bf16[768,384]{1,0:T(8,128)(2,1)S(1)} %maximum_select_fusion.4.refs_1_), channel_id=1, source_target_pairs={{0,4},{4,0},{8,12},{12,8},{16,20},{20,16},{24,28},{28,24},{1,5},{5... | collective-permute-start | bytes 1769480 | tf_op jit(solution)/shard_map/ppermute | solution.py:989
  (203 other events, 1809.2 us)
Sparse Core Ops, SparseCore 0:
  246.8 73.2 reduce-scatter.1
